TPU v7x, 32 devices: a whole 2x2x4 slice. The times are simulated.
32 devices in a mesh: seq: 8 (over z, x), batch: 4 (over y, core).
Axes of the slice: x: 2, y: 2, z: 4, core: 2. Of those that a mesh axis runs over, the one named last changes fastest.
Arguments:
- tokens: bfloat16 [8, 1024, 768], P('batch', 'seq'), may hold values from -6 to 6
- cotangent: bfloat16 [8, 1024, 768], P('batch', 'seq'), may hold values from -6 to 6
- lengths: int32 [8, 3], P('batch'), may hold values from 1 to 960, 1024 in all within a row
- attn_in: bfloat16 [2, 768, 2304], P(None, None, 'batch'), may hold values from -0.21875 to 0.21875
- attn_out: bfloat16 [2, 768, 768], P(None, None, 'batch'), may hold values from -1.25 to 1.25
- mlp_in: bfloat16 [2, 768, 3072], P(None, None, 'batch'), may hold values from -0.21875 to 0.21875
- mlp_out: bfloat16 [2, 3072, 768], P(None, None, 'batch'), may hold values from -0.109375 to 0.109375
- norm_gains: bfloat16 [2, 2, 768], P(None, None, 'batch'), may hold values from 0.5 to 1.5
- norm_biases: bfloat16 [2, 2, 768], P(None, None, 'batch'), may hold values from -1.5 to 1.5
- feature_maps: bfloat16 [2, 2, 64, 768], P(None, None, None, 'batch'), may hold values from -1.5 to 1.5
Outputs:
- block_output: bfloat16 [8, 1024, 768], P('batch', 'seq')
- grad_tokens: bfloat16 [8, 1024, 768], P('batch', 'seq')
- grad_attn_in: float32 [2, 768, 2304], P(None, None, 'batch')
- grad_attn_out: float32 [2, 768, 768], P(None, None, 'batch')
- grad_mlp_in: float32 [2, 768, 3072], P(None, None, 'batch')
- grad_mlp_out: float32 [2, 3072, 768], P(None, None, 'batch')
- grad_norm_gains: float32 [2, 2, 768], P(None, None, 'batch')
- grad_norm_biases: float32 [2, 2, 768], P(None, None, 'batch')
- grad_feature_maps: float32 [2, 2, 64, 768], P(None, None, None, 'batch')
- grad_mlp_norm_biases: float32 [2, 768], P(None, 'batch')
Inputs may be any that keep to these rules, and one draw needn't show every extreme that they name: `lengths`: the 3 sequences of a row lie end to end and fill its 1024 positions; the longest has exactly 960 positions.
All inputs are finite; a program needn't handle non-finite values.
Results may differ from a plain program's by a relative error of at most 0.025.
Values may be sent and summed in bfloat16 or wider, within the bound.
A program may use at most 320 MiB of HBM per device.

v0:
```python
import jax
import jax.numpy as jnp
from jax import lax
from jax.sharding import PartitionSpec as P

D = 768
H = 12
HD = 64


EPSILON = 1e-05
HIGH = lax.Precision.HIGHEST


def carried_in(value, axis, combine, identity):
    devices, position = (lax.axis_size(axis), lax.axis_index(axis))
    everything = jax.tree.map(
        lambda part, kind: lax.all_gather(part.astype(kind), axis),
        value,
        (jnp.bfloat16, jnp.bfloat16, jnp.bfloat16),
    )
    start = jax.tree.map(
        lambda part, zero: jnp.broadcast_to(jnp.asarray(zero, part.dtype), part.shape),
        value,
        identity,
    )

    def step(k, before):
        reached = k < position
        new = combine(
            before, jax.tree.map(lambda part, own: part[k].astype(own.dtype), everything, value)
        )
        return jax.tree.map(lambda a, b: jnp.where(reached, a, b), new, before)

    return lax.fori_loop(0, devices, step, start)


def carried_in_2(value, axis, join, neutral):
    count = lax.axis_size(axis)
    place = lax.axis_index(axis)
    ahead = count - 1 - place
    gathered = jax.tree.map(
        lambda a, kind: lax.all_gather(a.astype(kind), axis),
        value,
        jax.tree.map(lambda a: jnp.bfloat16 if a.dtype == jnp.float32 else a.dtype, value),
    )
    state = jax.tree.map(lambda a, e: jnp.zeros_like(a) + jnp.asarray(e, a.dtype), value, neutral)

    def one(step, state):
        source = count - 1 - step
        return join(
            state,
            jax.tree.map(
                lambda a, own: lax.dynamic_index_in_dim(a, source, 0, False).astype(own.dtype),
                gathered,
                value,
            ),
        )

    return lax.fori_loop(0, ahead, one, state)


def layer_norm(inputs, norm_gain, norm_shift):
    average = jnp.mean(inputs, axis=-1, keepdims=True)
    centred = inputs - average
    spread = jnp.mean(centred * centred, axis=-1, keepdims=True)
    return centred * lax.rsqrt(spread + EPSILON) * norm_gain + norm_shift


def activate(inputs):
    return jax.nn.gelu(inputs, approximate=True)


def feature(inputs, maps):
    logits = jnp.einsum("mshd,hde->mshe", inputs, maps, precision=HIGH)
    return jnp.concatenate(
        [jax.nn.softmax(logits, axis=-1), jax.nn.softmax(-logits, axis=-1)], axis=-1
    )


def combine(earlier, later):
    keep_going = 1.0 - later[2]
    return (
        later[0] + keep_going[:, None, None, None] * earlier[0],
        later[1] + keep_going[:, None, None] * earlier[1],
        jnp.maximum(earlier[2], later[2]),
    )


def shards(
    tokens,
    cotangent,
    lengths,
    attn_in,
    attn_out,
    mlp_in,
    mlp_out,
    norm_gains,
    norm_biases,
    feature_maps,
):
    micro_count, tok_rows, model_width = tokens.shape
    layer_count = attn_in.shape[0]
    first_position = lax.axis_index("seq") * tok_rows
    positions = first_position + jnp.arange(tok_rows, dtype=jnp.int32)
    starts = jnp.cumsum(lengths, axis=1) - lengths
    segment_ids = (
        jnp.sum((starts[:, None, :] <= positions[None, :, None]).astype(jnp.int32), axis=2) - 1
    )
    prior_segment = jnp.sum((starts <= first_position - 1).astype(jnp.int32), axis=1) - 1
    final_segment = segment_ids[:, -1]
    in_chain = (segment_ids == prior_segment[:, None]).astype(jnp.float32)
    in_last = (segment_ids == final_segment[:, None]).astype(jnp.float32)
    restart = (final_segment != prior_segment).astype(jnp.float32)
    lower = jnp.tril(jnp.ones((tok_rows, tok_rows), jnp.float32))
    same_mask = (segment_ids[:, :, None] == segment_ids[:, None, :]).astype(jnp.float32) * lower[
        None
    ]
    identity = (
        jnp.zeros((micro_count, H, 2 * HD, HD), jnp.float32),
        jnp.zeros((micro_count, H, 2 * HD), jnp.float32),
        jnp.zeros((micro_count,), jnp.float32),
    )

    def prepare(projected, raw_maps):
        layer_maps = jnp.transpose(raw_maps.reshape(2, HD, H, HD), (0, 2, 1, 3))
        query_part = projected[..., :D].reshape(micro_count, tok_rows, H, HD)
        key_part = projected[..., D : 2 * D].reshape(micro_count, tok_rows, H, HD)
        value_part = projected[..., 2 * D :].reshape(micro_count, tok_rows, H, HD)
        return (feature(query_part, layer_maps[0]), feature(key_part, layer_maps[1]), value_part)

    def summarize(feat_key, value_part):
        masked_key = feat_key * in_last[:, :, None, None]
        return (
            jnp.einsum("mjhf,mjhd->mhfd", masked_key, value_part, precision=HIGH),
            jnp.sum(masked_key, axis=1),
        )

    def read_out(feat_query, feat_key, value_part, state_sum, state_norm):
        scores = (
            jnp.einsum("mihf,mjhf->mhij", feat_query, feat_key, precision=HIGH) * same_mask[:, None]
        )
        numerator = jnp.einsum("mhij,mjhd->mihd", scores, value_part, precision=HIGH)
        numerator = numerator + in_chain[:, :, None, None] * jnp.einsum(
            "mihf,mhfd->mihd", feat_query, state_sum, precision=HIGH
        )
        denominator = jnp.transpose(jnp.sum(scores, axis=3), (0, 2, 1))
        denominator = denominator + in_chain[:, :, None] * jnp.einsum(
            "mihf,mhf->mih", feat_query, state_norm, precision=HIGH
        )
        return (numerator / denominator[..., None]).reshape(micro_count, tok_rows, H * HD)

    hidden = tokens.astype(jnp.float32)
    saved = []
    for layer in range(layer_count):
        weight_tree = (
            lax.all_gather(attn_in[layer], "batch", axis=1, tiled=True),
            lax.all_gather(attn_out[layer], "batch", axis=1, tiled=True),
            lax.all_gather(mlp_in[layer], "batch", axis=1, tiled=True),
            lax.all_gather(mlp_out[layer], "batch", axis=1, tiled=True),
            lax.all_gather(norm_gains[layer], "batch", axis=1, tiled=True),
            lax.all_gather(norm_biases[layer], "batch", axis=1, tiled=True),
            lax.all_gather(feature_maps[layer], "batch", axis=2, tiled=True),
        )
        gains = weight_tree[4].astype(jnp.float32)
        shifts = weight_tree[5].astype(jnp.float32)
        normed_first, norm_first_back = jax.vjp(layer_norm, hidden, gains[0], shifts[0])
        attention_normed_input = normed_first.astype(jnp.bfloat16)
        projected = jnp.einsum(
            "mrd,dc->mrc",
            attention_normed_input,
            weight_tree[0],
            preferred_element_type=jnp.float32,
        )
        features, prepare_back = jax.vjp(prepare, projected, weight_tree[6].astype(jnp.float32))
        local_state, summary_back = jax.vjp(summarize, features[1], features[2])
        incoming = carried_in((local_state[0], local_state[1], restart), "seq", combine, identity)
        attended, reread_output = jax.vjp(
            read_out, features[0], features[1], features[2], incoming[0], incoming[1]
        )
        attended_low = attended.astype(jnp.bfloat16)
        middle = hidden + jnp.einsum(
            "mri,io->mro", attended_low, weight_tree[1], preferred_element_type=jnp.float32
        )
        normed_second, norm_second_back = jax.vjp(layer_norm, middle, gains[1], shifts[1])
        perceptron_normed_input = normed_second.astype(jnp.bfloat16)
        upward = jnp.einsum(
            "xuo,oc->xuc",
            perceptron_normed_input,
            weight_tree[2],
            preferred_element_type=jnp.float32,
        )
        activated_full, gelu_back = jax.vjp(activate, upward)
        activated_hidden = activated_full.astype(jnp.bfloat16)
        hidden = middle + jnp.einsum(
            "nvq,qb->nvb", activated_hidden, weight_tree[3], preferred_element_type=jnp.float32
        )
        kept = None
        saved.append(
            (
                kept,
                norm_first_back,
                attention_normed_input,
                prepare_back,
                summary_back,
                reread_output,
                attended_low,
                norm_second_back,
                perceptron_normed_input,
                gelu_back,
                activated_hidden,
            )
        )
    block_output = hidden.astype(jnp.bfloat16)
    grad_hidden = cotangent.astype(jnp.float32)
    layer_grads = [None] * layer_count
    for layer in reversed(range(layer_count)):
        (
            kept,
            norm_first_back,
            attention_normed_input,
            prepare_back,
            summary_back,
            reread_output,
            attended_low,
            norm_second_back,
            perceptron_normed_input,
            gelu_back,
            activated_hidden,
        ) = saved[layer]
        weight_tree = (
            lax.all_gather(attn_in[layer], "batch", axis=1, tiled=True),
            lax.all_gather(attn_out[layer], "batch", axis=1, tiled=True),
            lax.all_gather(mlp_in[layer], "batch", axis=1, tiled=True),
            lax.all_gather(mlp_out[layer], "batch", axis=1, tiled=True),
            lax.all_gather(norm_gains[layer], "batch", axis=1, tiled=True),
            lax.all_gather(norm_biases[layer], "batch", axis=1, tiled=True),
            lax.all_gather(feature_maps[layer], "batch", axis=2, tiled=True),
        )
        gradient_lowered = grad_hidden.astype(jnp.bfloat16)
        grad_down = jnp.einsum(
            "cba,cbw->aw", activated_hidden, gradient_lowered, preferred_element_type=jnp.float32
        )
        grad_activated = jnp.einsum(
            "zxs,js->zxj", gradient_lowered, weight_tree[3], preferred_element_type=jnp.float32
        )
        gradient_upward_path = gelu_back(grad_activated)[0].astype(jnp.bfloat16)
        grad_up = jnp.einsum(
            "aoq,aos->qs",
            perceptron_normed_input,
            gradient_upward_path,
            preferred_element_type=jnp.float32,
        )
        grad_normed_mlp = jnp.einsum(
            "gkp,up->gku", gradient_upward_path, weight_tree[2], preferred_element_type=jnp.float32
        )
        grad_middle_norm, grad_gain_second, grad_shift_second = norm_second_back(grad_normed_mlp)
        grad_middle = grad_hidden + grad_middle_norm
        grad_branch = grad_middle.astype(jnp.bfloat16)
        grad_out = jnp.einsum(
            "mri,mro->io", attended_low, grad_branch, preferred_element_type=jnp.float32
        )
        grad_attended = jnp.einsum(
            "mro,io->mri", grad_branch, weight_tree[1], preferred_element_type=jnp.float32
        )
        grad_query, grad_key, grad_value, grad_state_sum, grad_state_norm = reread_output(
            grad_attended
        )
        outgoing = carried_in_2(
            (grad_state_sum, grad_state_norm, restart), "seq", combine, identity
        )
        grad_key_more, grad_value_more = summary_back((outgoing[0], outgoing[1]))
        grad_projected, gradient_feature_tables = prepare_back(
            (grad_query, grad_key + grad_key_more, grad_value + grad_value_more)
        )
        grad_projected_low = grad_projected.astype(jnp.bfloat16)
        grad_in = jnp.einsum(
            "mrd,mrc->dc",
            attention_normed_input,
            grad_projected_low,
            preferred_element_type=jnp.float32,
        )
        grad_normed_attn = jnp.einsum(
            "mrc,dc->mrd", grad_projected_low, weight_tree[0], preferred_element_type=jnp.float32
        )
        grad_hidden_norm, grad_gain_first, grad_shift_first = norm_first_back(grad_normed_attn)
        grad_hidden = grad_middle + grad_hidden_norm
        grads = (
            grad_in,
            grad_out,
            grad_up,
            grad_down,
            jnp.stack([grad_gain_first, grad_gain_second]),
            jnp.stack([grad_shift_first, grad_shift_second]),
            gradient_feature_tables,
        )
        layer_grads[layer] = grads
    first_grads = layer_grads[0]
    second_grads = layer_grads[1]
    shares = (
        lax.psum_scatter(
            first_grads[0].astype(jnp.bfloat16), "batch", scatter_dimension=1, tiled=True
        ).astype(jnp.float32),
        lax.psum_scatter(
            first_grads[1].astype(jnp.bfloat16), "batch", scatter_dimension=1, tiled=True
        ).astype(jnp.float32),
        lax.psum_scatter(
            first_grads[2].astype(jnp.bfloat16), "batch", scatter_dimension=1, tiled=True
        ).astype(jnp.float32),
        lax.psum_scatter(
            first_grads[3].astype(jnp.bfloat16), "batch", scatter_dimension=1, tiled=True
        ).astype(jnp.float32),
        lax.psum_scatter(
            first_grads[4].astype(jnp.bfloat16), "batch", scatter_dimension=1, tiled=True
        ).astype(jnp.float32),
        lax.psum_scatter(
            first_grads[5].astype(jnp.bfloat16), "batch", scatter_dimension=1, tiled=True
        ).astype(jnp.float32),
        lax.psum_scatter(
            first_grads[6].astype(jnp.bfloat16), "batch", scatter_dimension=2, tiled=True
        ).astype(jnp.float32),
        lax.psum_scatter(
            second_grads[0].astype(jnp.bfloat16), "batch", scatter_dimension=1, tiled=True
        ).astype(jnp.float32),
        lax.psum_scatter(
            second_grads[1].astype(jnp.bfloat16), "batch", scatter_dimension=1, tiled=True
        ).astype(jnp.float32),
        lax.psum_scatter(
            second_grads[2].astype(jnp.bfloat16), "batch", scatter_dimension=1, tiled=True
        ).astype(jnp.float32),
        lax.psum_scatter(
            second_grads[3].astype(jnp.bfloat16), "batch", scatter_dimension=1, tiled=True
        ).astype(jnp.float32),
        lax.psum_scatter(
            second_grads[4].astype(jnp.bfloat16), "batch", scatter_dimension=1, tiled=True
        ).astype(jnp.float32),
        lax.psum_scatter(
            second_grads[5].astype(jnp.bfloat16), "batch", scatter_dimension=1, tiled=True
        ).astype(jnp.float32),
        lax.psum_scatter(
            second_grads[6].astype(jnp.bfloat16), "batch", scatter_dimension=2, tiled=True
        ).astype(jnp.float32),
    )
    summed = lax.psum(
        (
            shares[0],
            shares[1],
            shares[2],
            shares[3],
            shares[4],
            shares[5],
            shares[6],
            shares[7],
            shares[8],
            shares[9],
            shares[10],
            shares[11],
            shares[12],
            shares[13],
        ),
        "seq",
    )
    layer_grads = [summed[:7], summed[7:]]
    stacked = [
        jnp.stack([layer_grads[layer][member] for layer in range(layer_count)])
        for member in range(7)
    ]
    return (
        block_output,
        grad_hidden.astype(jnp.bfloat16),
        stacked[0],
        stacked[1],
        stacked[2],
        stacked[3],
        stacked[4],
        stacked[5],
        stacked[6],
        stacked[5][:, 1],
    )


def solution(mesh):
    in_specs = (
        P("batch", "seq", None),
        P("batch", "seq", None),
        P("batch", None),
        P(None, None, "batch"),
        P(None, None, "batch"),
        P(None, None, "batch"),
        P(None, None, "batch"),
        P(None, None, "batch"),
        P(None, None, "batch"),
        P(None, None, None, "batch"),
    )
    out_specs = (
        P("batch", "seq", None),
        P("batch", "seq", None),
        P(None, None, "batch"),
        P(None, None, "batch"),
        P(None, None, "batch"),
        P(None, None, "batch"),
        P(None, None, "batch"),
        P(None, None, "batch"),
        P(None, None, None, "batch"),
        P(None, "batch"),
    )
    return jax.shard_map(shards, mesh=mesh, in_specs=in_specs, out_specs=out_specs, check_vma=False)
```

profile of v0, /device:TPU:0, one launch (start us, length us, event | category | flops | bytes accessed | tf_op | source)
XLA Modules:
  0.0 1590.8 jit_solution(15398688171440088466)
XLA Ops:
  10.8 7.9 all-gather.1
  20.0 8.7 all-gather
  30.3 9.1 all-gather.3
  40.1 4.6 slice_reduce_fusion.4
  44.7 4.5 slice_reduce_fusion.5
  64.0 3.9 fusion.137
  71.6 3.2 fusion.232
  75.5 20.7 %all-gather.22 = bf16[8,1,2]{2,1,0:T(2,128)(2,1)S(1)} all-gather(bf16[1,1,2]{2,1,0:T(2,128)(2,1)S(1)} %fusion.222), channel_id=1, replica_groups=mesh['seq'=8,'batch'=4] {'seq'}, dimensions={0}, use_global_device_ids=true | all-gather | bytes 36 | tf_op jit(solution)/shard_map/all_gather | solution.py:18
  98.0 6.4 all-gather.10
  104.8 5.1 slice_reduce_fusion
  110.1 7.1 all-gather.9
  117.6 5.1 slice_reduce_fusion.1
  122.9 6.6 all-gather.12
  134.7 32.5 %all-gather.5 = bf16[16,12,128]{2,1,0:T(8,128)(2,1)} all-gather(bf16[2,12,128]{2,1,0:T(8,128)(2,1)S(1)} %copy.760), channel_id=7, replica_groups=mesh['seq'=8,'batch'=4] {'seq'}, dimensions={0}, use_global_device_ids=true | all-gather | bytes 55296 | tf_op jit(solution)/shard_map/all_gather | solution.py:18
  168.9 3.3 fusion.244
  175.9 29.2 %while.66 = (s32[]{:T(128)}, f32[2,12,128,64]{3,2,1,0:T(8,128)S(1)}, f32[2,12,128]{2,1,0:T(8,128)S(1)}, s32[]{:T(128)}, bf16[8,2,12,128,64]{3,4,2,1,0:T(8,128)(2...) while((s32[]{:T(128)}, ...), condition=%wide.region_15.16_spmd.clone, body=%wide.region_14.15_spmd.clone.sunk | while | flops 998408 | bytes 3569827 | solution.py:35
  209.0 3.8 divide_convert_fusion.1
  215.8 5.5 fusion.38
  221.3 5.2 all-gather.44.cloned.1.call-done
  226.5 5.4 fusion.246
  232.2 26.5 %all-gather.46.cloned.1.call-done = bf16[1,768,2304]{1,2,0:T(8,128)(2,1)} async-done(((bf16[1,768,576]{1,2,0:T(8,128)(2,1)}), bf16[1,768,2304]{1,2,0:T(8,128)(2,1)}) %all-gather.46.cloned.1.call-update) | async-done | bytes 3538960 | tf_op jit(solution)/shard_map/all_gather | solution.py:157
  274.0 3.9 fusion.140
  286.5 32.8 %all-gather.14 = bf16[16,12,128]{2,1,0:T(8,128)(2,1)} all-gather(bf16[2,12,128]{2,1,0:T(8,128)(2,1)S(1)} %copy.784), channel_id=16, replica_groups=mesh['seq'=8,'batch'=4] {'seq'}, dimensions={0}, use_global_device_ids=true | all-gather | bytes 55296 | tf_op jit(solution)/shard_map/all_gather | solution.py:18
  321.3 3.3 fusion.251
  328.3 10.6 all-gather.48.cloned.1.call-done
  338.9 29.5 %while.67 = (s32[]{:T(128)}, f32[2,12,128,64]{3,2,1,0:T(8,128)S(1)}, f32[2,12,128]{2,1,0:T(8,128)S(1)}, s32[]{:T(128)}, bf16[8,2,12,128,64]{3,4,2,1,0:T(8,128)(2...) while((s32[]{:T(128)}, ...), condition=%wide.region_31.32_spmd.clone, body=%wide.region_30.31_spmd.clone.sunk | while | flops 998408 | bytes 3569827 | solution.py:35
  372.5 5.0 divide_convert_fusion
  381.5 14.4 all-gather.52.cloned.1.call-done
  395.9 5.8 fusion.34
  401.7 33.6 %all-gather.54.cloned.1.call-done = bf16[1,3072,768]{1,2,0:T(8,128)(2,1)} async-done(((bf16[1,3072,192]{1,2,0:T(8,128)(2,1)}), bf16[1,3072,768]{1,2,0:T(8,128)(2,1)}) %all-gather.54.cloned.1.call-update) | async-done | bytes 4718608 | tf_op jit(solution)/shard_map/all_gather | solution.py:160
  435.4 6.7 fusion.61
  448.4 3.9 convolution_convert_fusion.1
  454.5 4.1 add_multiply_fusion.1
  467.9 33.0 %all-gather.19 = bf16[16,12,128]{2,1,0:T(8,128)(2,1)} all-gather(bf16[2,12,128]{2,1,0:T(8,128)(2,1)S(1)} %bitcast.522), channel_id=21, replica_groups=mesh['seq'=8,'batch'=4] {'seq'}, dimensions={0}, use_global_device_ids=true | all-gather | bytes 55296 | tf_op jit(solution)/shard_map/all_gather | solution.py:43
  500.9 4.0 fusion.178
  504.9 8.5 all-gather.56.cloned.1.call-done
  513.6 24.2 %while.64 = (s32[]{:T(128)}, f32[2,12,128,64]{3,2,1,0:T(8,128)S(1)}, f32[2,12,128]{2,1,0:T(8,128)S(1)}, s32[]{:T(128)}, bf16[8,2,12,128,64]{3,4,2,1,0:T(8,128)(2...) while((s32[]{:T(128)}, ...), condition=%wide.region_39.40_spmd, body=%wide.region_38.39_spmd.sunk | while | flops 599050 | bytes 3569867 | solution.py:60
  540.7 3.5 bitcast_add_fusion.1
  555.0 3.6 fusion.54
  566.0 3.9 convolution_convert_fusion
  577.8 5.2 bitcast_convert_fusion.2
  584.0 5.7 bitcast_convert_fusion
  600.9 32.8 %all-gather.21 = bf16[16,12,128]{2,1,0:T(8,128)(2,1)} all-gather(bf16[2,12,128]{2,1,0:T(8,128)(2,1)S(1)} %bitcast.523), channel_id=23, replica_groups=mesh['seq'=8,'batch'=4] {'seq'}, dimensions={0}, use_global_device_ids=true | all-gather | bytes 55296 | tf_op jit(solution)/shard_map/all_gather | solution.py:43
  636.8 24.3 %while.65 = (s32[]{:T(128)}, f32[2,12,128,64]{3,2,1,0:T(8,128)S(1)}, f32[2,12,128]{2,1,0:T(8,128)S(1)}, s32[]{:T(128)}, bf16[8,2,12,128,64]{3,4,2,1,0:T(8,128)(2...) while((s32[]{:T(128)}, ...), condition=%wide.region_50.51_spmd, body=%wide.region_49.50_spmd.sunk | while | flops 599050 | bytes 3569867 | solution.py:60
  664.0 3.5 bitcast_add_fusion
  673.8 4.4 bitcast_convert_fusion.4
  679.4 5.2 bitcast_convert_fusion.3
  685.7 5.7 bitcast_convert_fusion.1
  713.0 45.0 %reduce-scatter.37.cloned.1.call-done = bf16[768,768]{1,0:T(8,128)(2,1)} async-done(((bf16[768,3072]{1,0:T(8,128)(2,1)}), bf16[768,768]{1,0:T(8,128)(2,1)}) %reduce-scatter.37.cloned.1.call-update) | async-done | bytes 1179664 | tf_op jit(solution)/shard_map/reduce_scatter | solution.py:328
  760.8 47.6 %reduce-scatter.41.cloned.1.call-done = bf16[3072,192]{0,1:T(8,128)(2,1)} async-done(((bf16[3072,768]{0,1:T(8,128)(2,1)}), bf16[3072,192]{0,1:T(8,128)(2,1)}) %reduce-scatter.41.cloned.1.call-update) | async-done | bytes 1179664 | tf_op jit(solution)/shard_map/reduce_scatter | solution.py:331
  811.5 3.8 fusion.224
  819.1 12.0 reduce-scatter.51.cloned.1.call-done
  832.7 41.9 %reduce-scatter.29.cloned.1.call-done = bf16[768,576]{0,1:T(8,128)(2,1)} async-done(((bf16[768,2304]{0,1:T(8,128)(2,1)}), bf16[768,576]{0,1:T(8,128)(2,1)}) %reduce-scatter.29.cloned.1.call-update) | async-done | bytes 884752 | tf_op jit(solution)/shard_map/reduce_scatter | solution.py:322
  877.1 48.5 %reduce-scatter.35.cloned.1.call-done = bf16[768,768]{1,0:T(8,128)(2,1)} async-done(((bf16[768,3072]{1,0:T(8,128)(2,1)}), bf16[768,768]{1,0:T(8,128)(2,1)}) %reduce-scatter.35.cloned.1.call-update) | async-done | bytes 1179664 | tf_op jit(solution)/shard_map/reduce_scatter | solution.py:307
  928.5 47.6 %reduce-scatter.39.cloned.1.call-done = bf16[3072,192]{0,1:T(8,128)(2,1)} async-done(((bf16[3072,768]{0,1:T(8,128)(2,1)}), bf16[3072,192]{0,1:T(8,128)(2,1)}) %reduce-scatter.39.cloned.1.call-update) | async-done | bytes 1179664 | tf_op jit(solution)/shard_map/reduce_scatter | solution.py:310
  979.0 40.3 %reduce-scatter.27.cloned.1.call-done = bf16[768,576]{0,1:T(8,128)(2,1)} async-done(((bf16[768,2304]{0,1:T(8,128)(2,1)}), bf16[768,576]{0,1:T(8,128)(2,1)}) %reduce-scatter.27.cloned.1.call-update) | async-done | bytes 884752 | tf_op jit(solution)/shard_map/reduce_scatter | solution.py:301
  1023.0 6.1 fusion.134
  1029.1 12.5 reduce-scatter.45.cloned.1.call-done
  1042.4 21.2 %reduce-scatter.49.cloned.1.call-done = bf16[192,2]{1,0:T(8,128)(2,1)} async-done(((bf16[768,2]{1,0:T(8,128)(2,1)}), bf16[192,2]{1,0:T(8,128)(2,1)}) %reduce-scatter.49.cloned.1.call-update) | async-done | bytes 784
  1067.0 19.4 %reduce-scatter.43.cloned.1.call-done = bf16[192,2]{1,0:T(8,128)(2,1)} async-done(((bf16[768,2]{1,0:T(8,128)(2,1)}), bf16[192,2]{1,0:T(8,128)(2,1)}) %reduce-scatter.43.cloned.1.call-update) | async-done | bytes 784
  1087.3 21.2 %reduce-scatter.47.cloned.1.call-done = bf16[192,2]{1,0:T(8,128)(2,1)} async-done(((bf16[768,2]{1,0:T(8,128)(2,1)}), bf16[192,2]{1,0:T(8,128)(2,1)}) %reduce-scatter.47.cloned.1.call-update) | async-done | bytes 784
  1109.4 22.2 %all-reduce.10 = (f32[1,2,192]{2,1,0:T(2,128)S(1)}, f32[1,2,192]{2,1,0:T(2,128)S(1)}, f32[1,2,192]{2,1,0:T(2,128)S(1)}, f32[1,2,192]{2,1,0:T(2,128)S(1)}) all-reduce(f32[1,2,192]{2,1,0:T(2,128)S(1)} %bitcast_convert_fusion.22, f32[1,2,192]{2,1,0:T(2,128)S(1)} %bitcast_convert_fusion.23, ...), channel_id=1, replica_groups=mesh['seq'=8,'batch'=4] {'seq'}, use_global_device_ids=true, to_apply=%region_80.81 | all-reduce | flops 1536 | bytes 12288 | tf_op jit(solution)/shard_map/psum | solution.py:344
  1132.8 437.2 %all-reduce.14.cloned.1.call-done = (f32[1,768,576]{1,2,0:T(8,128)}, f32[1,768,576]{1,2,0:T(8,128)}, f32[1,768,192]{1,2,0:T(8,128)}, f32[1,768,192]{1,2,0:T(8,12...) async-done(((f32[1,768,576]{1,2,0:T(8,128)}, ...) | async-done | bytes 14352400 | tf_op jit(solution)/shard_map/psum | solution.py:344
  1570.0 4.2 pad_maximum_fusion.2
  (983 shorter events, 322.3 us)
Async XLA Ops:
  7.2 42.7 %all-gather.36.cloned.1.call-start = ((), (), s32[]{:S(2)}) async-start(), calls=%async_computation.22 | async-start | bytes 4423680 | tf_op jit(solution)/shard_map/all_gather | solution.py:157
  10.0 19.1 %copy-start.251 = (s32[2,3]{1,0:T(2,128)S(1)}, s32[2,3]{1,0:T(2,128)}, u32[]{:S(2)}) copy-start(s32[2,3]{1,0:T(2,128)} %param.20) | copy-start | bytes 76
  10.0 19.5 %copy-start.179 = (bf16[2,2,64,192]{3,2,1,0:T(8,128)(2,1)S(1)}, bf16[2,2,64,192]{3,2,1,0:T(8,128)(2,1)}, u32[]{:S(2)}) copy-start(bf16[2,2,64,192]{3,2,1,0:T(8,128)(2,1)} %param.27) | copy-start | bytes 294916
  10.0 165.9 %all-gather.38.cloned.1.call-start = ((), (), s32[]{:S(2)}) async-start(), calls=%async_computation.23 | async-start | bytes 3538944 | tf_op jit(solution)/shard_map/all_gather | solution.py:18
  19.2 20.5 %copy-start.51 = (bf16[2,128,768]{2,1,0:T(8,128)(2,1)S(1)}, bf16[2,128,768]{2,1,0:T(8,128)(2,1)}, u32[]{:S(2)}) copy-start(bf16[2,128,768]{2,1,0:T(8,128)(2,1)} %param.18) | copy-start | bytes 1179652
  29.4 19.8 %copy-start.259 = (s32[2]{0:T(128)}, s32[2]{0:T(128)S(1)}, u32[]{:S(2)}) copy-start(s32[2]{0:T(128)S(1)} %get-tuple-element.854) | copy-start | bytes 28
  39.4 92.3 %copy-start.99 = (bf16[1,2,64,768]{2,3,1,0:T(8,128)(2,1)}, bf16[1,2,64,768]{2,3,1,0:T(8,128)(2,1)S(1)}, u32[]{:S(2)}) copy-start(bf16[1,2,64,768]{2,3,1,0:T(8,128)(2,1)S(1)} %copy.750) | copy-start | bytes 589828
  39.8 13.3 copy-start.224
  59.6 112.6 %copy-start.36 = (f32[2,128,768]{1,2,0:T(8,128)}, f32[2,128,768]{1,2,0:T(8,128)S(1)}, u32[]{:S(2)}) copy-start(f32[2,128,768]{1,2,0:T(8,128)S(1)} %copy.747) | copy-start | bytes 2359300
  67.9 144.9 %all-gather.40.cloned.1.call-start = ((), (), s32[]{:S(2)}) async-start(), calls=%async_computation.24 | async-start | bytes 1474560 | tf_op jit(solution)/shard_map/all_gather | solution.py:158
  69.9 145.3 %all-gather.42.cloned.1.call-start = ((), (), s32[]{:S(2)}) async-start(), calls=%async_computation.25 | async-start | bytes 5898240 | tf_op jit(solution)/shard_map/all_gather | solution.py:159
  71.6 154.9 %all-gather.44.cloned.1.call-start = ((), (), s32[]{:S(2)}) async-start(), calls=%async_computation.26 | async-start | bytes 5898240 | tf_op jit(solution)/shard_map/all_gather | solution.py:160
  74.8 22.2 %copy-start.234 = (s32[2,128]{1,0:T(2,128)S(1)}, s32[2,128]{1,0:T(2,128)}, u32[]{:S(2)}) copy-start(s32[2,128]{1,0:T(2,128)} %copy-done.233) | copy-start | bytes 3076
  74.8 23.0 %copy-start.249 = (bf16[1,2,192]{2,1,0:T(2,128)(2,1)S(1)}, bf16[1,2,192]{2,1,0:T(2,128)(2,1)}, u32[]{:S(2)}) copy-start(bf16[1,2,192]{2,1,0:T(2,128)(2,1)} %get-tuple-element.880) | copy-start | bytes 2308
  74.8 183.9 %all-gather.46.cloned.1.call-start = ((), (), s32[]{:S(2)}) async-start(), calls=%async_computation.27 | async-start | bytes 4423680 | tf_op jit(solution)/shard_map/all_gather | solution.py:157
  74.9 35.0 %copy-start.248 = (bf16[1,2,192]{2,1,0:T(2,128)(2,1)S(1)}, bf16[1,2,192]{2,1,0:T(2,128)(2,1)}, u32[]{:S(2)}) copy-start(bf16[1,2,192]{2,1,0:T(2,128)(2,1)} %get-tuple-element.878) | copy-start | bytes 2308
  75.4 263.5 %all-gather.48.cloned.1.call-start = ((), (), s32[]{:S(2)}) async-start(), calls=%async_computation.28 | async-start | bytes 3538944 | tf_op jit(solution)/shard_map/all_gather | solution.py:18
  104.8 18.0 %copy-start.156 = (bf16[1,2,64,192]{3,2,1,0:T(8,128)(2,1)S(1)}, bf16[1,2,64,192]{3,2,1,0:T(8,128)(2,1)}, u32[]{:S(2)}) copy-start(bf16[1,2,64,192]{3,2,1,0:T(8,128)(2,1)} %get-tuple-element.876) | copy-start | bytes 147460
  133.5 33.9 %copy-start.38 = (f32[2,128,12,64]{1,3,0,2:T(8,128)}, f32[2,128,12,64]{1,3,0,2:T(8,128)S(1)}, u32[]{:S(2)}) copy-start(f32[2,128,12,64]{1,3,0,2:T(8,128)S(1)} %get-tuple-element.889) | copy-start | bytes 2359300
  133.5 33.9 %copy-start.172 = (f32[2,128,12]{1,0,2:T(2,128)}, f32[2,128,12]{1,0,2:T(2,128)S(1)}, u32[]{:S(2)}) copy-start(f32[2,128,12]{1,0,2:T(2,128)S(1)} %get-tuple-element.888) | copy-start | bytes 36868
  134.7 32.7 %copy-start.40 = (f32[2,128,12,64]{1,3,0,2:T(8,128)}, f32[2,128,12,64]{1,3,0,2:T(8,128)S(1)}, u32[]{:S(2)}) copy-start(f32[2,128,12,64]{1,3,0,2:T(8,128)S(1)} %get-tuple-element.891) | copy-start | bytes 2359300
  134.7 32.7 %copy-start.174 = (f32[2,128,12]{1,0,2:T(2,128)}, f32[2,128,12]{1,0,2:T(2,128)S(1)}, u32[]{:S(2)}) copy-start(f32[2,128,12]{1,0,2:T(2,128)S(1)} %get-tuple-element.890) | copy-start | bytes 36868
  214.9 11.6 copy-start.21
  221.3 37.4 %copy-start.176 = (f32[768]{0:T(1024)S(1)}, f32[768]{0:T(1024)}, u32[]{:S(2)}) copy-start(f32[768]{0:T(1024)} %get-tuple-element.761) | copy-start | bytes 9220
  221.3 37.4 %copy-start.187 = (f32[768]{0:T(1024)S(1)}, f32[768]{0:T(1024)}, u32[]{:S(2)}) copy-start(f32[768]{0:T(1024)} %get-tuple-element.763) | copy-start | bytes 9220
  231.9 30.0 %copy-start.14 = (f32[2,128,768]{2,1,0:T(8,128)}, f32[2,128,768]{2,1,0:T(8,128)S(1)}, u32[]{:S(2)}) copy-start(f32[2,128,768]{2,1,0:T(8,128)S(1)} %get-tuple-element.899) | copy-start | bytes 2359300
  231.9 26.8 %copy-start.199 = (f32[2,128]{1,0:T(2,128)}, f32[2,128]{1,0:T(2,128)S(1)}, u32[]{:S(2)}) copy-start(f32[2,128]{1,0:T(2,128)S(1)} %broadcast_multiply_fusion.5) | copy-start | bytes 3076
  232.1 26.6 %copy-start.239 = (f32[2,128]{1,0:T(2,128)}, f32[2,128]{1,0:T(2,128)S(1)}, u32[]{:S(2)}) copy-start(f32[2,128]{1,0:T(2,128)S(1)} %multiply_reduce_fusion.17) | copy-start | bytes 3076
  232.2 26.6 %copy-start.215 = (f32[2,128]{1,0:T(2,128)}, f32[2,128]{1,0:T(2,128)S(1)}, u32[]{:S(2)}) copy-start(f32[2,128]{1,0:T(2,128)S(1)} %fusion.219) | copy-start | bytes 3076
  269.9 54.7 %copy-start.46 = (f32[2,128,768]{1,2,0:T(8,128)}, f32[2,128,768]{1,2,0:T(8,128)S(1)}, u32[]{:S(2)}) copy-start(f32[2,128,768]{1,2,0:T(8,128)S(1)} %copy.773) | copy-start | bytes 2359300
  277.9 99.6 %all-gather.50.cloned.1.call-start = ((), (), s32[]{:S(2)}) async-start(), calls=%async_computation.29 | async-start | bytes 1474560 | tf_op jit(solution)/shard_map/all_gather | solution.py:158
  278.7 117.2 %all-gather.52.cloned.1.call-start = ((), (), s32[]{:S(2)}) async-start(), calls=%async_computation.30 | async-start | bytes 5898240 | tf_op jit(solution)/shard_map/all_gather | solution.py:159
  279.4 155.9 %all-gather.54.cloned.1.call-start = ((), (), s32[]{:S(2)}) async-start(), calls=%async_computation.31 | async-start | bytes 5898240 | tf_op jit(solution)/shard_map/all_gather | solution.py:160
  280.0 233.4 %all-gather.56.cloned.1.call-start = ((), (), s32[]{:S(2)}) async-start(), calls=%async_computation.32 | async-start | bytes 3538944 | tf_op jit(solution)/shard_map/all_gather | solution.py:43
  285.2 34.2 %copy-start.47 = (f32[2,128,12,64]{1,3,0,2:T(8,128)}, f32[2,128,12,64]{1,3,0,2:T(8,128)S(1)}, u32[]{:S(2)}) copy-start(f32[2,128,12,64]{1,3,0,2:T(8,128)S(1)} %get-tuple-element.905) | copy-start | bytes 2359300
  285.2 34.2 %copy-start.163 = (f32[2,128,12]{1,0,2:T(2,128)}, f32[2,128,12]{1,0,2:T(2,128)S(1)}, u32[]{:S(2)}) copy-start(f32[2,128,12]{1,0,2:T(2,128)S(1)} %get-tuple-element.904) | copy-start | bytes 36868
  286.5 33.1 %copy-start.49 = (f32[2,128,12,64]{1,3,0,2:T(8,128)}, f32[2,128,12,64]{1,3,0,2:T(8,128)S(1)}, u32[]{:S(2)}) copy-start(f32[2,128,12,64]{1,3,0,2:T(8,128)S(1)} %get-tuple-element.907) | copy-start | bytes 2359300
  286.5 33.1 %copy-start.165 = (f32[2,128,12]{1,0,2:T(2,128)}, f32[2,128,12]{1,0,2:T(2,128)S(1)}, u32[]{:S(2)}) copy-start(f32[2,128,12]{1,0,2:T(2,128)S(1)} %get-tuple-element.906) | copy-start | bytes 36868
  379.8 16.1 %copy-start.196 = (f32[2,128]{1,0:T(2,128)}, f32[2,128]{1,0:T(2,128)S(1)}, u32[]{:S(2)}) copy-start(f32[2,128]{1,0:T(2,128)S(1)} %broadcast_multiply_fusion.4) | copy-start | bytes 3076
  380.9 15.0 copy-start.241
  395.9 39.5 %copy-start.125 = (bf16[2,128,768]{2,1,0:T(8,128)(2,1)S(1)}, bf16[2,128,768]{2,1,0:T(8,128)(2,1)}, u32[]{:S(2)}) copy-start(bf16[2,128,768]{2,1,0:T(8,128)(2,1)} %param.19) | copy-start | bytes 1179652
  452.3 184.4 %all-gather.58.cloned.1.call-start = ((), (), s32[]{:S(2)}) async-start(), calls=%async_computation.33 | async-start | bytes 3538944 | tf_op jit(solution)/shard_map/all_gather | solution.py:43
  464.3 36.6 %copy-start.27 = (f32[2,12,128,128]{2,3,1,0:T(8,128)S(1)}, f32[2,12,128,128]{2,3,1,0:T(8,128)}, u32[]{:S(2)}) copy-start(f32[2,12,128,128]{2,3,1,0:T(8,128)} %copy-done.26) | copy-start | bytes 4718596
  464.3 36.5 %copy-start.83 = (f32[2,128,768]{1,2,0:T(8,128)S(1)}, f32[2,128,768]{1,2,0:T(8,128)}, u32[]{:S(2)}) copy-start(f32[2,128,768]{1,2,0:T(8,128)} %copy-done.82) | copy-start | bytes 2359300
  569.9 135.8 %reduce-scatter.33.cloned.1.call-start = ((), (), s32[]{:S(2)}) async-start(), calls=%async_computation.17 | async-start | bytes 1474560 | tf_op jit(solution)/shard_map/reduce_scatter | solution.py:325
  571.6 138.0 %reduce-scatter.53.cloned.1.call-start = ((), (), s32[]{:S(2)}) async-start(), calls=%async_computation.39 | async-start | bytes 245760
  576.0 135.2 %reduce-scatter.31.cloned.1.call-start = ((), (), s32[]{:S(2)}) async-start(), calls=%async_computation.16 | async-start | bytes 1474560 | tf_op jit(solution)/shard_map/reduce_scatter | solution.py:304
  577.7 180.3 %reduce-scatter.37.cloned.1.call-start = ((), (), s32[]{:S(2)}) async-start(), calls=%async_computation.19 | async-start | bytes 5898240 | tf_op jit(solution)/shard_map/reduce_scatter | solution.py:328
  583.0 225.4 %reduce-scatter.41.cloned.1.call-start = ((), (), s32[]{:S(2)}) async-start(), calls=%async_computation.21 | async-start | bytes 5898240 | tf_op jit(solution)/shard_map/reduce_scatter | solution.py:331
  589.7 241.3 %reduce-scatter.51.cloned.1.call-start = ((), (), s32[]{:S(2)}) async-start(), calls=%async_computation.38 | async-start | bytes 245760
  673.7 200.9 %reduce-scatter.29.cloned.1.call-start = ((), (), s32[]{:S(2)}) async-start(), calls=%async_computation.15 | async-start | bytes 4423680 | tf_op jit(solution)/shard_map/reduce_scatter | solution.py:322
  678.3 247.4 %reduce-scatter.35.cloned.1.call-start = ((), (), s32[]{:S(2)}) async-start(), calls=%async_computation.18 | async-start | bytes 5898240 | tf_op jit(solution)/shard_map/reduce_scatter | solution.py:307
  684.6 291.5 %reduce-scatter.39.cloned.1.call-start = ((), (), s32[]{:S(2)}) async-start(), calls=%async_computation.20 | async-start | bytes 5898240 | tf_op jit(solution)/shard_map/reduce_scatter | solution.py:310
  691.5 327.8 %reduce-scatter.27.cloned.1.call-start = ((), (), s32[]{:S(2)}) async-start(), calls=%async_computation.14 | async-start | bytes 4423680 | tf_op jit(solution)/shard_map/reduce_scatter | solution.py:301
  705.1 336.5 %reduce-scatter.45.cloned.1.call-start = ((), (), s32[]{:S(2)}) async-start(), calls=%async_computation.35 | async-start | bytes 245760
  708.5 355.2 %reduce-scatter.49.cloned.1.call-start = ((), (), s32[]{:S(2)}) async-start(), calls=%async_computation.37 | async-start | bytes 245760
  709.5 377.0 %reduce-scatter.43.cloned.1.call-start = ((), (), s32[]{:S(2)}) async-start(), calls=%async_computation.34 | async-start | bytes 245760
  760.8 50.6 %copy-start.136 = (f32[2,128,12,64]{1,3,2,0:T(8,128)S(1)}, f32[2,128,12,64]{1,3,2,0:T(8,128)}, u32[]{:S(2)}) copy-start(f32[2,128,12,64]{1,3,2,0:T(8,128)} %copy-done.135) | copy-start | bytes 2359300
  817.9 290.5 %reduce-scatter.47.cloned.1.call-start = ((), (), s32[]{:S(2)}) async-start(), calls=%async_computation.36 | async-start | bytes 245760
  818.9 751.1 %all-reduce.14.cloned.1.call-start = ((), (), s32[]{:S(2)}) async-start(), calls=%async_computation.40 | async-start | bytes 28835840 | tf_op jit(solution)/shard_map/psum | solution.py:344
  1023.0 42.2 %copy-start.62 = (f32[2,128,768]{2,1,0:T(8,128)S(1)}, f32[2,128,768]{2,1,0:T(8,128)}, u32[]{:S(2)}) copy-start(f32[2,128,768]{2,1,0:T(8,128)} %copy-done.61) | copy-start | bytes 2359300
  1023.0 42.2 %copy-start.227 = (f32[2,128]{1,0:T(2,128)S(1)}, f32[2,128]{1,0:T(2,128)}, u32[]{:S(2)}) copy-start(f32[2,128]{1,0:T(2,128)} %copy-done.226) | copy-start | bytes 3076
  1023.0 42.2 %copy-start.229 = (f32[2,128]{1,0:T(2,128)S(1)}, f32[2,128]{1,0:T(2,128)}, u32[]{:S(2)}) copy-start(f32[2,128]{1,0:T(2,128)} %copy-done.228) | copy-start | bytes 3076
  1131.6 442.6 %copy-start.250 = (f32[2,2,192]{2,1,0:T(2,128)}, f32[2,2,192]{2,1,0:T(2,128)S(1)}, u32[]{:S(2)}) copy-start(f32[2,2,192]{2,1,0:T(2,128)S(1)} %constant_dynamic-update-slice_fusion) | copy-start | bytes 9220
  (230 other events, 630.1 us)
Sparse Core Ops, SparseCore 0:
  10.2 37.6 all-gather.35
  68.1 61.7 all-gather.37
  131.4 16.0 all-gather.39
  149.5 37.4 all-gather.41
  189.0 37.4 all-gather.43
  227.9 30.7 all-gather.45
  278.0 60.8 all-gather.47
  340.5 16.2 all-gather.49
  358.4 37.4 all-gather.51
  397.8 37.4 all-gather.53
  452.4 60.9 all-gather.55
  570.0 58.3 all-gather.57
  631.6 24.4 reduce-scatter.32
  659.0 19.7 reduce-scatter.52
  681.4 25.7 reduce-scatter.30
  710.1 47.8 reduce-scatter.36
  760.5 47.8 reduce-scatter.40
  811.3 19.7 reduce-scatter.50
  834.2 40.4 reduce-scatter.28
  877.8 47.8 reduce-scatter.34
  928.2 47.8 reduce-scatter.38
  978.8 40.4 reduce-scatter.26
  1021.7 19.7 reduce-scatter.44
  1043.8 19.7 reduce-scatter.48
  1066.6 19.7 reduce-scatter.42
  1088.7 19.7 reduce-scatter.46
  1115.3 454.6 all-reduce.13
where the time goes:
time: 1610 us; the launch traced here: 1590 us
  waiting for transfers between devices  896 us (56%)
  blocking collectives  220 us (14%)
  matrix products  185 us (11%)
  local copies, waits for them, and re-layouts  134 us (8%)
  other arithmetic  134 us (8%)
  between operations  18.1 us (1%)
    psum x1, waiting for transfers between devices, shards(): lax.psum((shares[0], shares[1], shares[2], shares[3], shares[4], shares[5...  437 us
    unnamed x33, waiting for transfers between devices  89 us
    all_gather x3, blocking collectives, carried_in(): lax.all_gather(part.astype(kind), axis)  86 us
    all_gather x2, blocking collectives, carried_in_2(): lax.all_gather(a.astype(kind), axis)  65.8 us
    reduce_scatter x1, waiting for transfers between devices, shards(): lax.psum_scatter(first_grads[2].astype(jnp.bfloat16), 'batch', scatter_di...  48.5 us
    unnamed x559, local copies, waits for them, and re-layouts  47.9 us
    reduce_scatter x1, waiting for transfers between devices, shards(): lax.psum_scatter(first_grads[3].astype(jnp.bfloat16), 'batch', scatter_di...  47.6 us
    reduce_scatter x1, waiting for transfers between devices, shards(): lax.psum_scatter(second_grads[3].astype(jnp.bfloat16), 'batch', scatter_d...  47.6 us
  transfers between devices with their start and end apart: 27, of which 18 were waited for; matrix products, arithmetic and copies ran while one was open for 19% of the time, Pallas kernels for 0%

commit v1 on v0

v1 whole, which is shorter than its diff:
```python
import functools

import jax
import jax.numpy as jnp
from jax import lax
from jax.experimental import pallas as pl
from jax.experimental.pallas import tpu as pltpu
from jax.sharding import PartitionSpec as P

D = 768
H = 12
HD = 64
EPSILON = 1e-05
HIGH = lax.Precision.HIGH
BF = jnp.bfloat16
MESH = pl.DeviceIdType.MESH


def greet(peers):
    bar = pltpu.get_barrier_semaphore()
    for p in peers:
        pl.semaphore_signal(bar, inc=1, device_id=p, device_id_type=MESH)
    pl.semaphore_wait(bar, len(peers))

def remote(src, dst, ss, rs, dev):
    return pltpu.make_async_remote_copy(src_ref=src, dst_ref=dst, send_sem=ss, recv_sem=rs, device_id=dev, device_id_type=MESH)

def arrive(ref, sem):
    pltpu.make_async_copy(ref, ref, sem).wait()

def reduce_kernel(n, N, R, g_ref, o_ref, own, recvC, recvY, recvX, recvZ1, recvZ2, recvH, fin, out32,
                  lsem, csem, ysem, xsem, z1sem, z2sem, hsem, a2sem, a1sem, bsem, osem):
    s = lax.axis_index("seq"); b = lax.axis_index("batch")
    xl = s % 2; z = s // 2; b0 = z % 2; b1 = (z // 2) % 2
    levels = [l for l in range(2, 10) if (1 << l) < n // 2]
    par = b % 2; yy = b // 2
    core_dev = (s, b + 1 - 2 * par); y_dev = (s, (b + 2) % 4); x_dev = (s + 1 - 2 * xl, b)
    z1_dev = (s + 2 * (1 - 2 * b0), b); z2_dev = (s + 4 * (1 - 2 * b1), b)
    h_dev = lambda l: (s + (2 << l) * (1 - 2 * ((z // (1 << l)) % 2)), b)
    greet([core_dev, y_dev, x_dev, z1_dev, z2_dev] + [h_dev(l) for l in levels])
    ds = lambda i, k: pl.ds(pl.multiple_of(i * k, k), k)
    xc = ds(xl, 384); xo = ds(1 - xl, 384)
    Q = R // 4
    half = ds(b0, R // 2); quarter = pl.ds(pl.multiple_of(b0 * (R // 2) + b1 * Q, Q), Q)
    cC = lambda c: remote(g_ref.at[c, 1 - par], recvC.at[c], csem.at[0, c], csem.at[1, c], core_dev)
    cL = lambda c: pltpu.make_async_copy(g_ref.at[c, par], own.at[c % 8], lsem.at[c % 8])
    cY = lambda c: remote(recvC.at[c, 1 - yy], recvY.at[c], ysem.at[0, c], ysem.at[1, c], y_dev)
    cX = lambda c: remote(recvY.at[c, :, xo], recvX.at[c], xsem.at[0, c], xsem.at[1, c], x_dev)
    cZ1 = lambda c: remote(recvX.at[c, ds(1 - b0, R // 2)], recvZ1.at[c], z1sem.at[0, c], z1sem.at[1, c], z1_dev)
    cZ2 = lambda c: remote(recvZ1.at[c, ds(1 - b1, Q)], recvZ2.at[c], z2sem.at[0, c], z2sem.at[1, c], z2_dev)
    cH = lambda c, i: remote(recvH.at[c, len(levels)], recvH.at[c, i], hsem.at[0, c], hsem.at[1, c], h_dev(levels[i]))
    cA2 = lambda c: remote(fin.at[c, quarter, xc], fin.at[c, quarter, xc], a2sem.at[0, c], a2sem.at[1, c], z2_dev)
    cA1 = lambda c: remote(fin.at[c, half, xc], fin.at[c, half, xc], a1sem.at[0, c], a1sem.at[1, c], z1_dev)
    cB = lambda c: remote(fin.at[c, :, xc], fin.at[c, :, xc], bsem.at[0, c], bsem.at[1, c], x_dev)
    cO = lambda c: pltpu.make_async_copy(out32.at[c % 2], o_ref.at[c], osem.at[c % 2])
    f32 = jnp.float32; bf = BF
    def add(a, b_): return (a.astype(f32) + b_.astype(f32)).astype(bf)
    def when(c, fn):
        @pl.when((c >= 0) & (c < N))
        def _(): fn(c)
    def stage0(c):
        cL(c).start(); cC(c).start()
    def stageY(c):
        cL(c).wait(); cC(c).wait_recv()
        recvC[c, 1 - yy] = add(recvC[c, 1 - yy], own[c % 8, 1 - yy])
        cY(c).start()
        recvC[c, yy] = add(recvC[c, yy], own[c % 8, yy])
    def stageX(c):
        cY(c).wait_recv()
        recvY[c, :, xo] = add(recvY[c, :, xo], recvC[c, yy, :, xo])
        cX(c).start()
        recvY[c, :, xc] = add(recvY[c, :, xc], recvC[c, yy, :, xc])
    def stageZ1(c):
        cX(c).wait_recv()
        recvX[c] = add(recvX[c], recvY[c, :, xc])
        cZ1(c).start()
    def stageZ2(c):
        cZ1(c).wait_recv()
        recvZ1[c] = add(recvZ1[c], recvX[c, half])
        cZ2(c).start()
    def stageA2(c):
        cZ2(c).wait_recv()
        t = add(recvZ2[c], recvZ1[c, ds(b1, Q)])
        for i in range(len(levels)):
            recvH[c, len(levels)] = t
            cH(c, i).start(); cH(c, i).wait()
            t = add(t, recvH[c, i])
        fin[c, quarter, xc] = t
        cA2(c).start()
    def stageA1(c):
        cA2(c).wait_recv(); cA1(c).start()
    def stageB(c):
        cA1(c).wait_recv(); cB(c).start()
    def stageO(c):
        cB(c).wait_recv()
        @pl.when(c >= 2)
        def _(): cO(c - 2).wait()
        out32[c % 2] = fin[c].astype(f32)
        cO(c).start()
    def drain(c, carry):
        for f in (cC, cY, cX, cZ1, cZ2, cA2, cA1, cB): f(c).wait_send()
        return carry
    stages = [stage0, stageY, stageX, stageZ1, stageZ2, stageA2, stageA1, stageB, stageO]
    def step(t, carry):
        for i, f in enumerate(stages): when(t - i, f)
        return carry
    lax.fori_loop(0, N + 8, step, 0)
    for c in range(max(0, N - 2), N): cO(c).wait()
    lax.fori_loop(0, N, drain, 0)

def reduce_grads(n, g):
    N, _, _, R, _ = g.shape
    bf = BF
    nl = len([l for l in range(2, 10) if (1 << l) < n // 2])
    S = lambda: pltpu.SemaphoreType.DMA((2, N))
    V = lambda *shp: pltpu.VMEM(shp, bf)
    return pl.pallas_call(functools.partial(reduce_kernel, n, N, R), name="reduce_grads",
        out_shape=jax.ShapeDtypeStruct((N, R, D), jnp.float32),
        in_specs=[pl.BlockSpec(memory_space=pl.ANY)], out_specs=pl.BlockSpec(memory_space=pl.ANY),
        scratch_shapes=[V(8, 2, R, D), V(N, 2, R, D), V(N, R, D), V(N, R, 384), V(N, R // 2, 384), V(N, R // 4, 384),
            V(N if nl else 1, nl + 1, R // 4, 384), V(N, R, D), pltpu.VMEM((2, R, D), jnp.float32),
            pltpu.SemaphoreType.DMA((8,))] + [S() for _ in range(9)] + [pltpu.SemaphoreType.DMA((2,))],
        compiler_params=pltpu.CompilerParams(collective_id=1, has_side_effects=True, vmem_limit_bytes=62*2**20))(g)

def offsets(c, b):
    if c < 3:
        return b * 576 + c * 192
    if c < 4:
        return 2304 + b * 192
    if c < 8:
        return 3072 + b * 768 + (c - 4) * 192
    return 6144 + (c - 8) * 768 + b * 192


def gather_kernel(
    w_ref, s_ref, o_ref, t_ref, lsem, ysem, xsem, own_sem, near_sem, far_sem, small_sem
):
    s = lax.axis_index("seq")
    b = lax.axis_index("batch")
    xl = s % 2
    core = b + 1 - 2 * (b % 2)
    far = (b + 2) % 4
    layers = w_ref.shape[0]
    core_dev, y_dev, x_dev = (s, core), (s, far), (s + 1 - 2 * xl, b)
    others = [(s, (b + k) % 4) for k in range(1, 4)]
    greet([core_dev, y_dev, x_dev, (s, (far + 1 - 2 * (far % 2)))])
    smalls = [
        remote(s_ref, t_ref.at[b], small_sem.at[0, k], small_sem.at[1, 2 - k], dev)
        for k, dev in enumerate(others)
    ]
    small_here = pltpu.make_async_copy(s_ref, t_ref.at[b], lsem.at[layers * 12])
    for copy in smalls + [small_here]:
        copy.start()

    def rows(c, who, part, size):
        return pl.ds(pl.multiple_of(offsets(c % 12, who) + part * 96, 32), size)

    def same(c, who, part, size, sem, dev):
        place = o_ref.at[c // 12, rows(c, who, part, size)]
        return remote(place, place, sem.at[0, c], sem.at[1, c], dev)

    def here(c):
        return w_ref.at[c // 12, pl.ds((c % 12) * 192, 192)]

    def out_y(c):
        src = w_ref.at[c // 12, pl.ds(pl.multiple_of((c % 12) * 192 + xl * 96, 32), 96)]
        return remote(src, o_ref.at[c // 12, rows(c, b, xl, 96)], ysem.at[0, c], ysem.at[1, c], y_dev)

    def out_core(c):
        return remote(here(c), o_ref.at[c // 12, rows(c, b, 0, 192)], own_sem.at[0, c], own_sem.at[1, c], core_dev)

    def stay(c):
        return pltpu.make_async_copy(here(c), o_ref.at[c // 12, rows(c, b, 0, 192)], lsem.at[c])

    out_x = lambda c: same(c, far, xl, 96, xsem, x_dev)
    near = lambda c: same(c, far, xl, 96, near_sem, core_dev)
    last = lambda c: same(c, far, 1 - xl, 96, far_sem, core_dev)
    count = layers * 12
    for c in range(count):
        out_y(c).start()
        out_core(c).start()
        stay(c).start()
    for c in range(count + 1):
        if c < count:
            out_y(c).wait_recv()
            out_x(c).start()
            near(c).start()
        if c >= 1:
            out_x(c - 1).wait_recv()
            last(c - 1).start()
    for c in range(count):
        stay(c).wait()
        for copy in (out_core(c), near(c), last(c)):
            copy.wait()
        out_y(c).wait_send()
        out_x(c).wait_send()
    small_here.wait()
    for copy in smalls:
        copy.wait()


def gather_weights(w, small):
    layers = w.shape[0]
    pair = lambda: pltpu.SemaphoreType.DMA((2, layers * 12))
    return pl.pallas_call(
        gather_kernel,
        name="gather_weights",
        out_shape=(
            jax.ShapeDtypeStruct((layers, 9216, D), BF),
            jax.ShapeDtypeStruct((4,) + small.shape, BF),
        ),
        in_specs=[pl.BlockSpec(memory_space=pl.ANY)] * 2,
        out_specs=[pl.BlockSpec(memory_space=pl.ANY)] * 2,
        scratch_shapes=[pltpu.SemaphoreType.DMA((layers * 12 + 1,))]
        + [pair() for _ in range(5)]
        + [pltpu.SemaphoreType.DMA((2, 3))],
        compiler_params=pltpu.CompilerParams(collective_id=0, has_side_effects=True),
    )(w, small)


def layer_norm(inputs, norm_gain, norm_shift):
    average = jnp.mean(inputs, axis=-1, keepdims=True)
    centred = inputs - average
    spread = jnp.mean(centred * centred, axis=-1, keepdims=True)
    return centred * lax.rsqrt(spread + EPSILON) * norm_gain + norm_shift


def activate(inputs):
    return jax.nn.gelu(inputs, approximate=True)


def feature(inputs, maps):
    logits = jnp.einsum("mshd,hde->mshe", inputs, maps, precision=HIGH)
    return jnp.concatenate(
        [jax.nn.softmax(logits, axis=-1), jax.nn.softmax(-logits, axis=-1)], axis=-1
    )


def shards(tokens, cotangent, lengths, attn_in, attn_out, mlp_in, mlp_out, norm_gains, norm_biases, feature_maps):
    micro_count, tok_rows, _ = tokens.shape
    layer_count = attn_in.shape[0]
    n = lax.axis_size("seq")
    me = lax.axis_index("seq")
    first_position = me * tok_rows
    positions = first_position + jnp.arange(tok_rows, dtype=jnp.int32)
    starts = jnp.cumsum(lengths, axis=1) - lengths
    seg = lambda p: jnp.sum((starts[:, None, :] <= p[None, :, None]).astype(jnp.int32), axis=2) - 1
    segment_ids = seg(positions)
    firsts = jnp.arange(n, dtype=jnp.int32) * tok_rows
    prior_all = seg(firsts - 1)
    final_all = seg(firsts + tok_rows - 1)
    prior_segment = seg((first_position - 1)[None])
    final_segment = segment_ids[:, -1:]
    in_chain = (segment_ids == prior_segment).astype(jnp.float32)
    in_last = (segment_ids == final_segment).astype(jnp.float32)
    order = jnp.arange(n)
    take = ((final_all == prior_segment) & (order < me)[None]).astype(jnp.float32)
    give = ((prior_all == final_segment) & (order > me)[None]).astype(jnp.float32)
    lower = jnp.tril(jnp.ones((tok_rows, tok_rows), jnp.float32))
    same_mask = (segment_ids[:, :, None] == segment_ids[:, None, :]).astype(jnp.float32) * lower[None]

    packed = jnp.concatenate(
        [
            jnp.swapaxes(attn_in, 1, 2),
            jnp.swapaxes(attn_out, 1, 2),
            mlp_in,
            jnp.transpose(mlp_out.reshape(layer_count, 4, 768, 192), (0, 1, 3, 2)).reshape(layer_count, 768, 768),
        ],
        axis=1,
    )
    small = jnp.concatenate([norm_gains[:, :, None], norm_biases[:, :, None], feature_maps], axis=2)
    small = jnp.pad(small.reshape(layer_count * 2 * 66, 192), ((0, (-layer_count * 132) % 16), (0, 64)))
    weights, smalls = gather_weights(packed, small)
    smalls = smalls[:, : layer_count * 132, :192].reshape(4, layer_count, 2, 66, 192)
    smalls = jnp.transpose(smalls, (1, 2, 3, 0, 4)).reshape(layer_count, 2, 66, 768).astype(jnp.float32)

    def prepare(projected, raw_maps):
        layer_maps = jnp.transpose(raw_maps.reshape(2, HD, H, HD), (0, 2, 1, 3))
        query_part = projected[..., :D].reshape(micro_count, tok_rows, H, HD)
        key_part = projected[..., D : 2 * D].reshape(micro_count, tok_rows, H, HD)
        value_part = projected[..., 2 * D :].reshape(micro_count, tok_rows, H, HD)
        return (feature(query_part, layer_maps[0]), feature(key_part, layer_maps[1]), value_part)

    def summarize(feat_key, value_part):
        masked_key = feat_key * in_last[:, :, None, None]
        return (
            jnp.einsum("mjhf,mjhd->mhfd", masked_key, value_part, precision=HIGH),
            jnp.sum(masked_key, axis=1),
        )

    def exchange(state, pick):
        both = jnp.concatenate([state[0], state[1][..., None]], axis=-1).astype(BF)
        every = lax.all_gather(both.reshape(micro_count, H * 2 * HD * (HD + 1)), "seq")
        got = jnp.einsum("kmx,mk->mx", every, pick.astype(BF), preferred_element_type=jnp.float32)
        got = got.reshape(micro_count, H, 2 * HD, HD + 1)
        return got[..., :HD], got[..., HD]

    def read_out(feat_query, feat_key, value_part, state_sum, state_norm):
        scores = jnp.einsum("mihf,mjhf->mhij", feat_query, feat_key, precision=HIGH) * same_mask[:, None]
        numerator = jnp.einsum("mhij,mjhd->mihd", scores, value_part, precision=HIGH)
        numerator = numerator + in_chain[:, :, None, None] * jnp.einsum(
            "mihf,mhfd->mihd", feat_query, state_sum, precision=HIGH
        )
        denominator = jnp.transpose(jnp.sum(scores, axis=3), (0, 2, 1))
        denominator = denominator + in_chain[:, :, None] * jnp.einsum(
            "mihf,mhf->mih", feat_query, state_norm, precision=HIGH
        )
        return (numerator / denominator[..., None]).reshape(micro_count, tok_rows, H * HD)

    F32 = jnp.float32
    hidden = tokens.astype(F32)
    saved = []
    parts = [
        (weights[l, :2304], weights[l, 2304:3072], weights[l, 3072:6144].reshape(4, 768, 768), weights[l, 6144:].reshape(4, 768, 768))
        for l in range(layer_count)
    ]
    for layer in range(layer_count):
        w_in, w_out, w_up, w_down = parts[layer]
        gains, shifts, maps = smalls[layer, :, 0], smalls[layer, :, 1], smalls[layer, :, 2:]
        normed_first, norm_first_back = jax.vjp(layer_norm, hidden, gains[0], shifts[0])
        normed_attn = normed_first.astype(BF)
        projected = jnp.einsum("mrd,cd->mrc", normed_attn, w_in, preferred_element_type=F32)
        features, prepare_back = jax.vjp(prepare, projected, maps)
        local_state, summary_back = jax.vjp(summarize, features[1], features[2])
        incoming = exchange(local_state, take)
        attended, reread_output = jax.vjp(read_out, features[0], features[1], features[2], incoming[0], incoming[1])
        attended_low = attended.astype(BF)
        middle = hidden + jnp.einsum("mri,oi->mro", attended_low, w_out, preferred_element_type=F32)
        normed_second, norm_second_back = jax.vjp(layer_norm, middle, gains[1], shifts[1])
        normed_mlp = normed_second.astype(BF)
        upward = jnp.einsum("mrd,kdc->mrkc", normed_mlp, w_up, preferred_element_type=F32)
        activated_full, gelu_back = jax.vjp(activate, upward)
        activated = activated_full.astype(BF)
        hidden = middle + jnp.einsum("mrkc,koc->mro", activated, w_down, preferred_element_type=F32)
        saved.append(
            (norm_first_back, normed_attn, prepare_back, summary_back, reread_output, attended_low, norm_second_back, normed_mlp, gelu_back, activated)
        )
    block_output = hidden.astype(BF)
    grad_hidden = cotangent.astype(F32)
    chunks = [None] * layer_count
    small_grads = [None] * layer_count
    for layer in reversed(range(layer_count)):
        (norm_first_back, normed_attn, prepare_back, summary_back, reread_output, attended_low, norm_second_back, normed_mlp, gelu_back, activated) = saved[layer]
        w_in, w_out, w_up, w_down = parts[layer]
        grad_low = grad_hidden.astype(BF)
        g_down = jnp.einsum("mro,mrkc->koc", grad_low, activated, preferred_element_type=F32)
        grad_activated = jnp.einsum("mro,koc->mrkc", grad_low, w_down, preferred_element_type=F32)
        grad_upward = gelu_back(grad_activated)[0].astype(BF)
        g_up = jnp.einsum("mrd,mrkc->kdc", normed_mlp, grad_upward, preferred_element_type=F32)
        grad_normed_mlp = jnp.einsum("mrkc,kdc->mrd", grad_upward, w_up, preferred_element_type=F32)
        grad_middle_norm, gg2, gb2 = norm_second_back(grad_normed_mlp)
        grad_middle = grad_hidden + grad_middle_norm
        grad_branch = grad_middle.astype(BF)
        g_out = jnp.einsum("mro,mri->oi", grad_branch, attended_low, preferred_element_type=F32)
        grad_attended = jnp.einsum("mro,oi->mri", grad_branch, w_out, preferred_element_type=F32)
        gq, gk, gv, gs, gn = reread_output(grad_attended)
        outgoing = exchange((gs, gn), give)
        gk_more, gv_more = summary_back(outgoing)
        grad_projected, g_maps = prepare_back((gq, gk + gk_more, gv + gv_more))
        grad_projected_low = grad_projected.astype(BF)
        g_in = jnp.einsum("mrc,mrd->cd", grad_projected_low, normed_attn, preferred_element_type=F32)
        grad_normed_attn = jnp.einsum("mrc,cd->mrd", grad_projected_low, w_in, preferred_element_type=F32)
        grad_hidden_norm, gg1, gb1 = norm_first_back(grad_normed_attn)
        grad_hidden = grad_middle + grad_hidden_norm
        chunks[layer] = jnp.concatenate(
            [
                jnp.transpose(g_in.astype(BF).reshape(4, 3, 192, D), (1, 0, 2, 3)),
                g_out.astype(BF).reshape(1, 4, 192, D),
                jnp.transpose(g_up.astype(BF).reshape(4, 4, 192, D), (1, 0, 2, 3)),
                g_down.astype(BF).reshape(4, 4, 192, D),
            ]
        )
        small_grads[layer] = jnp.concatenate(
            [jnp.stack([gg1, gg2])[:, None], jnp.stack([gb1, gb2])[:, None], g_maps], axis=1
        )
    small_grads = jnp.stack(small_grads).reshape(-1, 4, 192)
    small_rows = jnp.transpose(small_grads, (1, 0, 2)).reshape(1, 4, -1, D).astype(BF)
    small_count = small_rows.shape[2]
    small_rows = jnp.pad(small_rows, ((0, 0), (0, 0), (0, 192 - small_count), (0, 0)))
    everything = jnp.concatenate(chunks[::-1] + [small_rows])
    everything = jnp.swapaxes(everything.reshape(-1, 2, 2, 192, D), 1, 2)
    total = reduce_grads(n, everything)
    big = total[:-1].reshape(layer_count, 12, 192, D)[::-1]
    small_total = total[-1, :small_count].reshape(layer_count, 2, 66, 192)
    grad_in = jnp.swapaxes(big[:, :3].reshape(layer_count, 576, D), 1, 2)
    grad_out = jnp.swapaxes(big[:, 3], 1, 2)
    grad_up = big[:, 4:8].reshape(layer_count, D, D)
    grad_down = jnp.transpose(big[:, 8:], (0, 1, 3, 2)).reshape(layer_count, 3072, 192)
    return (
        block_output,
        grad_hidden.astype(BF),
        grad_in,
        grad_out,
        grad_up,
        grad_down,
        small_total[:, :, 0],
        small_total[:, :, 1],
        small_total[:, :, 2:],
        small_total[:, 1, 1],
    )


def solution(mesh):
    in_specs = (
        P("batch", "seq", None),
        P("batch", "seq", None),
        P("batch", None),
        P(None, None, "batch"),
        P(None, None, "batch"),
        P(None, None, "batch"),
        P(None, None, "batch"),
        P(None, None, "batch"),
        P(None, None, "batch"),
        P(None, None, None, "batch"),
    )
    out_specs = (
        P("batch", "seq", None),
        P("batch", "seq", None),
        P(None, None, "batch"),
        P(None, None, "batch"),
        P(None, None, "batch"),
        P(None, None, "batch"),
        P(None, None, "batch"),
        P(None, None, "batch"),
        P(None, None, None, "batch"),
        P(None, "batch"),
    )
    return jax.shard_map(shards, mesh=mesh, in_specs=in_specs, out_specs=out_specs, check_vma=False)
```

time: 1610 us -> 963 us (0.60)
  waiting for transfers between devices: 896 us -> 103 us
  Pallas kernels: 0 us -> 421 us
  blocking collectives: 220 us -> 0 us
  other arithmetic: 134 us -> 61.1 us
  local copies, waits for them, and re-layouts: 134 us -> 206 us
  matrix products: 185 us -> 143 us
    psum x1 -> x0, waiting for transfers between devices: 437 us -> none  [shards(): lax.psum((shares[0], shares[1], shares[2], shares[3], shares[4], shares[5...]
    pallas_call x0 -> x2, Pallas kernels: none -> 421 us  [the longest x1 225 us: gather_weights(): pl.pallas_call(gather_kernel, name='gather_weights', out_shape=(jax.Shape...]
    reduce_scatter x8 -> x0, waiting for transfers between devices: 271 us -> none  [the longest x1 48.5 us: shards(): lax.psum_scatter(first_grads[2].astype(jnp.bfloat16), 'batch', scatter_di...]
    all_gather x11 -> x0, blocking collectives: 198 us -> none  [the longest x3 86 us: carried_in(): lax.all_gather(part.astype(kind), axis)]
    unnamed x33 -> x4, waiting for transfers between devices: 89 us -> 0.07 us
    slice x11 -> x22, local copies, waits for them, and re-layouts: 21.1 us -> 64.7 us  [the longest x1 13.9 us: shards(): weights[l, 3072:6144].reshape(4, 768, 768)]
    dynamic_slice x60 -> x0, local copies, waits for them, and re-layouts: 42.4 us -> none  [the longest x32 22.7 us: step(): part[k].astype(own.dtype)]
    another operation x24 -> x3, other arithmetic: 33.8 us -> 1.81 us  [shards(): small_grads = jnp.stack(small_grads).reshape(-1, 4, 192)]
  transfers between devices with their start and end apart: 27 -> 4, of which waited for: 18 -> 4; matrix products, arithmetic and copies ran while one was open for 19% -> 13% of each run, Pallas kernels for 0% -> 0%
where the time goes in v1:
time: 963 us; the launch traced here: 951 us
  Pallas kernels  421 us (44%)
  local copies, waits for them, and re-layouts  206 us (21%)
  matrix products  143 us (15%)
  waiting for transfers between devices  103 us (11%)
  other arithmetic  61.1 us (6%)
  between operations  17.7 us (2%)
    pallas_call x1, Pallas kernels, gather_weights(): pl.pallas_call(gather_kernel, name='gather_weights', out_shape=(jax.Shape...  225 us
    pallas_call x1, Pallas kernels, reduce_grads(): pl.pallas_call(functools.partial(reduce_kernel, n, N, R), name='reduce_gr...  196 us
    all_gather x4, waiting for transfers between devices, exchange(): lax.all_gather(both.reshape(micro_count, H * 2 * HD * (HD + 1)), 'seq')  103 us
    unnamed x559, local copies, waits for them, and re-layouts  51 us
  transfers between devices with their start and end apart: 4, of which 4 were waited for; matrix products, arithmetic and copies ran while one was open for 13% of the time, Pallas kernels for 0%

profile of v1, /device:TPU:0, one launch (start us, length us, event | category | flops | bytes accessed | tf_op | source)
XLA Modules:
  0.0 951.5 jit_solution(1520088747452558420)
XLA Ops:
  10.0 5.7 pad_maximum_fusion.w_ref
  15.7 225.1 %gather_weights.1 = (bf16[2,9216,768]{2,1,0:T(8,128)(2,1)}, bf16[4,272,256]{2,1,0:T(8,128)(2,1)}) custom-call(bf16[2,2304,768]{2,1,0:T(8,128)(2,1)} %pad_maximum_fusion.w_ref, bf16[272,256]{1,0:T(8,128)(2,1)} %pad.38.s_ref), custom_call_target="tpu_custom_call" | custom-call | tf_op jit(solution)/shard_map/gather_weights/pallas_call | solution.py:205
  244.4 3.2 fusion.14
  275.9 13.9 %fusion.227 = (bf16[1,3072,768]{2,1,0:T(8,128)(2,1)}, bf16[1,3072,768]{2,1,0:T(8,128)(2,1)}, bf16[1,3072,768]{2,1,0:T(8,128)(2,1)}, bf16[1,3072,768]{2,1,0:T(8,128)(2,1)}) fusion(bf16[2,9216,768]{2,1,0:T(8,128)(2,1)} %get-tuple-element.13), kind=kLoop, calls=%fused_computation.411 | loop fusion | bytes 37748736 | tf_op jit(solution)/shard_map/slice | solution.py:314
  289.8 35.4 %all-gather.5.cloned.1.call-done = bf16[8,2,99840]{2,1,0:T(2,128)(2,1)} async-done(((bf16[1,2,99840]{2,1,0:T(2,128)(2,1)}), bf16[8,2,99840]{2,1,0:T(2,128)(2,1)}) %all-gather.5.cloned.1.call-update) | async-done | bytes 3194896 | tf_op jit(solution)/shard_map/all_gather | solution.py:293
  325.2 2.9 fusion.22
  329.4 3.5 reshape.579
  336.7 3.6 divide_convert_fusion.1
  342.7 2.6 fusion.210
  347.7 3.2 fusion.10
  356.3 12.7 %fusion.240 = (f32[2,128,12]{1,0,2:T(2,128)}, f32[2,128,12,64]{1,3,0,2:T(8,128)S(1)}) fusion(f32[2,128,12,64]{1,3,0,2:T(8,128)S(1)} %convolution_bitcast_fusion.7), kind=kOutput, calls=%fused_computation.424 | output fusion | flops 589887 | bytes 1585152 | tf_op jit(solution)/shard_map/jvp()/sub | solution.py:235
  369.0 2.6 copy.798
  379.0 2.2 convert_element_type.233
  381.4 3.2 slice_bitcast_fusion.1
  384.5 2.4 copy.818
  386.9 2.4 copy.842
  403.2 37.8 %all-gather.7.cloned.1.call-done = bf16[8,2,99840]{2,1,0:T(2,128)(2,1)} async-done(((bf16[1,2,99840]{2,1,0:T(2,128)(2,1)}), bf16[8,2,99840]{2,1,0:T(2,128)(2,1)}) %all-gather.7.cloned.1.call-update) | async-done | bytes 3194896 | tf_op jit(solution)/shard_map/all_gather | solution.py:293
  441.0 2.9 fusion.20
  445.2 3.5 reshape.583
  448.7 3.3 fusion.119
  456.0 4.0 fusion.207
  461.7 3.7 fusion.37
  476.2 3.3 convert_element_type.242
  485.7 2.5 copy.794
  495.0 2.5 copy.812
  497.5 3.0 add_multiply_fusion.1
  510.9 2.6 fusion.218
  513.5 4.0 bitcast_convert_fusion.3
  517.5 3.9 bitcast_convert_fusion.2
  521.4 2.7 fusion.109
  524.1 15.1 %all-gather.9.cloned.1.call-done = bf16[8,2,99840]{2,1,0:T(2,128)(2,1)} async-done(((bf16[1,2,99840]{2,1,0:T(2,128)(2,1)}), bf16[8,2,99840]{2,1,0:T(2,128)(2,1)}) %all-gather.9.cloned.1.call-update) | async-done | bytes 3194896 | tf_op jit(solution)/shard_map/all_gather | solution.py:293
  539.2 2.9 fusion.18
  543.4 3.5 reshape.584
  550.7 2.5 fusion.100
  553.1 2.6 copy.831
  555.8 3.8 bitcast_add_fusion.1
  562.9 3.7 multiply_reduce_fusion.9
  568.9 3.3 fusion.30
  572.3 2.8 multiply_reduce_fusion.2
  585.6 3.3 convert_element_type.250
  589.7 2.9 add_multiply_fusion
  616.6 2.6 fusion.219
  619.2 4.9 bitcast_convert_fusion.1
  624.1 2.6 copy_dynamic-update-slice_fusion.1
  626.8 2.8 copy_dynamic-update-slice_fusion.3
  630.6 3.8 bitcast_convert_fusion
  634.4 14.2 %all-gather.11.cloned.1.call-done = bf16[8,2,99840]{2,1,0:T(2,128)(2,1)} async-done(((bf16[1,2,99840]{2,1,0:T(2,128)(2,1)}), bf16[8,2,99840]{2,1,0:T(2,128)(2,1)}) %all-gather.11.cloned.1.call-update) | async-done | bytes 3194896 | tf_op jit(solution)/shard_map/all_gather | solution.py:293
  648.6 2.9 fusion.16
  652.8 3.7 reshape.588
  662.0 3.8 bitcast_add_fusion
  672.1 3.2 fusion.144
  675.3 3.0 bitcast_convert_fusion.4
  683.8 2.6 convert_element_type.267
  692.0 2.6 copy_dynamic-update-slice_fusion
  694.5 2.7 copy_dynamic-update-slice_fusion.2
  698.3 195.7 %reduce_grads.1 = f32[25,192,768]{2,1,0:T(8,128)} custom-call(bf16[25,2,2,192,768]{4,3,2,1,0:T(8,128)(2,1)} %bitcast.502), custom_call_target="tpu_custom_call" | custom-call | tf_op jit(solution)/shard_map/reduce_grads/pallas_call | solution.py:117
  894.0 11.3 %slice.217 = f32[24,192,768]{2,1,0:T(8,128)} slice(f32[25,192,768]{2,1,0:T(8,128)} %reduce_grads.1), slice={[0:24], [0:192], [0:768]} | slice | bytes 28311552 | tf_op jit(solution)/shard_map/slice | solution.py:383
  905.3 8.3 fusion.228
  915.8 2.4 slice_bitcast_fusion
  925.5 2.6 reverse_bitcast_fusion
  928.1 2.9 copy.1043
  931.0 4.8 slice.223
  937.9 2.5 reverse_bitcast_fusion.1
  942.2 2.3 add_convert_fusion.4
  (793 shorter events, 194.9 us)
Async XLA Ops:
  7.2 318.0 %all-gather.5.cloned.1.call-start = ((), (), s32[]{:S(2)}) async-start(), calls=%async_computation | async-start | bytes 3594240 | tf_op jit(solution)/shard_map/all_gather | solution.py:293
  244.0 98.6 %copy-start.160 = (f32[768]{0:T(1024)}, f32[768]{0:T(1024)S(1)}, u32[]{:S(2)}) copy-start(f32[768]{0:T(1024)S(1)} %get-tuple-element.34) | copy-start | bytes 9220
  244.0 103.7 %copy-start.166 = (f32[768]{0:T(1024)}, f32[768]{0:T(1024)S(1)}, u32[]{:S(2)}) copy-start(f32[768]{0:T(1024)S(1)} %get-tuple-element.33) | copy-start | bytes 9220
  250.5 15.8 %copy-start.88 = (bf16[1,2,64,768]{2,3,1,0:T(8,128)(2,1)}, bf16[1,2,64,768]{2,3,1,0:T(8,128)(2,1)S(1)}, u32[]{:S(2)}) copy-start(bf16[1,2,64,768]{2,3,1,0:T(8,128)(2,1)S(1)} %copy.779) | copy-start | bytes 589828
  256.0 80.6 %copy-start.169 = (f32[2,128]{1,0:T(2,128)}, f32[2,128]{1,0:T(2,128)S(1)}, u32[]{:S(2)}) copy-start(f32[2,128]{1,0:T(2,128)S(1)} %get-tuple-element.85) | copy-start | bytes 3076
  263.8 177.1 %all-gather.7.cloned.1.call-start = ((), (), s32[]{:S(2)}) async-start(), calls=%async_computation.1 | async-start | bytes 3594240 | tf_op jit(solution)/shard_map/all_gather | solution.py:293
  266.2 59.0 %copy-start.216 = (bf16[2,8,1]{1,0,2:T(2,128)(2,1)}, bf16[2,8,1]{1,0,2:T(2,128)(2,1)S(1)}, u32[]{:S(2)}) copy-start(bf16[2,8,1]{1,0,2:T(2,128)(2,1)S(1)} %fusion.205) | copy-start | bytes 100
  270.1 66.5 %copy-start = (f32[2,128,12,64]{1,3,0,2:T(8,128)}, f32[2,128,12,64]{1,3,0,2:T(8,128)S(1)}, u32[]{:S(2)}) copy-start(f32[2,128,12,64]{1,3,0,2:T(8,128)S(1)} %get-tuple-element.126) | copy-start | bytes 2359300
  270.1 66.5 %copy-start.2 = (f32[2,128,12,64]{1,3,0,2:T(8,128)}, f32[2,128,12,64]{1,3,0,2:T(8,128)S(1)}, u32[]{:S(2)}) copy-start(f32[2,128,12,64]{1,3,0,2:T(8,128)S(1)} %get-tuple-element.127) | copy-start | bytes 2359300
  332.8 9.8 %slice-start.4 = ((s8[4718592]{0:T(1024)(128)(4,1)}), s8[4194304]{0:T(1024)(128)(4,1)S(1)}, s32[]{:S(2)}) async-start(s8[4718592]{0:T(1024)(128)(4,1)} %bitcast.509), calls=%async_computation.8 | async-start | bytes 8388608
  336.6 6.0 slice-start.5
  356.3 15.3 %copy-start.35 = (f32[2,128,12,64]{1,3,0,2:T(8,128)}, f32[2,128,12,64]{1,3,0,2:T(8,128)S(1)}, u32[]{:S(2)}) copy-start(f32[2,128,12,64]{1,3,0,2:T(8,128)S(1)} %get-tuple-element.105) | copy-start | bytes 2359300
  381.3 157.9 %all-gather.9.cloned.1.call-start = ((), (), s32[]{:S(2)}) async-start(), calls=%async_computation.2 | async-start | bytes 3594240 | tf_op jit(solution)/shard_map/all_gather | solution.py:293
  396.1 4.2 copy-start.4
  401.4 39.6 %copy-start.217 = (bf16[2,8,1]{1,0,2:T(2,128)(2,1)S(1)}, bf16[2,8,1]{1,0,2:T(2,128)(2,1)}, u32[]{:S(2)}) copy-start(bf16[2,8,1]{1,0,2:T(2,128)(2,1)} %copy-done.216) | copy-start | bytes 100
  452.1 19.4 %copy-start.152 = (f32[2,12,128]{2,1,0:T(8,128)}, f32[2,12,128]{2,1,0:T(8,128)S(1)}, u32[]{:S(2)}) copy-start(f32[2,12,128]{2,1,0:T(8,128)S(1)} %copy.819) | copy-start | bytes 36868
  452.1 9.5 %slice-start.14 = ((s8[4718592]{0:T(1024)(128)(4,1)}), s8[4194304]{0:T(1024)(128)(4,1)S(1)}, s32[]{:S(2)}) async-start(s8[4718592]{0:T(1024)(128)(4,1)} %bitcast.543), calls=%async_computation.18 | async-start | bytes 8388608
  455.7 11.8 %copy-start.14 = (f32[2,128,768]{2,1,0:T(8,128)}, f32[2,128,768]{2,1,0:T(8,128)S(1)}, u32[]{:S(2)}) copy-start(f32[2,128,768]{2,1,0:T(8,128)S(1)} %get-tuple-element.115) | copy-start | bytes 2359300
  455.7 11.8 %copy-start.191 = (f32[2,128]{1,0:T(2,128)}, f32[2,128]{1,0:T(2,128)S(1)}, u32[]{:S(2)}) copy-start(f32[2,128]{1,0:T(2,128)S(1)} %broadcast_multiply_fusion.6) | copy-start | bytes 3076
  455.7 5.9 slice-start.15
  456.0 11.5 %copy-start.199 = (f32[2,128]{1,0:T(2,128)}, f32[2,128]{1,0:T(2,128)S(1)}, u32[]{:S(2)}) copy-start(f32[2,128]{1,0:T(2,128)S(1)} %fusion.201) | copy-start | bytes 3076
  456.0 5.7 copy-start.118
  456.0 9.4 slice-start.8
  479.5 169.1 %all-gather.11.cloned.1.call-start = ((), (), s32[]{:S(2)}) async-start(), calls=%async_computation.3 | async-start | bytes 3594240 | tf_op jit(solution)/shard_map/all_gather | solution.py:293
  513.5 4.0 copy-start.117
  513.5 4.0 copy-start.119
  513.5 7.9 slice-start.16
  517.5 3.9 slice-start.17
  521.4 17.8 %copy-start.214 = (bf16[2,8,1]{1,0,2:T(2,128)(2,1)S(1)}, bf16[2,8,1]{1,0,2:T(2,128)(2,1)}, u32[]{:S(2)}) copy-start(bf16[2,8,1]{1,0,2:T(2,128)(2,1)} %fusion.204) | copy-start | bytes 100
  555.7 3.9 copy-start.36
  555.8 3.9 copy-start.38
  561.3 6.9 slice-start.12
  562.2 4.4 copy-start.107
  562.9 5.4 slice-start.13
  567.9 4.4 slice-start.6
  568.9 7.4 copy-start.67
  578.7 3.9 copy-start.58
  600.6 7.7 copy-start.51
  603.9 5.8 copy-start.96
  603.9 5.8 copy-start.134
  614.6 4.6 copy-start.47
  614.6 4.6 copy-start.100
  614.6 4.6 copy-start.161
  614.6 4.6 copy-start.190
  614.6 4.6 copy-start.198
  616.6 7.5 slice-start
  616.6 10.2 %slice-start.18 = ((s8[4718592]{0:T(1024)(128)(4,1)}), s8[4194304]{0:T(1024)(128)(4,1)S(1)}, s32[]{:S(2)}) async-start(s8[4718592]{0:T(1024)(128)(4,1)} %bitcast.551), calls=%async_computation.22 | async-start | bytes 8388608
  619.2 4.9 slice-start.1
  619.2 7.5 slice-start.19
  630.6 18.0 %copy-start.215 = (bf16[2,8,1]{1,0,2:T(2,128)(2,1)S(1)}, bf16[2,8,1]{1,0,2:T(2,128)(2,1)}, u32[]{:S(2)}) copy-start(bf16[2,8,1]{1,0,2:T(2,128)(2,1)} %fusion.204) | copy-start | bytes 100
  662.0 3.9 copy-start.27
  662.0 3.9 copy-start.180
  662.0 3.9 copy-start.181
  681.7 5.9 copy-start.94
  687.6 4.2 slice-start.2
  687.6 4.3 slice-start.3
  689.7 4.8 slice-start.20
  937.9 4.3 copy-start.238
  937.9 4.3 copy-start.57
  937.9 4.3 copy-start.69
  937.9 4.3 copy-start.83
  937.9 4.3 copy-start.221
  937.9 4.3 copy-start.223
  937.9 4.3 copy-start.226
  (213 other events, 459.1 us)
Sparse Core Ops, SparseCore 0:
  264.0 61.1 all-gather.4
  381.4 59.5 all-gather.6
  479.7 59.5 all-gather.8
  589.1 59.4 all-gather.10

commit v2 on v1

v2 whole, which is shorter than its diff:
```python
import functools

import jax
import jax.numpy as jnp
from jax import lax
from jax.experimental import pallas as pl
from jax.experimental.pallas import tpu as pltpu
from jax.sharding import PartitionSpec as P

D = 768
H = 12
HD = 64
EPSILON = 1e-05
GELU = 0.7978845608028654
STATE_ROWS = 896
F32 = jnp.float32
BF = jnp.bfloat16
MESH = pl.DeviceIdType.MESH


def greet(peers):
    bar = pltpu.get_barrier_semaphore()
    for p in peers:
        pl.semaphore_signal(bar, inc=1, device_id=p, device_id_type=MESH)
    pl.semaphore_wait(bar, len(peers))

def remote(src, dst, ss, rs, dev):
    return pltpu.make_async_remote_copy(src_ref=src, dst_ref=dst, send_sem=ss, recv_sem=rs, device_id=dev, device_id_type=MESH)

def arrive(ref, sem):
    pltpu.make_async_copy(ref, ref, sem).wait()

def offsets(c, b):
    if c < 3:
        return b * 576 + c * 192
    if c < 4:
        return 2304 + b * 192
    if c < 8:
        return 3072 + b * 768 + (c - 4) * 192
    return 6144 + (c - 8) * 768 + b * 192


def small_kernel(s_ref, t_ref, sem, here_sem):
    s = lax.axis_index("seq")
    b = lax.axis_index("batch")
    others = [(s, (b + k) % 4) for k in range(1, 4)]
    greet(others)
    copies = [remote(s_ref, t_ref.at[b], sem.at[0, k], sem.at[1, 2 - k], dev) for k, dev in enumerate(others)]
    for copy in copies:
        copy.start()
    t_ref[b] = s_ref[...]
    for copy in copies:
        copy.wait()


def gather_small(small):
    return pl.pallas_call(
        small_kernel,
        name="gather_small",
        out_shape=jax.ShapeDtypeStruct((4,) + small.shape, BF),
        in_specs=[pl.BlockSpec(memory_space=pltpu.VMEM)],
        out_specs=pl.BlockSpec(memory_space=pltpu.VMEM),
        scratch_shapes=[pltpu.SemaphoreType.DMA((2, 3)), pltpu.SemaphoreType.DMA((1,))],
        compiler_params=pltpu.CompilerParams(collective_id=2, has_side_effects=True),
    )(small)


def nn(a, b):
    return lax.dot_general(a, b, (((1,), (0,)), ((), ())), preferred_element_type=F32)


def nt(a, b):
    return lax.dot_general(a, b, (((1,), (1,)), ((), ())), preferred_element_type=F32)


def normalize(v):
    centred = v - jnp.mean(v, axis=-1, keepdims=True)
    return centred * lax.rsqrt(jnp.mean(centred * centred, axis=-1, keepdims=True) + EPSILON)


def span(i, k):
    return pl.ds(pl.multiple_of(i * k, k), k)


def owners(n):
    group = max(16, STATE_ROWS // n)
    return group, STATE_ROWS // group


def parts_of(v):
    high = v.astype(BF)
    return high, (v - high.astype(F32)).astype(BF)


class Exchange:
    def __init__(self, n, seq, batch, state, taken, sums, got, sem):
        self.n, self.seq, self.batch = n, seq, batch
        self.state, self.taken, self.sums, self.got, self.sem = state, taken, sums, got, sem
        self.group, self.count = owners(n)

    def outgoing(self, d):
        peer = (self.seq + d) % self.n
        return peer, remote(
            self.state.at[:, span(peer % self.count, self.group)], self.taken.at[self.seq],
            self.sem.at[0], self.sem.at[1], (peer, self.batch),
        )

    def returning(self, d):
        peer = (self.seq + d) % self.n
        return remote(
            self.sums.at[peer], self.got.at[:, span(self.seq % self.count, self.group)],
            self.sem.at[2], self.sem.at[3], (peer, self.batch),
        )

    def owned(self, fn):
        if self.count == self.n:
            fn()
        else:
            pl.when(self.seq < self.count)(fn)

    def send(self):
        for d in range(1, self.n):
            peer, copy = self.outgoing(d)
            if self.count == self.n:
                copy.start()
            else:
                pl.when(peer < self.count)(copy.start)

        def keep():
            self.taken[self.seq] = self.state[:, span(self.seq % self.count, self.group)]

        self.owned(keep)

    def turn(self, coef):
        def work():
            arrive(self.taken.at[pl.ds(0, self.n - 1)], self.sem.at[1])

            def one(p, carry):
                for r in range(2):
                    def add(k, total):
                        return total + coef[(r * self.n + p) * self.n + k] * self.taken[k, r].astype(F32)

                    zero = jnp.zeros((self.group, 128), F32)
                    if self.n <= 8:
                        total = zero
                        for k in range(self.n):
                            total = add(k, total)
                    else:
                        total = lax.fori_loop(0, self.n, add, zero)
                    self.sums[p, r] = total.astype(BF)
                return carry

            lax.fori_loop(0, self.n, one, 0)
            for d in range(1, self.n):
                self.returning(d).start()
            self.got[:, span(self.seq % self.count, self.group)] = self.sums[self.seq]

        self.owned(work)

    def receive(self):
        if self.count == self.n:
            arrive(self.got.at[:, pl.ds(0, self.group * (self.n - 1))], self.sem.at[3])
        else:
            @pl.when(self.seq < self.count)
            def _():
                arrive(self.got.at[:, pl.ds(0, self.group * (self.count - 1))], self.sem.at[3])

            @pl.when(self.seq >= self.count)
            def _():
                arrive(self.got.at[:, pl.ds(0, self.group * self.count)], self.sem.at[3])

    def finish(self):
        if self.count == self.n:
            arrive(self.state.at[:, pl.ds(0, self.group * (self.n - 1))], self.sem.at[0])
            arrive(self.sums.at[pl.ds(0, self.n - 1)], self.sem.at[2])
        else:
            @pl.when(self.seq < self.count)
            def _():
                arrive(self.state.at[:, pl.ds(0, self.group * (self.count - 1))], self.sem.at[0])
                arrive(self.sums.at[pl.ds(0, self.n - 1)], self.sem.at[2])

            @pl.when(self.seq >= self.count)
            def _():
                arrive(self.state.at[:, pl.ds(0, self.group * self.count)], self.sem.at[0])


def forward_kernel(
    n, tok, w_ref, norms, maps, mask, chain, last, coef,
    o_w, o_h, o_mid, o_na, o_nm, o_qkv, o_phi, o_att, o_rz, o_act, o_dg, o_got, o_lo, o_attl, o_out,
    w, h, mid, na, nm, qkv, phi, att, attl, rz, act, dg, got, proj, pq, num, zz, norm_sum, state, taken, sums, qlo, mu, means,
    lsem, ysem, xsem, own_sem, near_sem, far_sem, esem, msem, ssem,
):
    s = lax.axis_index("seq")
    b = lax.axis_index("batch")
    xl = s % 2
    core = b + 1 - 2 * (b % 2)
    far = (b + 2) % 4
    layers = 2
    core_dev, y_dev, x_dev = (s, core), (s, far), (s + 1 - 2 * xl, b)
    greet([core_dev, y_dev] + [((s + d) % n, b) for d in range(1, n)])

    def rows(c, who, part, size):
        return pl.ds(pl.multiple_of(offsets(c % 12, who) + part * 96, 32), size)

    def same(c, who, part, size, sem, dev):
        place = w.at[c // 12, rows(c, who, part, size)]
        return remote(place, place, sem.at[0, c], sem.at[1, c], dev)

    def here(c):
        return w_ref.at[c // 12, pl.ds((c % 12) * 192, 192)]

    def out_y(c):
        src = w_ref.at[c // 12, pl.ds(pl.multiple_of((c % 12) * 192 + xl * 96, 32), 96)]
        return remote(src, w.at[c // 12, rows(c, b, xl, 96)], ysem.at[0, c], ysem.at[1, c], y_dev)

    def out_core(c):
        return remote(here(c), w.at[c // 12, rows(c, b, 0, 192)], own_sem.at[0, c], own_sem.at[1, c], core_dev)

    def stay(c):
        return pltpu.make_async_copy(here(c), w.at[c // 12, rows(c, b, 0, 192)], lsem.at[c])

    out_x = lambda c: same(c, far, xl, 96, xsem, x_dev)
    near = lambda c: same(c, far, xl, 96, near_sem, core_dev)
    rest = lambda c: same(c, far, 1 - xl, 96, far_sem, core_dev)
    count = layers * 12
    for c in range(count):
        out_y(c).start()
        out_core(c).start()
        stay(c).start()

    place = [0]

    def pump(k=1):
        for _ in range(k):
            c = place[0]
            if c > count:
                return
            if c < count:
                out_y(c).wait_recv()
                out_x(c).start()
                near(c).start()
            if c >= 1:
                out_x(c - 1).wait_recv()
                rest(c - 1).start()
            place[0] += 1

    def need(lo, hi):
        while place[0] <= hi:
            pump()
        for c in range(lo, hi):
            stay(c).wait()
            for copy in (out_core(c), near(c), rest(c)):
                copy.wait_recv()

    def mean_copy(l, d):
        peer = (s + d) % n
        return remote(means.at[l, s], means.at[l, s], msem.at[l, 0], msem.at[l, 1], (peer, b))

    stores = []

    def store(src, dst, i):
        copy = pltpu.make_async_copy(src, dst, ssem.at[i])
        copy.start()
        stores.append(copy)
        return copy

    left = lax.broadcasted_iota(jnp.int32, (128, 128), 1) < 64
    lanes = lax.broadcasted_iota(jnp.int32, (128, 128), 1)
    rows_i = lax.broadcasted_iota(jnp.int32, (128, 128), 0)
    ones = jnp.ones((128, 128), BF)
    h[0] = tok[...].astype(F32)
    phi_store = act_store = dg_store = None
    for l in range(layers):
        base = l * 12
        na[l] = (normalize(h[l]) * norms[l, 0, 0:1] + norms[l, 0, 1:2]).astype(BF)
        own = [jnp.mean(na[l, r * 128 : (r + 1) * 128].astype(F32), axis=0, keepdims=True) for r in range(2)]
        means[l, s] = jnp.concatenate(own + [jnp.zeros((6, D), F32)], axis=0)
        for d in range(1, n):
            mean_copy(l, d).start()
        need(base, base + 3)
        for t in range(9):
            piece = nt(na[l], w[l, t * 256 : (t + 1) * 256])
            if t < 6:
                proj[:, t * 256 : (t + 1) * 256] = piece
            else:
                if t == 6:
                    arrive(means.at[l, pl.ds(0, n - 1)], msem.at[l, 1])
                    mean = lax.fori_loop(0, n, lambda k, v: v + means[l, k], jnp.zeros((8, D), F32)) / n
                    mean = jnp.concatenate([mean, mean], axis=0).astype(BF)
                shift = nt(mean, w[l, t * 256 : (t + 1) * 256])[:8]
                mu[:, (t - 6) * 256 : (t - 5) * 256] = shift
                piece = jnp.concatenate([piece[:128] - shift[:1], piece[128:] - shift[1:2]], axis=0)
            qkv[l, :, t * 256 : (t + 1) * 256] = piece.astype(BF)
            if t == 4:
                pump()
        if phi_store is not None:
            phi_store.wait()
            stores[:] = [c for c in stores if c is not phi_store]
        norm_sum[...] = jnp.zeros_like(norm_sum)

        def value(hp, r):
            return jnp.concatenate([qkv[l, pl.ds(r * 128, 128), pl.ds(pl.multiple_of(1536 + hp * 128, 128), 128)], ones], axis=1)

        def features(hp, carry):
            for which in range(2):
                x = proj[:, pl.ds(pl.multiple_of(which * 768 + hp * 128, 128), 128)]
                high = x.astype(BF)
                low = (x - high.astype(F32)).astype(BF)
                qlo[l, :, pl.ds(pl.multiple_of(which * 768 + hp * 128, 128), 128)] = low
                m = maps[l, which, hp]
                logits = nt(m, high) + nt(m, low)
                for half in range(2):
                    t = logits[64 * half : 64 * half + 64]
                    up = jnp.exp(t - jnp.max(t, axis=0, keepdims=True))
                    down = jnp.exp(jnp.min(t, axis=0, keepdims=True) - t)
                    at = pl.multiple_of(hp * 256 + half * 128, 128)
                    phi[which, pl.ds(at, 64)] = (up * (1.0 / jnp.sum(up, axis=0, keepdims=True))).astype(BF)
                    phi[which, pl.ds(at + 64, 64)] = (down * (1.0 / jnp.sum(down, axis=0, keepdims=True))).astype(BF)
            for r in range(2):
                v = value(hp, r)
                got_ = []
                for half in range(2):
                    key = phi[1, pl.ds(pl.multiple_of(hp * 256 + half * 128, 128), 128), r * 128 : (r + 1) * 128]
                    both = nn((key.astype(F32) * last[r]).astype(BF), v)
                    got_.append(both[:, :128])
                    norm_sum[r] += jnp.where(lanes % 64 == hp * 2 + half, both[:, 128:], 0.0)
                state[l, r, span(hp, 128)] = jnp.where(left, got_[0], got_[1]).astype(BF)
            return carry

        lax.fori_loop(0, 6, features, 0)
        for r in range(2):
            state[l, r, 768:896] = norm_sum[r].astype(BF)
        swap = Exchange(n, s, b, state.at[l], taken.at[l], sums.at[l], got.at[l], esem.at[l])
        swap.send()
        phi_store = store(phi, o_phi.at[l], l * 16 + 0)
        store(na.at[l], o_na.at[l], l * 16 + 1)
        store(qlo.at[l], o_lo.at[l], l * 16 + 13)
        store(qkv.at[l], o_qkv.at[l], l * 16 + 2)
        store(h.at[l], o_h.at[l], l * 16 + 3)
        pump()

        def scores(hp, carry):
            for r in range(2):
                v = value(hp, r)
                both = []
                for half in range(2):
                    at = pl.ds(pl.multiple_of(hp * 256 + half * 128, 128), 128)
                    query = phi[0, at, r * 128 : (r + 1) * 128].astype(F32).T.astype(BF)
                    pq[r * 128 : (r + 1) * 128, at] = query
                    key = phi[1, at, r * 128 : (r + 1) * 128]
                    both.append(nn((nn(query, key) * mask[r]).astype(BF), v))
                at = span(hp, 128)
                num[r * 128 : (r + 1) * 128, at] = jnp.where(left, both[0][:, :128], both[1][:, :128])
                zz[r * 128 : (r + 1) * 128, at] = jnp.where(left, both[0][:, 128:], both[1][:, 128:])
            return carry

        lax.fori_loop(0, 3, scores, 0)
        swap.turn(coef)
        lax.fori_loop(3, 6, scores, 0)
        pump()
        swap.receive()

        def finish(hp, carry):
            at = span(hp, 128)
            for r in range(2):
                both = []
                for half in range(2):
                    query = pq[r * 128 : (r + 1) * 128, pl.ds(pl.multiple_of(hp * 256 + half * 128, 128), 128)]
                    pick = (rows_i == hp * 2 + half).astype(BF)
                    column = nn(got[l, r, 768:896], pick).astype(BF)
                    both.append(nn(query, jnp.concatenate([got[l, r, at], column], axis=1)))
                c = chain[r]
                z = zz[r * 128 : (r + 1) * 128, at] + c * jnp.where(left, both[0][:, 128:], both[1][:, 128:])
                top = num[r * 128 : (r + 1) * 128, at] + c * jnp.where(left, both[0][:, :128], both[1][:, :128])
                inverse = 1.0 / z
                out = top * inverse
                rz[l, r * 128 : (r + 1) * 128, at] = inverse
                att[l, r * 128 : (r + 1) * 128, at] = out
                attl[l, r * 128 : (r + 1) * 128, at] = (out + mu[r : r + 1, at]).astype(BF)
            return carry

        lax.fori_loop(0, 6, finish, 0)
        store(got.at[l], o_got.at[l], l * 16 + 4)
        store(rz.at[l], o_rz.at[l], l * 16 + 5)
        store(att.at[l], o_att.at[l], l * 16 + 6)
        store(attl.at[l], o_attl.at[l], l * 16 + 7)
        need(base + 3, base + 4)
        for t in range(3):
            at = slice(t * 256, (t + 1) * 256)
            mid[l, :, at] = h[l, :, at] + nt(attl[l], w[l, 2304 + t * 256 : 2304 + (t + 1) * 256])
        nm[l] = (normalize(mid[l]) * norms[l, 1, 0:1] + norms[l, 1, 1:2]).astype(BF)
        store(mid.at[l], o_mid.at[l], l * 16 + 8)
        store(nm.at[l], o_nm.at[l], l * 16 + 9)
        need(base + 4, base + 8)
        if act_store is not None:
            for copy in (act_store, dg_store):
                copy.wait()
                stores[:] = [c for c in stores if c is not copy]
        for k in range(4):
            for t in range(3):
                at = slice(t * 256, (t + 1) * 256)
                u = nn(nm[l], w[l, 3072 + k * 768 : 3072 + (k + 1) * 768, at])
                square = u * u
                bend = jnp.tanh(GELU * u * (1.0 + 0.044715 * square))
                act[k, :, at] = (0.5 * u * (1.0 + bend)).astype(BF)
                slope = 0.5 * (1.0 + bend) + 0.5 * u * (1.0 - bend * bend) * GELU * (1.0 + 0.134145 * square)
                dg[k, :, at] = slope.astype(BF)
            pump()
        act_store = store(act, o_act.at[l], l * 16 + 10)
        dg_store = store(dg, o_dg.at[l], l * 16 + 11)
        for k in range(4):
            need(base + 8 + k, base + 9 + k)
            for t in range(3):
                at = slice(t * 256, (t + 1) * 256)
                first = 6144 + k * 768 + t * 256
                y = nt(act[k], w[l, first : first + 256])
                before = mid[l, :, at] if k == 0 else h[l + 1, :, at]
                h[l + 1, :, at] = before + y
        store(w.at[l], o_w.at[l], l * 16 + 12)
    o_out[...] = h[layers].astype(BF)
    for copy in stores:
        copy.wait()
    for l in range(layers):
        arrive(means.at[l, pl.ds(0, n - 1)], msem.at[l, 0])
        Exchange(n, s, b, state.at[l], taken.at[l], sums.at[l], got.at[l], esem.at[l]).finish()
    for c in range(count):
        for copy in (out_y(c), out_x(c), out_core(c), near(c), rest(c)):
            copy.wait_send()


def forward(n, tok, w, norms, maps, mask, chain, last, coef):
    group, _ = owners(n)
    m = tok.shape[0]
    hbm = lambda shape, kind: jax.ShapeDtypeStruct(shape, kind)
    outs = (
        hbm((2, 9216, D), BF), hbm((2, m, D), F32), hbm((2, m, D), F32), hbm((2, m, D), BF), hbm((2, m, D), BF),
        hbm((2, m, 2304), BF), hbm((2, 2, 1536, m), BF), hbm((2, m, D), F32), hbm((2, m, D), F32),
        hbm((2, 4, m, D), BF), hbm((2, 4, m, D), BF), hbm((2, 2, STATE_ROWS, 128), BF), hbm((2, m, 1536), BF), hbm((2, m, D), BF), hbm((m, D), BF),
    )
    vmem = pl.BlockSpec(memory_space=pltpu.VMEM)
    anywhere = pl.BlockSpec(memory_space=pl.ANY)
    pair = lambda: pltpu.SemaphoreType.DMA((2, 24))
    V = lambda kind, *shape: pltpu.VMEM(shape, kind)
    return pl.pallas_call(
        functools.partial(forward_kernel, n),
        name="forward",
        out_shape=outs,
        in_specs=[vmem, anywhere, vmem, vmem, vmem, vmem, vmem, pl.BlockSpec(memory_space=pltpu.SMEM)],
        out_specs=[anywhere] * 14 + [vmem],
        scratch_shapes=[
            V(BF, 2, 9216, D), V(F32, 3, m, D), V(F32, 2, m, D), V(BF, 2, m, D), V(BF, 2, m, D), V(BF, 2, m, 2304),
            V(BF, 2, 1536, m), V(F32, 2, m, D), V(BF, 2, m, D), V(F32, 2, m, D), V(BF, 4, m, D), V(BF, 4, m, D),
            V(BF, 2, 2, STATE_ROWS, 128), V(F32, m, 1536), V(BF, m, 1536), V(F32, m, D), V(F32, m, D), V(F32, 2, 128, 128),
            V(BF, 2, 2, STATE_ROWS, 128), V(BF, 2, n, 2, group, 128), V(BF, 2, n, 2, group, 128), V(BF, 2, m, 1536), V(F32, 8, D), V(F32, 2, n, 8, D),
            pltpu.SemaphoreType.DMA((24,)), pair(), pair(), pair(), pair(), pair(),
            pltpu.SemaphoreType.DMA((2, 4)), pltpu.SemaphoreType.DMA((2, 2)), pltpu.SemaphoreType.DMA((32,)),
        ],
        compiler_params=pltpu.CompilerParams(collective_id=0, has_side_effects=True, vmem_limit_bytes=63 * 2**20),
    )(tok, w, norms, maps, mask, chain, last, coef)


def norm_back(y, v, gain):
    centred = v - jnp.mean(v, axis=-1, keepdims=True)
    scale = lax.rsqrt(jnp.mean(centred * centred, axis=-1, keepdims=True) + EPSILON)
    n = centred * scale
    yg = y * gain
    back = scale * (yg - jnp.mean(yg, axis=-1, keepdims=True) - n * jnp.mean(yg * n, axis=-1, keepdims=True))
    return back, jnp.sum(n * y, axis=0, keepdims=True), jnp.sum(y, axis=0, keepdims=True)


def softmax_back(s, g):
    s = s.astype(F32)
    plus, minus = s[:64], s[64:]
    mean = lambda p, v: jnp.sum(p * v, axis=0, keepdims=True) / jnp.sum(p, axis=0, keepdims=True)
    up = plus * (g[:64] - mean(plus, g[:64]))
    down = minus * (g[64:] - mean(minus, g[64:]))
    return up - down


CHUNK = 192


def backward_kernel(
    n, count,
    cot, norms, maps, mask, chain, last, coef,
    i_w, i_h, i_mid, i_na, i_nm, i_qkv, i_phi, i_att, i_rz, i_act, i_dg, i_got, i_lo, i_attl,
    o_grad, o_tok,
    recv_c, recv_y, recv_x, recv_1, recv_2, recv_h, g, wbuf, actb, dgb, nm, mid, att, rz, qkv, phi, got, na, h, qlo, attl,
    gh, du, gatt, gphik, gvt, dqkvt, flip, dn, gm, gnorm, norm_sum, state, taken, sums, back,
    csem, ysem, xsem, z1sem, z2sem, hsem, a2sem, a1sem, bsem, osem, esem, wsem, asem, lsem,
):
    s = lax.axis_index("seq")
    b = lax.axis_index("batch")
    xl, z = s % 2, s // 2
    b0, b1 = z % 2, (z // 2) % 2
    par, yy = b % 2, b // 2
    levels = [v for v in range(2, 10) if (1 << v) < n // 2]
    core_dev, y_dev, x_dev = (s, b + 1 - 2 * par), (s, (b + 2) % 4), (s + 1 - 2 * xl, b)
    z1_dev, z2_dev = (s + 2 * (1 - 2 * b0), b), (s + 4 * (1 - 2 * b1), b)
    h_dev = lambda v: (s + (2 << v) * (1 - 2 * ((z // (1 << v)) % 2)), b)
    greet([core_dev, y_dev] + [((s + d) % n, b) for d in range(1, n)])

    quarter_rows = CHUNK // 4
    xc, xo = span(xl, 384), span(1 - xl, 384)
    half = span(b0, CHUNK // 2)
    quarter = pl.ds(pl.multiple_of(b0 * (CHUNK // 2) + b1 * quarter_rows, 16), quarter_rows)
    fin = recv_y
    cC = lambda c: remote(g.at[c % 2, 1 - par], recv_c.at[c], csem.at[0, c], csem.at[1, c], core_dev)
    cY = lambda c: remote(recv_c.at[c, 1 - yy], recv_y.at[c], ysem.at[0, c], ysem.at[1, c], y_dev)
    cX = lambda c: remote(recv_y.at[c, :, xo], recv_x.at[c], xsem.at[0, c], xsem.at[1, c], x_dev)
    cZ1 = lambda c: remote(recv_x.at[c, span(1 - b0, CHUNK // 2)], recv_1.at[c], z1sem.at[0, c], z1sem.at[1, c], z1_dev)
    cZ2 = lambda c: remote(recv_1.at[c, span(1 - b1, quarter_rows)], recv_2.at[c], z2sem.at[0, c], z2sem.at[1, c], z2_dev)
    cH = lambda c, i: remote(recv_h.at[c, len(levels)], recv_h.at[c, i], hsem.at[0, c, i], hsem.at[1, c, i], h_dev(levels[i]))
    cA2 = lambda c: remote(fin.at[c, quarter, xc], fin.at[c, quarter, xc], a2sem.at[0, c], a2sem.at[1, c], z2_dev)
    cA1 = lambda c: remote(fin.at[c, half, xc], fin.at[c, half, xc], a1sem.at[0, c], a1sem.at[1, c], z1_dev)
    cB = lambda c: remote(fin.at[c, :, xc], fin.at[c, :, xc], bsem.at[0, c], bsem.at[1, c], x_dev)
    cO = lambda c: pltpu.make_async_copy(fin.at[c], o_grad.at[c], osem.at[c])

    def add(a, b_):
        return (a.astype(F32) + b_.astype(F32)).astype(BF)

    def absorb(c):
        cC(c).wait_recv()
        recv_c[c] = add(recv_c[c], g[c % 2, par])

    def stage_y(c):
        cY(c).start()

    def stage_x(c):
        cY(c).wait_recv()
        recv_y[c, :, xo] = add(recv_y[c, :, xo], recv_c[c, yy, :, xo])
        cX(c).start()
        recv_y[c, :, xc] = add(recv_y[c, :, xc], recv_c[c, yy, :, xc])

    def stage_z1(c):
        cX(c).wait_recv()
        recv_x[c] = add(recv_x[c], recv_y[c, :, xc])
        cZ1(c).start()

    def stage_z2(c):
        cZ1(c).wait_recv()
        recv_1[c] = add(recv_1[c], recv_x[c, half])
        cZ2(c).start()

    def stage_a2(c):
        cZ2(c).wait_recv()
        cX(c).wait_send()
        t = add(recv_2[c], recv_1[c, span(b1, quarter_rows)])
        for i in range(len(levels)):
            recv_h[c, len(levels)] = t
            cH(c, i).start()
            cH(c, i).wait()
            t = add(t, recv_h[c, i])
        fin[c, quarter, xc] = t
        cA2(c).start()

    def stage_a1(c):
        cA2(c).wait_recv()
        cA1(c).start()

    def stage_b(c):
        cA1(c).wait_recv()
        cB(c).start()

    def stage_o(c):
        cB(c).wait_recv()
        cO(c).start()

    stages = [stage_y, stage_x, stage_z1, stage_z2, stage_a2, stage_a1, stage_b, stage_o]

    def step(t):
        for i, stage in enumerate(stages):
            c = t - i
            if isinstance(c, int):
                if 0 <= c < count:
                    stage(c)
            else:
                pl.when((c >= 0) & (c < count))(functools.partial(stage, c))

    slot = [0]

    def pump(k=1):
        for _ in range(k):
            step(slot[0])
            slot[0] += 1

    def produce(c, block):
        @pl.when(c >= 2)
        def _():
            cC(c - 2).wait_send()

        for k in range(4):
            g[c % 2, k % 2, k // 2] = block(k).astype(BF)
        cC(c).start()

    def produced(c):
        pl.when(c >= 0)(functools.partial(absorb, c))

    left = lax.broadcasted_iota(jnp.int32, (128, 128), 1) < 64
    lanes = lax.broadcasted_iota(jnp.int32, (128, 128), 1)
    parts = []
    for l in (1, 0):
        parts += [(l, 6144), (l, 7680), (l, 3072), (l, 4608), (l, 1536), (l, 0)]

    def fetch(i):
        if i < len(parts):
            l, first = parts[i]
            return pltpu.make_async_copy(i_w.at[l, pl.ds(first, 1536)], wbuf.at[i % 2], wsem.at[i % 2])
        return None

    def fetch_start(i):
        if i < len(parts):
            fetch(i).start()

    mlp_loads = lambda l: [
        pltpu.make_async_copy(src.at[l], dst, lsem.at[i]) for i, (src, dst) in enumerate(((i_nm, nm), (i_mid, mid)))
    ]
    att_loads = lambda l: [
        pltpu.make_async_copy(src.at[l], dst, lsem.at[i + 2])
        for i, (src, dst) in enumerate(
            ((i_att, att), (i_rz, rz), (i_qkv, qkv), (i_phi, phi), (i_got, got), (i_na, na), (i_h, h), (i_lo, qlo), (i_attl, attl))
        )
    ]
    act_load = lambda l, k: pltpu.make_async_copy(i_act.at[l, k], actb.at[k % 2], asem.at[0, k % 2])
    dg_load = lambda l, k: pltpu.make_async_copy(i_dg.at[l, k], dgb.at[k % 2], asem.at[1, k % 2])

    def start(copies):
        for copy in copies:
            copy.start()

    def wait(copies):
        for copy in copies:
            copy.wait()

    def transposed(src):
        for t in range(6):
            flip[t * 128 : (t + 1) * 128] = src(t).T.astype(BF)

    fetch_start(0)
    fetch_start(1)
    for k in range(2):
        act_load(1, k).start()
        dg_load(1, k).start()
    start(mlp_loads(1))
    start(att_loads(1))
    gh[...] = cot[...].astype(F32)
    for l in (1, 0):
        c0 = (1 - l) * 12
        w0 = (1 - l) * 6
        transposed(lambda t: gh[:, t * 128 : (t + 1) * 128])
        for k in range(4):
            if k % 2 == 0:
                fetch(w0 + k // 2).wait()
            act_load(l, k).wait()
            dg_load(l, k).wait()
            low = gh[...].astype(BF)
            for t in range(3):
                at = slice(t * 256, (t + 1) * 256)
                du[k, :, at] = (nn(low, wbuf[(k // 2) % 2, (k % 2) * 768 : (k % 2 + 1) * 768, at]) * dgb[k % 2, :, at].astype(F32)).astype(BF)
            produce(c0 + k, lambda q, k=k: nn(flip[q * 192 : (q + 1) * 192], actb[k % 2]))
            produced(c0 + k - 1)
            if k < 2:
                act_load(l, k + 2).start()
                dg_load(l, k + 2).start()
            if k % 2 == 1:
                fetch_start(w0 + 2 + k // 2)
            if k == 2 or (k > 0 and l == 0):
                pump()
        wait(mlp_loads(l))
        for k in range(4):
            if k % 2 == 0:
                fetch(w0 + 2 + k // 2).wait()
            for t in range(3):
                at = slice(t * 256, (t + 1) * 256)
                term = nt(du[k], wbuf[(k // 2) % 2, (k % 2) * 768 + t * 256 : (k % 2) * 768 + (t + 1) * 256])
                if k == 0:
                    dn[:, at] = term
                else:
                    dn[:, at] += term
            if k % 2 == 1:
                fetch_start(w0 + 4 + k // 2)
        transposed(lambda t: nm[:, t * 128 : (t + 1) * 128].astype(F32))

        def up_chunk(j, carry):
            produce(c0 + 4 + j, lambda q: nn(flip[span(j, 192)], du[q]))
            produced(c0 + 3 + j)
            return carry

        lax.fori_loop(0, 2, up_chunk, 0)
        pump()
        lax.fori_loop(2, 4, up_chunk, 0)
        pump()
        grad, gg, gb = norm_back(dn[...], mid[...], norms[l, 1, 0:1])
        gnorm[l * 4 + 2 : l * 4 + 3] = gg
        gnorm[l * 4 + 3 : l * 4 + 4] = gb
        gh[...] += grad
        if l == 1:
            start(mlp_loads(0))
            for k in range(2):
                act_load(0, k).start()
                dg_load(0, k).start()
        wait(att_loads(l))
        transposed(lambda t: gh[:, t * 128 : (t + 1) * 128])
        produce(c0 + 8, lambda q: nn(flip[q * 192 : (q + 1) * 192], attl[...]))
        produced(c0 + 7)
        fetch(w0 + 4).wait()
        low = gh[...].astype(BF)
        for t in range(3):
            at = slice(t * 256, (t + 1) * 256)
            gatt[:, at] = nn(low, wbuf[0, 768:1536, at]) * rz[:, at]
        norm_sum[...] = jnp.zeros_like(norm_sum)

        def attention(hp, carry):
            at = span(hp, 128)
            deltas = []
            for r in range(2):
                rr = slice(r * 128, (r + 1) * 128)
                gp = gatt[rr, at]
                gpb = gp.astype(BF)
                gpt = gp.T.astype(BF)
                gp = gpb.astype(F32)
                ga = gp * att[rr, at]
                v = qkv[rr, pl.ds(pl.multiple_of(1536 + hp * 128, 128), 128)]
                states, pair = [], []
                for k in range(2):
                    keep = left if k == 0 else jnp.logical_not(left)
                    ghalf = jnp.where(keep, gp, 0.0).astype(BF)
                    c = jnp.sum(jnp.where(keep, ga, 0.0), axis=1, keepdims=True)
                    c_high = c.astype(BF).astype(F32)
                    csel = jnp.where(lanes == hp * 2 + k, -c_high, jnp.where(lanes == hp * 2 + k + 64, c_high - c, 0.0)).astype(BF)
                    fat = pl.ds(pl.multiple_of(hp * 256 + k * 128, 128), 128)
                    phq, phk = phi[0, fat, rr], phi[1, fat, rr]
                    da, da_low = parts_of((nt(ghalf, v) - c) * mask[r])
                    a = (nn(phq.astype(F32).T.astype(BF), phk) * mask[r]).astype(BF)
                    far = nt(
                        jnp.concatenate([got[r, at], got[r, 768:896]], axis=1), jnp.concatenate([ghalf, csel], axis=1)
                    )
                    gq = nt(phk, da) + nt(phk, da_low) + chain[r] * far
                    gphik[fat, rr] = nn(phq, da) + nn(phq, da_low)
                    gvt[pl.ds(pl.multiple_of(hp * 128 + k * 64, 64), 64), rr] = nn(gpt, a)[k * 64 : (k + 1) * 64]
                    here = nn((phq.astype(F32) * chain[r]).astype(BF), jnp.concatenate([gpb, csel], axis=1))
                    states.append(here[:, :128])
                    norm_sum[r] += here[:, 128:]
                    pair.append(softmax_back(phq, gq))
                state[r, at] = jnp.where(left, states[0], states[1]).astype(BF)
                deltas.append(jnp.concatenate(pair, axis=0))
            delta, delta_low = parts_of(jnp.concatenate(deltas, axis=1))
            dqkvt[at] = nn(maps[l, 0, hp], delta).astype(BF)
            gm[l, 0, hp] = nn(delta, qkv[:, at]) + nn(delta_low, qkv[:, at]) + nn(delta, qlo[:, at])
            return carry

        lax.fori_loop(0, 3, attention, 0)
        pump()
        lax.fori_loop(3, 6, attention, 0)
        for r in range(2):
            state[r, 768:896] = norm_sum[r].astype(BF)
        swap = Exchange(n, s, b, state, taken, sums, back, esem.at[l])
        swap.send()
        produced(c0 + 8)
        pump()
        swap.turn(coef)
        pump()
        swap.receive()

        def keys(hp, carry):
            at = span(hp, 128)
            deltas = []
            for r in range(2):
                rr = slice(r * 128, (r + 1) * 128)
                v = qkv[rr, pl.ds(pl.multiple_of(1536 + hp * 128, 128), 128)].astype(F32)
                turned = back[r, at].astype(F32).T.astype(BF)
                both = jnp.concatenate([back[r, at], back[r, 768:896]], axis=1)
                pair = []
                for k in range(2):
                    keep = left if k == 0 else jnp.logical_not(left)
                    vhalf = jnp.where(keep, v, 0.0).astype(BF)
                    pick = (lanes % 64 == hp * 2 + k).astype(BF)
                    fat = pl.ds(pl.multiple_of(hp * 256 + k * 128, 128), 128)
                    phk = phi[1, fat, rr]
                    gk = gphik[fat, rr] + last[r] * nt(both, jnp.concatenate([vhalf, pick], axis=1))
                    more = last[r] * nn(turned, phk)[k * 64 : (k + 1) * 64]
                    hat = pl.multiple_of(hp * 128 + k * 64, 64)
                    dqkvt[pl.ds(1536 + hat, 64), rr] = (gvt[pl.ds(hat, 64), rr] + more).astype(BF)
                    pair.append(softmax_back(phk, gk))
                deltas.append(jnp.concatenate(pair, axis=0))
            delta, delta_low = parts_of(jnp.concatenate(deltas, axis=1))
            key_at = pl.ds(pl.multiple_of(768 + hp * 128, 128), 128)
            dqkvt[key_at] = nn(maps[l, 1, hp], delta).astype(BF)
            gm[l, 1, hp] = nn(delta, qkv[:, key_at]) + nn(delta_low, qkv[:, key_at]) + nn(delta, qlo[:, key_at])
            return carry

        lax.fori_loop(0, 6, keys, 0)
        swap.finish()
        pump()

        def in_chunk(j, carry):
            produce(c0 + 9 + j, lambda q: nn(dqkvt[pl.ds(pl.multiple_of(q * 576 + j * 192, 64), 192)], na[...]))

            @pl.when(j > 0)
            def _():
                absorb(c0 + 8 + j)

            return carry

        lax.fori_loop(0, 3, in_chunk, 0)
        fetch(w0 + 5).wait()
        for t in range(9):
            piece = jnp.concatenate(
                [dqkvt[t * 256 : t * 256 + 128].astype(F32).T, dqkvt[t * 256 + 128 : t * 256 + 256].astype(F32).T], axis=1
            ).astype(BF)
            place = wbuf[1, t * 256 : (t + 1) * 256] if t < 6 else wbuf[0, (t - 6) * 256 : (t - 5) * 256]
            term = nn(piece, place)
            if t == 0:
                dn[...] = term
            else:
                dn[...] += term
        fetch_start(w0 + 6)
        fetch_start(w0 + 7)
        grad, gg, gb = norm_back(dn[...], h[...], norms[l, 0, 0:1])
        gnorm[l * 4 : l * 4 + 1] = gg
        gnorm[l * 4 + 1 : l * 4 + 2] = gb
        gh[...] += grad
        if l == 1:
            start(att_loads(0))
        pump()
    o_tok[...] = gh[...].astype(BF)
    c = count - 1
    cC(c - 2).wait_send()
    for k in range(4):
        into = g.at[c % 2, k % 2, k // 2]
        into[...] = jnp.zeros((CHUNK, D), BF)
        into[128:144] = jnp.concatenate([gnorm[...], jnp.zeros((8, D), F32)], axis=0).astype(BF)
        for l in range(2):
            for which in range(2):
                tiles = [None, None]
                for head in range(3 * k, 3 * k + 3):
                    side = head % 2
                    block = gm[l, which, head // 2][side * 64 : (side + 1) * 64]
                    block = jnp.where(left[:64] if side == 0 else jnp.logical_not(left[:64]), block, 0.0)
                    tile = (head % 3) // 2
                    tiles[tile] = block if tiles[tile] is None else tiles[tile] + block
                for tile in range(2):
                    first = (which * 2 + tile) * 128
                    into[l * 64 : (l + 1) * 64, first : first + 128] = tiles[tile].astype(BF)
    cC(c).start()
    absorb(c - 1)
    absorb(c)

    def tail(t, carry):
        step(t)
        return carry

    lax.fori_loop(slot[0], count + len(stages) - 1, tail, 0)
    cC(count - 2).wait_send()
    cC(count - 1).wait_send()

    def drain(c, carry):
        for copy in (cY, cZ1, cZ2, cA2, cA1, cB):
            copy(c).wait_send()
        cO(c).wait()
        return carry

    lax.fori_loop(0, count, drain, 0)


def backward(n, cot, norms, maps, mask, chain, last, coef, saved):
    group, _ = owners(n)
    m = cot.shape[0]
    count = 25
    extra = len([v for v in range(2, 10) if (1 << v) < n // 2])
    vmem = pl.BlockSpec(memory_space=pltpu.VMEM)
    anywhere = pl.BlockSpec(memory_space=pl.ANY)
    pair = lambda: pltpu.SemaphoreType.DMA((2, count))
    V = lambda kind, *shape: pltpu.VMEM(shape, kind)
    return pl.pallas_call(
        functools.partial(backward_kernel, n, count),
        name="backward",
        out_shape=(jax.ShapeDtypeStruct((count, CHUNK, D), BF), jax.ShapeDtypeStruct((m, D), BF)),
        in_specs=[vmem] * 6 + [pl.BlockSpec(memory_space=pltpu.SMEM)] + [anywhere] * 14,
        out_specs=[anywhere, vmem],
        scratch_shapes=[
            V(BF, count, 2, CHUNK, D), V(BF, count, CHUNK, D), V(BF, count, CHUNK, 384), V(BF, count, CHUNK // 2, 384),
            V(BF, count, CHUNK // 4, 384), V(BF, count if extra else 1, extra + 1, CHUNK // 4, 384), V(BF, 2, 2, 2, CHUNK, D),
            V(BF, 2, 1536, D), V(BF, 2, m, D), V(BF, 2, m, D), V(BF, m, D), V(F32, m, D), V(F32, m, D), V(F32, m, D),
            V(BF, m, 2304), V(BF, 2, 1536, m), V(BF, 2, STATE_ROWS, 128), V(BF, m, D), V(F32, m, D), V(BF, m, 1536), V(BF, m, D),
            V(F32, m, D), V(BF, 4, m, D), V(F32, m, D), V(F32, 1536, m), V(F32, D, m), V(BF, 2304, m), V(BF, D, m), V(F32, m, D),
            V(F32, 2, 2, 6, 128, 128), V(F32, 8, D), V(F32, 2, 128, 128), V(BF, 2, STATE_ROWS, 128),
            V(BF, n, 2, group, 128), V(BF, n, 2, group, 128), V(BF, 2, STATE_ROWS, 128),
            pair(), pair(), pair(), pair(), pair(), pltpu.SemaphoreType.DMA((2, count, max(extra, 1))), pair(), pair(), pair(),
            pltpu.SemaphoreType.DMA((count,)), pltpu.SemaphoreType.DMA((2, 4)), pltpu.SemaphoreType.DMA((2,)),
            pltpu.SemaphoreType.DMA((2, 2)), pltpu.SemaphoreType.DMA((11,)),
        ],
        compiler_params=pltpu.CompilerParams(collective_id=1, has_side_effects=True, vmem_limit_bytes=63 * 2**20),
    )(cot, norms, maps, mask, chain, last, coef, *saved)


def prologue(lengths, attn_in, attn_out, mlp_in, mlp_out, norm_gains, norm_biases, feature_maps, tok_rows):
    layers = attn_in.shape[0]
    n = lax.axis_size("seq")
    me = lax.axis_index("seq")
    first = me * tok_rows
    starts = jnp.cumsum(lengths, axis=1) - lengths
    seg = lambda p: jnp.sum((starts[:, None, :] <= p[None, :, None]).astype(jnp.int32), axis=2) - 1
    ids = seg(first + jnp.arange(tok_rows, dtype=jnp.int32))
    firsts = jnp.arange(n, dtype=jnp.int32) * tok_rows
    before, final = seg(firsts - 1), seg(firsts + tok_rows - 1)
    prior = seg((first - 1)[None])
    chain = jnp.broadcast_to((ids == prior).astype(F32)[:, :, None], ids.shape + (128,))
    last = (ids == ids[:, -1:]).astype(F32)[:, None, :]
    lower = jnp.tril(jnp.ones((tok_rows, tok_rows), F32))
    mask = (ids[:, :, None] == ids[:, None, :]).astype(F32) * lower[None]
    order = jnp.arange(n)
    coef = ((final[:, None, :] == before[:, :, None]) & (order[None, :] < order[:, None])[None]).astype(F32)
    coef_back = jnp.swapaxes(coef, 1, 2)
    packed = jnp.concatenate(
        [
            jnp.swapaxes(attn_in, 1, 2),
            jnp.swapaxes(attn_out, 1, 2),
            mlp_in,
            jnp.transpose(mlp_out.reshape(layers, 4, 768, 192), (0, 1, 3, 2)).reshape(layers, 768, 768),
        ],
        axis=1,
    )
    small = jnp.concatenate([norm_gains[:, :, None], norm_biases[:, :, None], feature_maps], axis=2)
    small = jnp.pad(small.reshape(layers * 132, 192), ((0, (-layers * 132) % 16), (0, 64)))
    smalls = gather_small(small)[:, : layers * 132, :192].reshape(4, layers, 2, 66, 192)
    smalls = jnp.transpose(smalls, (1, 2, 3, 0, 4)).reshape(layers, 2, 66, 768)
    norms = smalls[:, :, :2].astype(F32)
    maps = jnp.transpose(smalls[:, :, 2:].reshape(layers, 2, 64, 6, 2, 64), (0, 1, 3, 4, 5, 2))
    maps = (maps[:, :, :, :, :, None, :] * jnp.eye(2, dtype=BF)[:, None, :, None]).reshape(layers, 2, 6, 128, 128)
    chain_row = (ids == prior).astype(F32)[:, None, :]
    return packed, norms, maps, jnp.swapaxes(maps, 3, 4), mask, chain, chain_row, last, coef.reshape(-1), coef_back.reshape(-1)


def shards(tokens, cotangent, lengths, attn_in, attn_out, mlp_in, mlp_out, norm_gains, norm_biases, feature_maps):
    tok_rows = tokens.shape[1]
    layers = attn_in.shape[0]
    n = lax.axis_size("seq")
    packed, norms, maps, maps_back, mask, chain, chain_row, last, coef, coef_back = prologue(
        lengths, attn_in, attn_out, mlp_in, mlp_out, norm_gains, norm_biases, feature_maps, tok_rows
    )
    *saved, block_output = forward(n, tokens.reshape(-1, D), packed, norms, maps, mask, chain, last, coef)
    total, grad_tokens = backward(
        n, cotangent.reshape(-1, D), norms, maps_back, mask, chain_row, last, coef_back, saved
    )
    big = total[:-1].reshape(layers, 12, CHUNK, D)[::-1]
    turn = lambda v: jnp.swapaxes(v, -1, -2).astype(F32)
    grad_in = turn(big[:, 9:].reshape(layers, 576, D))
    grad_out = turn(big[:, 8])
    grad_up = big[:, 4:8].reshape(layers, D, D).astype(F32)
    grad_down = turn(big[:, :4]).reshape(layers, 3072, 192)
    b = lax.axis_index("batch")
    norm_rows = lax.dynamic_slice(total[-1, 128:136], (0, b * 192), (8, 192)).astype(F32).reshape(layers, 2, 2, 192)
    tiles = total[-1, :128, :512].astype(F32).reshape(layers, 64, 2, 2, 2, 64)
    even = b % 2 == 0
    first = jnp.where(even, tiles[:, :, :, 0, 0], tiles[:, :, :, 0, 1])
    second = jnp.where(even, tiles[:, :, :, 0, 1], tiles[:, :, :, 0, 0])
    third = jnp.where(even, tiles[:, :, :, 1, 0], tiles[:, :, :, 1, 1])
    grad_maps = jnp.stack([first, second, third], axis=3)
    grad_maps = jnp.transpose(grad_maps, (0, 2, 4, 3, 1)).reshape(layers, 2, 64, 192)
    return (
        block_output.reshape(tokens.shape),
        grad_tokens.reshape(tokens.shape),
        grad_in,
        grad_out,
        grad_up,
        grad_down,
        norm_rows[:, :, 0],
        norm_rows[:, :, 1],
        grad_maps,
        norm_rows[:, 1, 1],
    )


def solution(mesh):
    in_specs = (
        P("batch", "seq", None),
        P("batch", "seq", None),
        P("batch", None),
        P(None, None, "batch"),
        P(None, None, "batch"),
        P(None, None, "batch"),
        P(None, None, "batch"),
        P(None, None, "batch"),
        P(None, None, "batch"),
        P(None, None, None, "batch"),
    )
    out_specs = (
        P("batch", "seq", None),
        P("batch", "seq", None),
        P(None, None, "batch"),
        P(None, None, "batch"),
        P(None, None, "batch"),
        P(None, None, "batch"),
        P(None, None, "batch"),
        P(None, None, "batch"),
        P(None, None, None, "batch"),
        P(None, "batch"),
    )
    return jax.shard_map(shards, mesh=mesh, in_specs=in_specs, out_specs=out_specs, check_vma=False)
```

time: 963 us -> 469 us (0.49)
  local copies, waits for them, and re-layouts: 206 us -> 42.1 us
  matrix products: 143 us -> 0 us
  waiting for transfers between devices: 103 us -> 0 us
  other arithmetic: 61.1 us -> 18.3 us
  Pallas kernels: 421 us -> 403 us
  between operations: 17.7 us -> 1.16 us
    dot_general x68 -> x0, matrix products: 143 us -> none  [the longest x6 14.5 us: read_out(): jnp.einsum('mhij,mjhd->mihd', scores, value_part, precision=HIGH)]
    all_gather x4 -> x0, waiting for transfers between devices: 103 us -> none  [exchange(): lax.all_gather(both.reshape(micro_count, H * 2 * HD * (HD + 1)), 'seq')]
    slice x31 -> x13, local copies, waits for them, and re-layouts: 75.5 us -> 20.8 us  [the longest x1 6.61 us: shards(): big = total[:-1].reshape(layers, 12, CHUNK, D)[::-1]]
    unnamed x559 -> x18, local copies, waits for them, and re-layouts: 51 us -> 6.24 us
    sub x11 -> x5, other arithmetic: 21.3 us -> 0.03 us  [the longest x3 0.02 us: prologue(): jnp.sum((starts[:, None, :] <= p[None, :, None]).astype(jnp.int32), axis=2)]
    pallas_call x2 -> x3, Pallas kernels: 421 us -> 403 us  [the longest x1 242 us: backward(): pl.pallas_call(functools.partial(backward_kernel, n, count), name='backwa...]
    reshape x10 -> x5, local copies, waits for them, and re-layouts: 21.8 us -> 5.93 us  [the longest x1 2.86 us: shards(): grad_down = turn(big[:, :4]).reshape(layers, 3072, 192)]
    convert_element_type x7 -> x4, local copies, waits for them, and re-layouts: 17.2 us -> 1.59 us  [the longest x2 1.2 us: prologue(): ((final[:, None, :] == before[:, :, None]) & (order[None, :] < order[:, N...]
  transfers between devices with their start and end apart: 4 -> 0, of which waited for: 4 -> 0; matrix products, arithmetic and copies ran while one was open for 13% -> 0% of each run, Pallas kernels for 0% -> 0%
where the time goes in v2:
time: 469 us; the launch traced here: 465 us
  Pallas kernels  403 us (86%)
  local copies, waits for them, and re-layouts  42.1 us (9%)
  other arithmetic  18.3 us (4%)
    pallas_call x1, Pallas kernels, backward(): pl.pallas_call(functools.partial(backward_kernel, n, count), name='backwa...  242 us
    pallas_call x1, Pallas kernels, forward(): pl.pallas_call(functools.partial(forward_kernel, n), name='forward', out_...  150 us
    pallas_call x1, Pallas kernels, gather_small(): pl.pallas_call(small_kernel, name='gather_small', out_shape=jax.ShapeDtyp...  11.2 us

profile of v2, /device:TPU:0, one launch (start us, length us, event | category | flops | bytes accessed | tf_op | source)
XLA Modules:
  0.0 465.0 jit_solution(10178436704843334409)
XLA Ops:
  0.7 0.9 reduce_window_sum.11
  1.6 0.8 fusion.5
  2.4 0.1 copy.60
  2.4 0.1 fusion.2
  2.5 0.1 fusion.3
  2.6 0.1 compare_convert_fusion.5
  2.7 0.2 slice_reduce_fusion
  2.9 0.6 compare_convert_fusion.3
  3.5 0.7 copy.54
  4.2 0.7 copy.55
  4.9 0.1 and_convert_fusion
  5.0 0.6 reshape.318.coef
  5.6 0.6 reshape.317.coef
  6.2 0.1 mul.48
  6.3 0.1 mul.49
  6.4 0.8 compare_select_fusion.mask
  7.2 0.8 broadcast_in_dim.16.chain
  7.9 1.0 pad_maximum_fusion.2
  8.9 0.1 reshape.306
  8.9 0.7 pad.4.s_ref
  9.6 11.2 %gather_small.1 = bf16[4,272,256]{2,1,0:T(8,128)(2,1)} custom-call(bf16[272,256]{1,0:T(8,128)(2,1)} %pad.4.s_ref), custom_call_target="tpu_custom_call" | custom-call | tf_op jit(solution)/shard_map/gather_small/pallas_call | solution.py:57
  20.9 1.1 slice.70
  21.9 0.2 copy.56
  22.2 0.6 reshape.327
  22.7 0.6 slice_convert_fusion.1.norms
  23.4 0.1 slice.94
  23.5 0.4 copy.76
  23.9 0.5 reshape.309
  24.4 0.8 copy.59
  25.1 1.5 mul.46
  26.7 0.9 mul.47
  27.6 0.9 fusion.11.maps
  28.5 0.1 broadcast_multiply_fusion
  28.6 0.0 copy-start.1
  28.6 0.0 copy-start.2
  28.6 1.2 copy.62.maps
  29.8 2.0 copy.99
  31.8 0.6 copy-done
  32.3 3.5 pad_maximum_fusion.w_ref
  35.8 150.3 %forward.1 = (bf16[2,9216,768]{2,1,0:T(8,128)(2,1)}, f32[2,256,768]{2,1,0:T(8,128)}, f32[2,256,768]{2,1,0:T(8,128)}, bf16[2,256,768]{2,1,0:T(8,128)(2,1)}, bf16[...) custom-call(bf16[256,768]{1,0:T(8,128)(2,1)} %bitcast.84, ...), custom_call_target="tpu_custom_call" | custom-call | tf_op jit(solution)/shard_map/forward/pallas_call | solution.py:444
  186.2 241.9 %backward.1 = (bf16[25,192,768]{2,1,0:T(8,128)(2,1)}, bf16[256,768]{1,0:T(8,128)(2,1)}) custom-call(bf16[256,768]{1,0:T(8,128)(2,1)} %bitcast.81, f32[2,2,2,768]{3,2,1,0:T(2,128)} %slice_convert_fusion.1.norms, bf16[2,2,6,128,128]{4,3,2,1,0:T(8,128)(2,1)} %fusion.11.maps, f32[2,128,128]{2,1,0:T(8,128)} %compare_select_fusion.mask, ...), custom_call_target="tpu_custom_call" | custom-call | tf_op jit(solution)/shard_map/backward/pallas_call | solution.py:875
  428.1 0.7 slice.84
  428.8 0.1 dynamic-slice_convert_fusion
  428.9 0.6 copy.102
  429.5 0.6 copy.100
  430.1 0.6 copy.101
  430.7 0.9 slice_convert_fusion
  431.6 6.6 %slice.75 = bf16[24,192,768]{2,1,0:T(8,128)(2,1)} slice(bf16[25,192,768]{2,1,0:T(8,128)(2,1)} %get-tuple-element.43), slice={[0:24], [0:192], [0:768]} | slice | bytes 14155776 | tf_op jit(solution)/shard_map/slice | solution.py:946
  438.2 0.4 reshape.323
  438.6 0.4 fusion.9
  439.1 0.9 copy.74
  440.0 1.1 slice_bitcast_fusion
  441.1 1.1 convert_bitcast_fusion.2
  442.2 2.8 slice.95
  445.0 4.1 fusion.8
  449.1 2.8 slice.77
  451.9 3.5 convert_bitcast_fusion.1
  455.4 0.4 convert_bitcast_fusion
  455.9 2.9 copy.86
  458.7 1.8 slice.81
  460.6 2.7 bitcast_convert_fusion
  463.3 0.7 copy.105
  464.0 0.0 copy-done.4
  464.0 0.7 copy.106
  (21 shorter events, 0.2 us)
Async XLA Ops:
  28.6 3.2 copy-start.1
  28.6 3.2 copy-start.2
  29.8 2.6 copy-start
  460.5 2.7 copy-start.3
  460.6 3.5 copy-start.4

commit v3 on v2

--- a/solution.py
+++ b/solution.py
@@ -327,7 +327,10 @@
                 state[l, r, span(hp, 128)] = jnp.where(left, got_[0], got_[1]).astype(BF)
             return carry
 
-        lax.fori_loop(0, 6, features, 0)
+        for k in range(3):
+            lax.fori_loop(2 * k, 2 * k + 2, features, 0)
+            if k < 2:
+                pump()
         for r in range(2):
             state[l, r, 768:896] = norm_sum[r].astype(BF)
         swap = Exchange(n, s, b, state.at[l], taken.at[l], sums.at[l], got.at[l], esem.at[l])
@@ -355,9 +358,10 @@
             return carry
 
         lax.fori_loop(0, 3, scores, 0)
+        pump()
         swap.turn(coef)
         lax.fori_loop(3, 6, scores, 0)
-        pump()
+        pump(2)
         swap.receive()
 
         def finish(hp, carry):
@@ -478,6 +482,10 @@
 
 
 CHUNK = 192
+PLAN = {
+    1: [0, 0, 0, 0, 0, 1, 0, 1, 2, 2, 0, 1, 0, 1],
+    0: [0, 0, 0, 1, 0, 1, 0, 1, 3, 2, 0, 1, 0, 1],
+}
 
 
 def backward_kernel(
@@ -521,10 +529,9 @@
 
     def absorb(c):
         cC(c).wait_recv()
-        recv_c[c] = add(recv_c[c], g[c % 2, par])
-
-    def stage_y(c):
+        recv_c[c, 1 - yy] = add(recv_c[c, 1 - yy], g[c % 2, par, 1 - yy])
         cY(c).start()
+        recv_c[c, yy] = add(recv_c[c, yy], g[c % 2, par, yy])
 
     def stage_x(c):
         cY(c).wait_recv()
@@ -533,7 +540,7 @@
         recv_y[c, :, xc] = add(recv_y[c, :, xc], recv_c[c, yy, :, xc])
 
     def stage_z1(c):
-        cX(c).wait_recv()
+        cX(c).wait()
         recv_x[c] = add(recv_x[c], recv_y[c, :, xc])
         cZ1(c).start()
 
@@ -544,7 +551,6 @@
 
     def stage_a2(c):
         cZ2(c).wait_recv()
-        cX(c).wait_send()
         t = add(recv_2[c], recv_1[c, span(b1, quarter_rows)])
         for i in range(len(levels)):
             recv_h[c, len(levels)] = t
@@ -566,7 +572,7 @@
         cB(c).wait_recv()
         cO(c).start()
 
-    stages = [stage_y, stage_x, stage_z1, stage_z2, stage_a2, stage_a1, stage_b, stage_o]
+    stages = [stage_x, stage_z1, stage_z2, stage_a2, stage_a1, stage_b, stage_o]
 
     def step(t):
         for i, stage in enumerate(stages):
@@ -647,6 +653,7 @@
     for l in (1, 0):
         c0 = (1 - l) * 12
         w0 = (1 - l) * 6
+        plan = PLAN[l]
         transposed(lambda t: gh[:, t * 128 : (t + 1) * 128])
         for k in range(4):
             if k % 2 == 0:
@@ -664,8 +671,7 @@
                 dg_load(l, k + 2).start()
             if k % 2 == 1:
                 fetch_start(w0 + 2 + k // 2)
-            if k == 2 or (k > 0 and l == 0):
-                pump()
+            pump(plan[k])
         wait(mlp_loads(l))
         for k in range(4):
             if k % 2 == 0:
@@ -686,10 +692,9 @@
             produced(c0 + 3 + j)
             return carry
 
-        lax.fori_loop(0, 2, up_chunk, 0)
-        pump()
-        lax.fori_loop(2, 4, up_chunk, 0)
-        pump()
+        pump(plan[4])
+        lax.fori_loop(0, 4, up_chunk, 0)
+        pump(plan[5])
         grad, gg, gb = norm_back(dn[...], mid[...], norms[l, 1, 0:1])
         gnorm[l * 4 + 2 : l * 4 + 3] = gg
         gnorm[l * 4 + 3 : l * 4 + 4] = gb
@@ -749,17 +754,18 @@
             gm[l, 0, hp] = nn(delta, qkv[:, at]) + nn(delta_low, qkv[:, at]) + nn(delta, qlo[:, at])
             return carry
 
-        lax.fori_loop(0, 3, attention, 0)
-        pump()
-        lax.fori_loop(3, 6, attention, 0)
+        for k in range(3):
+            lax.fori_loop(2 * k, 2 * k + 2, attention, 0)
+            if k < 2:
+                pump(plan[6 + k])
         for r in range(2):
             state[r, 768:896] = norm_sum[r].astype(BF)
         swap = Exchange(n, s, b, state, taken, sums, back, esem.at[l])
         swap.send()
         produced(c0 + 8)
-        pump()
+        pump(plan[8])
         swap.turn(coef)
-        pump()
+        pump(plan[9])
         swap.receive()
 
         def keys(hp, carry):
@@ -789,9 +795,11 @@
             gm[l, 1, hp] = nn(delta, qkv[:, key_at]) + nn(delta_low, qkv[:, key_at]) + nn(delta, qlo[:, key_at])
             return carry
 
-        lax.fori_loop(0, 6, keys, 0)
+        for k in range(3):
+            lax.fori_loop(2 * k, 2 * k + 2, keys, 0)
+            if k < 2:
+                pump(plan[10 + k])
         swap.finish()
-        pump()
 
         def in_chunk(j, carry):
             produce(c0 + 9 + j, lambda q: nn(dqkvt[pl.ds(pl.multiple_of(q * 576 + j * 192, 64), 192)], na[...]))
@@ -803,6 +811,7 @@
             return carry
 
         lax.fori_loop(0, 3, in_chunk, 0)
+        pump(plan[12])
         fetch(w0 + 5).wait()
         for t in range(9):
             piece = jnp.concatenate(
@@ -822,7 +831,8 @@
         gh[...] += grad
         if l == 1:
             start(att_loads(0))
-        pump()
+        pump(plan[13])
+        assert slot[0] <= c0 + 11
     o_tok[...] = gh[...].astype(BF)
     c = count - 1
     cC(c - 2).wait_send()
@@ -892,6 +902,40 @@
         ],
         compiler_params=pltpu.CompilerParams(collective_id=1, has_side_effects=True, vmem_limit_bytes=63 * 2**20),
     )(cot, norms, maps, mask, chain, last, coef, *saved)
+
+
+def finish_kernel(x_ref, down, up, out, inner):
+    j = pl.program_id(1)
+
+    @pl.when(j == 0)
+    def _():
+        for k in range(4):
+            down[0, :, k * D : (k + 1) * D] = x_ref[k].astype(F32)
+
+    @pl.when(j == 1)
+    def _():
+        for k in range(4):
+            up[0, k * CHUNK : (k + 1) * CHUNK] = x_ref[k].astype(F32)
+
+    @pl.when(j == 2)
+    def _():
+        out[0] = x_ref[0].astype(F32)
+        for k in range(3):
+            inner[0, k * CHUNK : (k + 1) * CHUNK] = x_ref[k + 1].astype(F32)
+
+
+def finish(total, layers):
+    shape = lambda *dims: jax.ShapeDtypeStruct((layers,) + dims, F32)
+    whole = lambda *dims: pl.BlockSpec((1,) + dims, lambda l, j: (l, 0, 0))
+    return pl.pallas_call(
+        finish_kernel,
+        name="finish",
+        grid=(layers, 3),
+        out_shape=(shape(CHUNK, 3072), shape(D, D), shape(CHUNK, D), shape(3 * CHUNK, D)),
+        in_specs=[pl.BlockSpec((4, CHUNK, D), lambda l, j: ((layers - 1 - l) * 3 + j, 0, 0))],
+        out_specs=[whole(CHUNK, 3072), whole(D, D), whole(CHUNK, D), whole(3 * CHUNK, D)],
+        compiler_params=pltpu.CompilerParams(vmem_limit_bytes=40 * 2**20),
+    )(total)
 
 
 def prologue(lengths, attn_in, attn_out, mlp_in, mlp_out, norm_gains, norm_biases, feature_maps, tok_rows):
@@ -943,12 +987,8 @@
     total, grad_tokens = backward(
         n, cotangent.reshape(-1, D), norms, maps_back, mask, chain_row, last, coef_back, saved
     )
-    big = total[:-1].reshape(layers, 12, CHUNK, D)[::-1]
-    turn = lambda v: jnp.swapaxes(v, -1, -2).astype(F32)
-    grad_in = turn(big[:, 9:].reshape(layers, 576, D))
-    grad_out = turn(big[:, 8])
-    grad_up = big[:, 4:8].reshape(layers, D, D).astype(F32)
-    grad_down = turn(big[:, :4]).reshape(layers, 3072, 192)
+    grad_down, grad_up, grad_out, grad_in = finish(total, layers)
+    grad_down, grad_out, grad_in = (jnp.swapaxes(v, 1, 2) for v in (grad_down, grad_out, grad_in))
     b = lax.axis_index("batch")
     norm_rows = lax.dynamic_slice(total[-1, 128:136], (0, b * 192), (8, 192)).astype(F32).reshape(layers, 2, 2, 192)
     tiles = total[-1, :128, :512].astype(F32).reshape(layers, 64, 2, 2, 2, 64)

time: 469 us -> 422 us (0.90)
  Pallas kernels: 403 us -> 383 us
  local copies, waits for them, and re-layouts: 42.1 us -> 23 us
  other arithmetic: 18.3 us -> 10.6 us
    slice x5 -> x0, local copies, waits for them, and re-layouts: 18.2 us -> none  [the longest x1 6.61 us: shards(): big = total[:-1].reshape(layers, 12, CHUNK, D)[::-1]]
    pallas_call x1, Pallas kernels: 150 us -> 132 us  [forward(): pl.pallas_call(functools.partial(forward_kernel, n), name='forward', out_...]
    pallas_call x1, Pallas kernels: 242 us -> 232 us  [backward(): pl.pallas_call(functools.partial(backward_kernel, n, count), name='backwa...]
    convert_element_type x3 -> x0, other arithmetic: 7.33 us -> none  [the longest x2 4.63 us: shards(): turn = lambda v: jnp.swapaxes(v, -1, -2).astype(F32)]
    pallas_call x0 -> x1, Pallas kernels: none -> 6.78 us  [finish(): pl.pallas_call(finish_kernel, name='finish', grid=(layers, 3), out_shape=...]
where the time goes in v3:
time: 422 us; the launch traced here: 417 us
  Pallas kernels  383 us (91%)
  local copies, waits for them, and re-layouts  23 us (5%)
  other arithmetic  10.6 us (3%)
    pallas_call x1, Pallas kernels, backward(): pl.pallas_call(functools.partial(backward_kernel, n, count), name='backwa...  232 us
    pallas_call x1, Pallas kernels, forward(): pl.pallas_call(functools.partial(forward_kernel, n), name='forward', out_...  132 us
    pallas_call x1, Pallas kernels, gather_small(): pl.pallas_call(small_kernel, name='gather_small', out_shape=jax.ShapeDtyp...  11.2 us

profile of v3, /device:TPU:0, one launch (start us, length us, event | category | flops | bytes accessed | tf_op | source)
XLA Modules:
  0.0 417.5 jit_solution(15823499727690146660)
XLA Ops:
  0.7 0.9 reduce_window_sum.11
  1.6 0.8 fusion.5
  2.4 0.1 copy.56
  2.4 0.1 fusion.2
  2.5 0.1 fusion.3
  2.6 0.1 compare_convert_fusion.5
  2.7 0.2 slice_reduce_fusion
  2.9 0.6 compare_convert_fusion.3
  3.5 0.7 copy.50
  4.2 0.7 copy.51
  4.9 0.1 and_convert_fusion
  5.0 0.6 reshape.298.coef
  5.6 0.6 reshape.297.coef
  6.2 0.1 mul.48
  6.3 0.1 mul.49
  6.4 0.8 compare_select_fusion.mask
  7.2 0.8 broadcast_in_dim.16.chain
  7.9 1.0 pad_maximum_fusion.2
  8.9 0.1 reshape.289
  8.9 0.7 pad.4.s_ref
  9.6 11.2 %gather_small.1 = bf16[4,272,256]{2,1,0:T(8,128)(2,1)} custom-call(bf16[272,256]{1,0:T(8,128)(2,1)} %pad.4.s_ref), custom_call_target="tpu_custom_call" | custom-call | tf_op jit(solution)/shard_map/gather_small/pallas_call | solution.py:57
  20.9 1.1 slice.43
  22.0 0.2 copy.52
  22.2 0.6 reshape.301
  22.8 0.6 slice_convert_fusion.1.norms
  23.4 0.1 slice.58
  23.5 0.4 copy.70
  23.9 0.5 reshape.292
  24.4 0.8 copy.55
  25.1 1.5 mul.46
  26.7 0.9 mul.47
  27.6 0.9 fusion.10.maps
  28.5 0.1 broadcast_multiply_fusion
  28.6 0.0 copy-start.2
  28.6 0.0 copy-start.3
  28.6 1.2 copy.58.maps
  29.8 0.0 copy-start.1
  29.8 2.0 copy.91
  31.7 0.0 copy-done.2
  31.8 0.0 copy-done.3
  31.8 0.6 copy-done.1
  32.3 3.6 pad_maximum_fusion.w_ref
  35.9 132.3 %forward.1 = (bf16[2,9216,768]{2,1,0:T(8,128)(2,1)}, f32[2,256,768]{2,1,0:T(8,128)}, f32[2,256,768]{2,1,0:T(8,128)}, bf16[2,256,768]{2,1,0:T(8,128)(2,1)}, bf16[...) custom-call(bf16[256,768]{1,0:T(8,128)(2,1)} %bitcast.63, ...), custom_call_target="tpu_custom_call" | custom-call | tf_op jit(solution)/shard_map/forward/pallas_call | solution.py:448
  168.3 232.4 %backward.1 = (bf16[25,192,768]{2,1,0:T(8,128)(2,1)}, bf16[256,768]{1,0:T(8,128)(2,1)}) custom-call(bf16[256,768]{1,0:T(8,128)(2,1)} %bitcast.60, f32[2,2,2,768]{3,2,1,0:T(2,128)} %slice_convert_fusion.1.norms, bf16[2,2,6,128,128]{4,3,2,1,0:T(8,128)(2,1)} %fusion.10.maps, f32[2,128,128]{2,1,0:T(8,128)} %compare_select_fusion.mask, ...), custom_call_target="tpu_custom_call" | custom-call | tf_op jit(solution)/shard_map/backward/pallas_call | solution.py:885
  400.6 0.7 slice.48
  401.3 0.1 dynamic-slice_convert_fusion
  401.4 0.6 copy.94
  402.0 0.6 copy.92
  402.6 0.6 copy.93
  403.2 0.9 slice_convert_fusion
  404.1 0.4 reshape.300
  404.5 0.4 fusion.8
  405.0 0.9 copy.68
  405.9 0.0 copy-start
  405.9 3.1 copy-done
  409.0 0.0 copy-start.4
  409.0 0.0 copy-start.5
  409.0 6.8 %finish.1 = (f32[2,192,3072]{2,1,0:T(8,128)}, f32[2,768,768]{2,1,0:T(8,128)}, f32[2,192,768]{2,1,0:T(8,128)}, f32[2,576,768]{2,1,0:T(8,128)}) custom-call(bf16[25,192,768]{2,1,0:T(8,128)(2,1)S(1)} %copy-done), custom_call_target="tpu_custom_call" | custom-call | tf_op jit(solution)/shard_map/finish/pallas_call | solution.py:930
  415.8 0.0 copy-done.4
  415.8 0.7 copy.97
  416.5 0.0 copy-done.5
  416.5 0.7 copy.98
  (15 shorter events, 0.2 us)
Async XLA Ops:
  28.6 3.2 copy-start.2
  28.6 3.2 copy-start.3
  29.8 2.6 copy-start.1
  405.9 3.1 copy-start
  409.0 6.8 %copy-start.4 = (bf16[256,768]{1,0:T(8,128)(2,1)S(1)}, bf16[256,768]{1,0:T(8,128)(2,1)}, u32[]{:S(2)}) copy-start(bf16[256,768]{1,0:T(8,128)(2,1)} %get-tuple-element.31) | copy-start | bytes 1179652
  409.0 7.5 %copy-start.5 = (bf16[256,768]{1,0:T(8,128)(2,1)S(1)}, bf16[256,768]{1,0:T(8,128)(2,1)}, u32[]{:S(2)}) copy-start(bf16[256,768]{1,0:T(8,128)(2,1)} %get-tuple-element.46) | copy-start | bytes 1179652

commit v4 on v3

--- a/solution.py
+++ b/solution.py
@@ -40,17 +40,25 @@
     return 6144 + (c - 8) * 768 + b * 192
 
 
-def small_kernel(s_ref, t_ref, sem, here_sem):
+def small_kernel(s_ref, t_ref, sem):
     s = lax.axis_index("seq")
     b = lax.axis_index("batch")
-    others = [(s, (b + k) % 4) for k in range(1, 4)]
-    greet(others)
-    copies = [remote(s_ref, t_ref.at[b], sem.at[0, k], sem.at[1, 2 - k], dev) for k, dev in enumerate(others)]
-    for copy in copies:
+    core, far = b + 1 - 2 * (b % 2), (b + 2) % 4
+    greet([(s, core), (s, far)])
+
+    def send(src, who, k, dev):
+        return remote(src, t_ref.at[who], sem.at[0, k], sem.at[1, k], dev)
+
+    first = [send(s_ref, b, 0, (s, far)), send(s_ref, b, 1, (s, core))]
+    for copy in first:
         copy.start()
     t_ref[b] = s_ref[...]
-    for copy in copies:
-        copy.wait()
+    first[0].wait_recv()
+    second = send(t_ref.at[far], far, 2, (s, core))
+    second.start()
+    first[0].wait_send()
+    first[1].wait()
+    second.wait()
 
 
 def gather_small(small):
@@ -60,7 +68,7 @@
         out_shape=jax.ShapeDtypeStruct((4,) + small.shape, BF),
         in_specs=[pl.BlockSpec(memory_space=pltpu.VMEM)],
         out_specs=pl.BlockSpec(memory_space=pltpu.VMEM),
-        scratch_shapes=[pltpu.SemaphoreType.DMA((2, 3)), pltpu.SemaphoreType.DMA((1,))],
+        scratch_shapes=[pltpu.SemaphoreType.DMA((2, 3))],
         compiler_params=pltpu.CompilerParams(collective_id=2, has_side_effects=True),
     )(small)
 
@@ -93,22 +101,22 @@
 
 
 class Exchange:
-    def __init__(self, n, seq, batch, state, taken, sums, got, sem):
-        self.n, self.seq, self.batch = n, seq, batch
+    def __init__(self, n, seq, batch, row, state, taken, sums, got, sem):
+        self.n, self.seq, self.batch, self.row = n, seq, batch, row
         self.state, self.taken, self.sums, self.got, self.sem = state, taken, sums, got, sem
         self.group, self.count = owners(n)
 
     def outgoing(self, d):
         peer = (self.seq + d) % self.n
         return peer, remote(
-            self.state.at[:, span(peer % self.count, self.group)], self.taken.at[self.seq],
+            self.state.at[span(peer % self.count, self.group)], self.taken.at[self.seq],
             self.sem.at[0], self.sem.at[1], (peer, self.batch),
         )
 
     def returning(self, d):
         peer = (self.seq + d) % self.n
         return remote(
-            self.sums.at[peer], self.got.at[:, span(self.seq % self.count, self.group)],
+            self.sums.at[peer], self.got.at[span(self.seq % self.count, self.group)],
             self.sem.at[2], self.sem.at[3], (peer, self.batch),
         )
 
@@ -127,7 +135,7 @@
                 pl.when(peer < self.count)(copy.start)
 
         def keep():
-            self.taken[self.seq] = self.state[:, span(self.seq % self.count, self.group)]
+            self.taken[self.seq] = self.state[span(self.seq % self.count, self.group)]
 
         self.owned(keep)
 
@@ -136,52 +144,50 @@
             arrive(self.taken.at[pl.ds(0, self.n - 1)], self.sem.at[1])
 
             def one(p, carry):
-                for r in range(2):
-                    def add(k, total):
-                        return total + coef[(r * self.n + p) * self.n + k] * self.taken[k, r].astype(F32)
-
-                    zero = jnp.zeros((self.group, 128), F32)
-                    if self.n <= 8:
-                        total = zero
-                        for k in range(self.n):
-                            total = add(k, total)
-                    else:
-                        total = lax.fori_loop(0, self.n, add, zero)
-                    self.sums[p, r] = total.astype(BF)
+                def add(k, total):
+                    return total + coef[(self.row * self.n + p) * self.n + k] * self.taken[k].astype(F32)
+
+                total = jnp.zeros((self.group, 128), F32)
+                if self.n <= 8:
+                    for k in range(self.n):
+                        total = add(k, total)
+                else:
+                    total = lax.fori_loop(0, self.n, add, total)
+                self.sums[p] = total.astype(BF)
                 return carry
 
             lax.fori_loop(0, self.n, one, 0)
             for d in range(1, self.n):
                 self.returning(d).start()
-            self.got[:, span(self.seq % self.count, self.group)] = self.sums[self.seq]
+            self.got[span(self.seq % self.count, self.group)] = self.sums[self.seq]
 
         self.owned(work)
 
     def receive(self):
         if self.count == self.n:
-            arrive(self.got.at[:, pl.ds(0, self.group * (self.n - 1))], self.sem.at[3])
+            arrive(self.got.at[pl.ds(0, self.group * (self.n - 1))], self.sem.at[3])
         else:
             @pl.when(self.seq < self.count)
             def _():
-                arrive(self.got.at[:, pl.ds(0, self.group * (self.count - 1))], self.sem.at[3])
+                arrive(self.got.at[pl.ds(0, self.group * (self.count - 1))], self.sem.at[3])
 
             @pl.when(self.seq >= self.count)
             def _():
-                arrive(self.got.at[:, pl.ds(0, self.group * self.count)], self.sem.at[3])
+                arrive(self.got.at[pl.ds(0, self.group * self.count)], self.sem.at[3])
 
     def finish(self):
         if self.count == self.n:
-            arrive(self.state.at[:, pl.ds(0, self.group * (self.n - 1))], self.sem.at[0])
+            arrive(self.state.at[pl.ds(0, self.group * (self.n - 1))], self.sem.at[0])
             arrive(self.sums.at[pl.ds(0, self.n - 1)], self.sem.at[2])
         else:
             @pl.when(self.seq < self.count)
             def _():
-                arrive(self.state.at[:, pl.ds(0, self.group * (self.count - 1))], self.sem.at[0])
+                arrive(self.state.at[pl.ds(0, self.group * (self.count - 1))], self.sem.at[0])
                 arrive(self.sums.at[pl.ds(0, self.n - 1)], self.sem.at[2])
 
             @pl.when(self.seq >= self.count)
             def _():
-                arrive(self.state.at[:, pl.ds(0, self.group * self.count)], self.sem.at[0])
+                arrive(self.state.at[pl.ds(0, self.group * self.count)], self.sem.at[0])
 
 
 def forward_kernel(
@@ -252,6 +258,9 @@
             for copy in (out_core(c), near(c), rest(c)):
                 copy.wait_recv()
 
+    def exchange_of(l, r):
+        return Exchange(n, s, b, r, state.at[l, r], taken.at[l, r], sums.at[l, r], got.at[l, r], esem.at[l, r])
+
     def mean_copy(l, d):
         peer = (s + d) % n
         return remote(means.at[l, s], means.at[l, s], msem.at[l, 0], msem.at[l, 1], (peer, b))
@@ -263,6 +272,10 @@
         copy.start()
         stores.append(copy)
         return copy
+
+    def keep_weights(l, first, size, i):
+        at = pl.ds(first, size)
+        store(w.at[l, at], o_w.at[l, at], 32 + l * 8 + i)
 
     left = lax.broadcasted_iota(jnp.int32, (128, 128), 1) < 64
     lanes = lax.broadcasted_iota(jnp.int32, (128, 128), 1)
@@ -301,12 +314,13 @@
         def value(hp, r):
             return jnp.concatenate([qkv[l, pl.ds(r * 128, 128), pl.ds(pl.multiple_of(1536 + hp * 128, 128), 128)], ones], axis=1)
 
-        def features(hp, carry):
+        def features(r, hp, carry):
+            rr = slice(r * 128, (r + 1) * 128)
             for which in range(2):
-                x = proj[:, pl.ds(pl.multiple_of(which * 768 + hp * 128, 128), 128)]
+                x = proj[rr, pl.ds(pl.multiple_of(which * 768 + hp * 128, 128), 128)]
                 high = x.astype(BF)
                 low = (x - high.astype(F32)).astype(BF)
-                qlo[l, :, pl.ds(pl.multiple_of(which * 768 + hp * 128, 128), 128)] = low
+                qlo[l, rr, pl.ds(pl.multiple_of(which * 768 + hp * 128, 128), 128)] = low
                 m = maps[l, which, hp]
                 logits = nt(m, high) + nt(m, low)
                 for half in range(2):
@@ -314,27 +328,26 @@
                     up = jnp.exp(t - jnp.max(t, axis=0, keepdims=True))
                     down = jnp.exp(jnp.min(t, axis=0, keepdims=True) - t)
                     at = pl.multiple_of(hp * 256 + half * 128, 128)
-                    phi[which, pl.ds(at, 64)] = (up * (1.0 / jnp.sum(up, axis=0, keepdims=True))).astype(BF)
-                    phi[which, pl.ds(at + 64, 64)] = (down * (1.0 / jnp.sum(down, axis=0, keepdims=True))).astype(BF)
-            for r in range(2):
-                v = value(hp, r)
-                got_ = []
-                for half in range(2):
-                    key = phi[1, pl.ds(pl.multiple_of(hp * 256 + half * 128, 128), 128), r * 128 : (r + 1) * 128]
-                    both = nn((key.astype(F32) * last[r]).astype(BF), v)
-                    got_.append(both[:, :128])
-                    norm_sum[r] += jnp.where(lanes % 64 == hp * 2 + half, both[:, 128:], 0.0)
-                state[l, r, span(hp, 128)] = jnp.where(left, got_[0], got_[1]).astype(BF)
+                    phi[which, pl.ds(at, 64), rr] = (up * (1.0 / jnp.sum(up, axis=0, keepdims=True))).astype(BF)
+                    phi[which, pl.ds(at + 64, 64), rr] = (down * (1.0 / jnp.sum(down, axis=0, keepdims=True))).astype(BF)
+            v = value(hp, r)
+            sums_ = []
+            for half in range(2):
+                key = phi[1, pl.ds(pl.multiple_of(hp * 256 + half * 128, 128), 128), rr]
+                both = nn((key.astype(F32) * last[r]).astype(BF), v)
+                sums_.append(both[:, :128])
+                norm_sum[r] += jnp.where(lanes % 64 == hp * 2 + half, both[:, 128:], 0.0)
+            state[l, r, span(hp, 128)] = jnp.where(left, sums_[0], sums_[1]).astype(BF)
             return carry
 
-        for k in range(3):
-            lax.fori_loop(2 * k, 2 * k + 2, features, 0)
-            if k < 2:
-                pump()
+        swaps = [exchange_of(l, r) for r in range(2)]
         for r in range(2):
+            for k in range(2):
+                lax.fori_loop(3 * k, 3 * k + 3, functools.partial(features, r), 0)
+                if k == 0:
+                    pump()
             state[l, r, 768:896] = norm_sum[r].astype(BF)
-        swap = Exchange(n, s, b, state.at[l], taken.at[l], sums.at[l], got.at[l], esem.at[l])
-        swap.send()
+            swaps[r].send()
         phi_store = store(phi, o_phi.at[l], l * 16 + 0)
         store(na.at[l], o_na.at[l], l * 16 + 1)
         store(qlo.at[l], o_lo.at[l], l * 16 + 13)
@@ -342,53 +355,53 @@
         store(h.at[l], o_h.at[l], l * 16 + 3)
         pump()
 
-        def scores(hp, carry):
-            for r in range(2):
-                v = value(hp, r)
-                both = []
-                for half in range(2):
-                    at = pl.ds(pl.multiple_of(hp * 256 + half * 128, 128), 128)
-                    query = phi[0, at, r * 128 : (r + 1) * 128].astype(F32).T.astype(BF)
-                    pq[r * 128 : (r + 1) * 128, at] = query
-                    key = phi[1, at, r * 128 : (r + 1) * 128]
-                    both.append(nn((nn(query, key) * mask[r]).astype(BF), v))
-                at = span(hp, 128)
-                num[r * 128 : (r + 1) * 128, at] = jnp.where(left, both[0][:, :128], both[1][:, :128])
-                zz[r * 128 : (r + 1) * 128, at] = jnp.where(left, both[0][:, 128:], both[1][:, 128:])
+        def scores(r, hp, carry):
+            v = value(hp, r)
+            both = []
+            for half in range(2):
+                at = pl.ds(pl.multiple_of(hp * 256 + half * 128, 128), 128)
+                query = phi[0, at, r * 128 : (r + 1) * 128].astype(F32).T.astype(BF)
+                pq[r * 128 : (r + 1) * 128, at] = query
+                key = phi[1, at, r * 128 : (r + 1) * 128]
+                both.append(nn((nn(query, key) * mask[r]).astype(BF), v))
+            at = span(hp, 128)
+            num[r * 128 : (r + 1) * 128, at] = jnp.where(left, both[0][:, :128], both[1][:, :128])
+            zz[r * 128 : (r + 1) * 128, at] = jnp.where(left, both[0][:, 128:], both[1][:, 128:])
             return carry
 
-        lax.fori_loop(0, 3, scores, 0)
+        def finish_row(r, hp, carry):
+            at = span(hp, 128)
+            both = []
+            for half in range(2):
+                query = pq[r * 128 : (r + 1) * 128, pl.ds(pl.multiple_of(hp * 256 + half * 128, 128), 128)]
+                pick = (rows_i == hp * 2 + half).astype(BF)
+                column = nn(got[l, r, 768:896], pick).astype(BF)
+                both.append(nn(query, jnp.concatenate([got[l, r, at], column], axis=1)))
+            c = chain[r]
+            z = zz[r * 128 : (r + 1) * 128, at] + c * jnp.where(left, both[0][:, 128:], both[1][:, 128:])
+            top = num[r * 128 : (r + 1) * 128, at] + c * jnp.where(left, both[0][:, :128], both[1][:, :128])
+            inverse = 1.0 / z
+            out = top * inverse
+            rz[l, r * 128 : (r + 1) * 128, at] = inverse
+            att[l, r * 128 : (r + 1) * 128, at] = out
+            attl[l, r * 128 : (r + 1) * 128, at] = (out + mu[r : r + 1, at]).astype(BF)
+            return carry
+
+        lax.fori_loop(0, 6, functools.partial(scores, 0), 0)
+        swaps[0].turn(coef)
         pump()
-        swap.turn(coef)
-        lax.fori_loop(3, 6, scores, 0)
+        lax.fori_loop(0, 6, functools.partial(scores, 1), 0)
+        swaps[1].turn(coef)
         pump(2)
-        swap.receive()
-
-        def finish(hp, carry):
-            at = span(hp, 128)
-            for r in range(2):
-                both = []
-                for half in range(2):
-                    query = pq[r * 128 : (r + 1) * 128, pl.ds(pl.multiple_of(hp * 256 + half * 128, 128), 128)]
-                    pick = (rows_i == hp * 2 + half).astype(BF)
-                    column = nn(got[l, r, 768:896], pick).astype(BF)
-                    both.append(nn(query, jnp.concatenate([got[l, r, at], column], axis=1)))
-                c = chain[r]
-                z = zz[r * 128 : (r + 1) * 128, at] + c * jnp.where(left, both[0][:, 128:], both[1][:, 128:])
-                top = num[r * 128 : (r + 1) * 128, at] + c * jnp.where(left, both[0][:, :128], both[1][:, :128])
-                inverse = 1.0 / z
-                out = top * inverse
-                rz[l, r * 128 : (r + 1) * 128, at] = inverse
-                att[l, r * 128 : (r + 1) * 128, at] = out
-                attl[l, r * 128 : (r + 1) * 128, at] = (out + mu[r : r + 1, at]).astype(BF)
-            return carry
-
-        lax.fori_loop(0, 6, finish, 0)
+        for r in range(2):
+            swaps[r].receive()
+            lax.fori_loop(0, 6, functools.partial(finish_row, r), 0)
         store(got.at[l], o_got.at[l], l * 16 + 4)
         store(rz.at[l], o_rz.at[l], l * 16 + 5)
         store(att.at[l], o_att.at[l], l * 16 + 6)
         store(attl.at[l], o_attl.at[l], l * 16 + 7)
         need(base + 3, base + 4)
+        keep_weights(l, 0, 3072, 0)
         for t in range(3):
             at = slice(t * 256, (t + 1) * 256)
             mid[l, :, at] = h[l, :, at] + nt(attl[l], w[l, 2304 + t * 256 : 2304 + (t + 1) * 256])
@@ -396,6 +409,7 @@
         store(mid.at[l], o_mid.at[l], l * 16 + 8)
         store(nm.at[l], o_nm.at[l], l * 16 + 9)
         need(base + 4, base + 8)
+        keep_weights(l, 3072, 3072, 1)
         if act_store is not None:
             for copy in (act_store, dg_store):
                 copy.wait()
@@ -414,19 +428,20 @@
         dg_store = store(dg, o_dg.at[l], l * 16 + 11)
         for k in range(4):
             need(base + 8 + k, base + 9 + k)
+            keep_weights(l, 6144 + k * 768, 768, 2 + k)
             for t in range(3):
                 at = slice(t * 256, (t + 1) * 256)
                 first = 6144 + k * 768 + t * 256
                 y = nt(act[k], w[l, first : first + 256])
                 before = mid[l, :, at] if k == 0 else h[l + 1, :, at]
                 h[l + 1, :, at] = before + y
-        store(w.at[l], o_w.at[l], l * 16 + 12)
     o_out[...] = h[layers].astype(BF)
     for copy in stores:
         copy.wait()
     for l in range(layers):
         arrive(means.at[l, pl.ds(0, n - 1)], msem.at[l, 0])
-        Exchange(n, s, b, state.at[l], taken.at[l], sums.at[l], got.at[l], esem.at[l]).finish()
+        for r in range(2):
+            exchange_of(l, r).finish()
     for c in range(count):
         for copy in (out_y(c), out_x(c), out_core(c), near(c), rest(c)):
             copy.wait_send()
@@ -455,9 +470,9 @@
             V(BF, 2, 9216, D), V(F32, 3, m, D), V(F32, 2, m, D), V(BF, 2, m, D), V(BF, 2, m, D), V(BF, 2, m, 2304),
             V(BF, 2, 1536, m), V(F32, 2, m, D), V(BF, 2, m, D), V(F32, 2, m, D), V(BF, 4, m, D), V(BF, 4, m, D),
             V(BF, 2, 2, STATE_ROWS, 128), V(F32, m, 1536), V(BF, m, 1536), V(F32, m, D), V(F32, m, D), V(F32, 2, 128, 128),
-            V(BF, 2, 2, STATE_ROWS, 128), V(BF, 2, n, 2, group, 128), V(BF, 2, n, 2, group, 128), V(BF, 2, m, 1536), V(F32, 8, D), V(F32, 2, n, 8, D),
+            V(BF, 2, 2, STATE_ROWS, 128), V(BF, 2, 2, n, group, 128), V(BF, 2, 2, n, group, 128), V(BF, 2, m, 1536), V(F32, 8, D), V(F32, 2, n, 8, D),
             pltpu.SemaphoreType.DMA((24,)), pair(), pair(), pair(), pair(), pair(),
-            pltpu.SemaphoreType.DMA((2, 4)), pltpu.SemaphoreType.DMA((2, 2)), pltpu.SemaphoreType.DMA((32,)),
+            pltpu.SemaphoreType.DMA((2, 2, 4)), pltpu.SemaphoreType.DMA((2, 2)), pltpu.SemaphoreType.DMA((48,)),
         ],
         compiler_params=pltpu.CompilerParams(collective_id=0, has_side_effects=True, vmem_limit_bytes=63 * 2**20),
     )(tok, w, norms, maps, mask, chain, last, coef)
@@ -643,12 +658,9 @@
             flip[t * 128 : (t + 1) * 128] = src(t).T.astype(BF)
 
     fetch_start(0)
-    fetch_start(1)
     for k in range(2):
         act_load(1, k).start()
         dg_load(1, k).start()
-    start(mlp_loads(1))
-    start(att_loads(1))
     gh[...] = cot[...].astype(F32)
     for l in (1, 0):
         c0 = (1 - l) * 12
@@ -658,6 +670,10 @@
         for k in range(4):
             if k % 2 == 0:
                 fetch(w0 + k // 2).wait()
+            if k == 0 and l == 1:
+                fetch_start(1)
+                start(mlp_loads(1))
+                start(att_loads(1))
             act_load(l, k).wait()
             dg_load(l, k).wait()
             low = gh[...].astype(BF)
@@ -760,13 +776,18 @@
                 pump(plan[6 + k])
         for r in range(2):
             state[r, 768:896] = norm_sum[r].astype(BF)
-        swap = Exchange(n, s, b, state, taken, sums, back, esem.at[l])
-        swap.send()
+        swaps = [
+            Exchange(n, s, b, r, state.at[r], taken.at[r], sums.at[r], back.at[r], esem.at[l, r]) for r in range(2)
+        ]
+        for swap in swaps:
+            swap.send()
         produced(c0 + 8)
         pump(plan[8])
-        swap.turn(coef)
+        for swap in swaps:
+            swap.turn(coef)
         pump(plan[9])
-        swap.receive()
+        for swap in swaps:
+            swap.receive()
 
         def keys(hp, carry):
             at = span(hp, 128)
@@ -799,7 +820,8 @@
             lax.fori_loop(2 * k, 2 * k + 2, keys, 0)
             if k < 2:
                 pump(plan[10 + k])
-        swap.finish()
+        for swap in swaps:
+            swap.finish()
 
         def in_chunk(j, carry):
             produce(c0 + 9 + j, lambda q: nn(dqkvt[pl.ds(pl.multiple_of(q * 576 + j * 192, 64), 192)], na[...]))
@@ -895,9 +917,9 @@
             V(BF, m, 2304), V(BF, 2, 1536, m), V(BF, 2, STATE_ROWS, 128), V(BF, m, D), V(F32, m, D), V(BF, m, 1536), V(BF, m, D),
             V(F32, m, D), V(BF, 4, m, D), V(F32, m, D), V(F32, 1536, m), V(F32, D, m), V(BF, 2304, m), V(BF, D, m), V(F32, m, D),
             V(F32, 2, 2, 6, 128, 128), V(F32, 8, D), V(F32, 2, 128, 128), V(BF, 2, STATE_ROWS, 128),
-            V(BF, n, 2, group, 128), V(BF, n, 2, group, 128), V(BF, 2, STATE_ROWS, 128),
+            V(BF, 2, n, group, 128), V(BF, 2, n, group, 128), V(BF, 2, STATE_ROWS, 128),
             pair(), pair(), pair(), pair(), pair(), pltpu.SemaphoreType.DMA((2, count, max(extra, 1))), pair(), pair(), pair(),
-            pltpu.SemaphoreType.DMA((count,)), pltpu.SemaphoreType.DMA((2, 4)), pltpu.SemaphoreType.DMA((2,)),
+            pltpu.SemaphoreType.DMA((count,)), pltpu.SemaphoreType.DMA((2, 2, 4)), pltpu.SemaphoreType.DMA((2,)),
             pltpu.SemaphoreType.DMA((2, 2)), pltpu.SemaphoreType.DMA((11,)),
         ],
         compiler_params=pltpu.CompilerParams(collective_id=1, has_side_effects=True, vmem_limit_bytes=63 * 2**20),
@@ -966,8 +988,9 @@
         axis=1,
     )
     small = jnp.concatenate([norm_gains[:, :, None], norm_biases[:, :, None], feature_maps], axis=2)
-    small = jnp.pad(small.reshape(layers * 132, 192), ((0, (-layers * 132) % 16), (0, 64)))
-    smalls = gather_small(small)[:, : layers * 132, :192].reshape(4, layers, 2, 66, 192)
+    count = layers * 33
+    small = jnp.pad(small.reshape(count, 768), ((0, -count % 16), (0, 0)))
+    smalls = gather_small(small)[:, :count].reshape(4, layers, 2, 66, 192)
     smalls = jnp.transpose(smalls, (1, 2, 3, 0, 4)).reshape(layers, 2, 66, 768)
     norms = smalls[:, :, :2].astype(F32)
     maps = jnp.transpose(smalls[:, :, 2:].reshape(layers, 2, 64, 6, 2, 64), (0, 1, 3, 4, 5, 2))

time: 422 us -> 418 us (level)
  Pallas kernels: 383 us -> 378 us
where the time goes in v4:
time: 418 us; the launch traced here: 413 us
  Pallas kernels  378 us (90%)
  local copies, waits for them, and re-layouts  23.8 us (6%)
  other arithmetic  10.6 us (3%)
    pallas_call x1, Pallas kernels, backward(): pl.pallas_call(functools.partial(backward_kernel, n, count), name='backwa...  231 us
    pallas_call x1, Pallas kernels, forward(): pl.pallas_call(functools.partial(forward_kernel, n), name='forward', out_...  130 us
    pallas_call x1, Pallas kernels, gather_small(): pl.pallas_call(small_kernel, name='gather_small', out_shape=jax.ShapeDtyp...  9.67 us

profile of v4, /device:TPU:0, one launch (start us, length us, event | category | flops | bytes accessed | tf_op | source)
XLA Modules:
  0.0 413.2 jit_solution(14470489098147301621)
XLA Ops:
  0.7 0.9 reduce_window_sum.11
  1.6 0.8 fusion.5
  2.4 0.1 copy.54
  2.4 0.1 fusion.2
  2.5 0.1 fusion.3
  2.6 0.1 compare_convert_fusion.5
  2.7 0.2 slice_reduce_fusion
  2.9 0.6 compare_convert_fusion.3
  3.5 0.7 copy.49
  4.2 0.7 copy.50
  4.9 0.1 and_convert_fusion
  5.0 0.6 reshape.298.coef
  5.6 0.6 reshape.297.coef
  6.2 0.1 mul.48
  6.3 0.1 mul.49
  6.4 0.8 compare_select_fusion.mask
  7.2 0.8 broadcast_in_dim.16.chain
  7.9 1.0 pad_maximum_fusion.2
  8.9 0.2 reshape.289
  9.0 0.7 pad.4.s_ref
  9.7 9.7 %gather_small.1 = bf16[4,80,768]{2,1,0:T(8,128)(2,1)} custom-call(bf16[80,768]{1,0:T(8,128)(2,1)} %pad.4.s_ref), custom_call_target="tpu_custom_call" | custom-call | tf_op jit(solution)/shard_map/gather_small/pallas_call | solution.py:65
  19.4 1.0 slice.43
  20.4 0.7 reshape.290
  21.1 0.4 copy.51
  21.5 0.7 reshape.291
  22.2 0.3 slice.58
  22.5 0.6 copy_convert_fusion.norms
  23.1 0.5 reshape.292
  23.6 0.8 copy.53
  24.4 1.5 mul.46
  25.9 0.9 mul.47
  26.8 0.9 fusion.10.maps
  27.8 0.1 broadcast_multiply_fusion
  27.8 0.0 copy-start.2
  27.8 0.0 copy-start.3
  27.8 1.2 copy.56.maps
  29.0 0.0 copy-start.1
  29.0 2.0 copy.89
  31.0 0.0 copy-done.2
  31.0 0.0 copy-done.3
  31.0 0.6 copy-done.1
  31.6 3.6 pad_maximum_fusion.w_ref
  35.1 130.1 %forward.1 = (bf16[2,9216,768]{2,1,0:T(8,128)(2,1)}, f32[2,256,768]{2,1,0:T(8,128)}, f32[2,256,768]{2,1,0:T(8,128)}, bf16[2,256,768]{2,1,0:T(8,128)(2,1)}, bf16[...) custom-call(bf16[256,768]{1,0:T(8,128)(2,1)} %bitcast.63, ...), custom_call_target="tpu_custom_call" | custom-call | tf_op jit(solution)/shard_map/forward/pallas_call | solution.py:463
  165.2 231.1 %backward.1 = (bf16[25,192,768]{2,1,0:T(8,128)(2,1)}, bf16[256,768]{1,0:T(8,128)(2,1)}) custom-call(bf16[256,768]{1,0:T(8,128)(2,1)} %bitcast.60, f32[2,2,2,768]{3,2,1,0:T(2,128)} %copy_convert_fusion.norms, bf16[2,2,6,128,128]{4,3,2,1,0:T(8,128)(2,1)} %fusion.10.maps, f32[2,128,128]{2,1,0:T(8,128)} %compare_select_fusion.mask, ...), custom_call_target="tpu_custom_call" | custom-call | tf_op jit(solution)/shard_map/backward/pallas_call | solution.py:907
  396.3 0.7 slice.48
  397.0 0.1 dynamic-slice_convert_fusion
  397.1 0.6 copy.92
  397.7 0.6 copy.90
  398.3 0.6 copy.91
  398.9 0.9 slice_convert_fusion
  399.8 0.4 reshape.300
  400.2 0.4 fusion.8
  400.7 0.9 copy.66
  401.6 0.0 copy-start
  401.6 3.1 copy-done
  404.7 0.0 copy-start.4
  404.7 0.0 copy-start.5
  404.7 6.8 %finish.1 = (f32[2,192,3072]{2,1,0:T(8,128)}, f32[2,768,768]{2,1,0:T(8,128)}, f32[2,192,768]{2,1,0:T(8,128)}, f32[2,576,768]{2,1,0:T(8,128)}) custom-call(bf16[25,192,768]{2,1,0:T(8,128)(2,1)S(1)} %copy-done), custom_call_target="tpu_custom_call" | custom-call | tf_op jit(solution)/shard_map/finish/pallas_call | solution.py:952
  411.5 0.0 copy-done.4
  411.5 0.7 copy.95
  412.2 0.0 copy-done.5
  412.2 0.7 copy.96
  (16 shorter events, 0.2 us)
Async XLA Ops:
  27.8 3.2 copy-start.2
  27.8 3.2 copy-start.3
  29.0 2.6 copy-start.1
  401.6 3.1 copy-start
  404.7 6.8 %copy-start.4 = (bf16[256,768]{1,0:T(8,128)(2,1)S(1)}, bf16[256,768]{1,0:T(8,128)(2,1)}, u32[]{:S(2)}) copy-start(bf16[256,768]{1,0:T(8,128)(2,1)} %get-tuple-element.31) | copy-start | bytes 1179652
  404.7 7.5 %copy-start.5 = (bf16[256,768]{1,0:T(8,128)(2,1)S(1)}, bf16[256,768]{1,0:T(8,128)(2,1)}, u32[]{:S(2)}) copy-start(bf16[256,768]{1,0:T(8,128)(2,1)} %get-tuple-element.46) | copy-start | bytes 1179652

commit v5 on v4

--- a/solution.py
+++ b/solution.py
@@ -498,8 +498,8 @@
 
 CHUNK = 192
 PLAN = {
-    1: [0, 0, 0, 0, 0, 1, 0, 1, 2, 2, 0, 1, 0, 1],
-    0: [0, 0, 0, 1, 0, 1, 0, 1, 3, 2, 0, 1, 0, 1],
+    1: [0, 0, 0, 0, 0, 1, 0, 1, 2, 2, 1, 1, 0, 1],
+    0: [0, 0, 0, 1, 0, 1, 1, 1, 3, 2, 1, 0, 0, 2],
 }
 
 

time: 418 us -> 416 us (level)
  no operation moved by 1% of the time
where the time goes in v5:
time: 416 us; the launch traced here: 411 us
  Pallas kernels  376 us (90%)
  local copies, waits for them, and re-layouts  23.8 us (6%)
  other arithmetic  10.6 us (3%)
    pallas_call x1, Pallas kernels, backward(): pl.pallas_call(functools.partial(backward_kernel, n, count), name='backwa...  229 us
    pallas_call x1, Pallas kernels, forward(): pl.pallas_call(functools.partial(forward_kernel, n), name='forward', out_...  130 us
    pallas_call x1, Pallas kernels, gather_small(): pl.pallas_call(small_kernel, name='gather_small', out_shape=jax.ShapeDtyp...  9.67 us

profile of v5, /device:TPU:0, one launch (start us, length us, event | category | flops | bytes accessed | tf_op | source)
XLA Modules:
  0.0 411.1 jit_solution(10186060028650010189)
XLA Ops:
  0.7 0.9 reduce_window_sum.11
  1.6 0.8 fusion.5
  2.4 0.1 copy.54
  2.4 0.1 fusion.2
  2.5 0.1 fusion.3
  2.6 0.1 compare_convert_fusion.5
  2.7 0.2 slice_reduce_fusion
  2.9 0.6 compare_convert_fusion.3
  3.5 0.7 copy.49
  4.2 0.7 copy.50
  4.9 0.1 and_convert_fusion
  5.0 0.6 reshape.298.coef
  5.6 0.6 reshape.297.coef
  6.2 0.1 mul.48
  6.3 0.1 mul.49
  6.4 0.8 compare_select_fusion.mask
  7.2 0.8 broadcast_in_dim.16.chain
  7.9 1.0 pad_maximum_fusion.2
  8.9 0.2 reshape.289
  9.0 0.7 pad.4.s_ref
  9.7 9.7 %gather_small.1 = bf16[4,80,768]{2,1,0:T(8,128)(2,1)} custom-call(bf16[80,768]{1,0:T(8,128)(2,1)} %pad.4.s_ref), custom_call_target="tpu_custom_call" | custom-call | tf_op jit(solution)/shard_map/gather_small/pallas_call | solution.py:65
  19.4 1.0 slice.43
  20.4 0.7 reshape.290
  21.1 0.4 copy.51
  21.5 0.7 reshape.291
  22.2 0.3 slice.58
  22.5 0.6 copy_convert_fusion.norms
  23.1 0.5 reshape.292
  23.6 0.8 copy.53
  24.4 1.5 mul.46
  25.9 0.9 mul.47
  26.8 0.9 fusion.10.maps
  27.8 0.1 broadcast_multiply_fusion
  27.8 0.0 copy-start.2
  27.8 0.0 copy-start.3
  27.8 1.2 copy.56.maps
  29.0 0.0 copy-start.1
  29.0 2.0 copy.89
  31.0 0.0 copy-done.2
  31.0 0.0 copy-done.3
  31.0 0.6 copy-done.1
  31.6 3.6 pad_maximum_fusion.w_ref
  35.1 130.1 %forward.1 = (bf16[2,9216,768]{2,1,0:T(8,128)(2,1)}, f32[2,256,768]{2,1,0:T(8,128)}, f32[2,256,768]{2,1,0:T(8,128)}, bf16[2,256,768]{2,1,0:T(8,128)(2,1)}, bf16[...) custom-call(bf16[256,768]{1,0:T(8,128)(2,1)} %bitcast.63, ...), custom_call_target="tpu_custom_call" | custom-call | tf_op jit(solution)/shard_map/forward/pallas_call | solution.py:463
  165.2 229.0 %backward.1 = (bf16[25,192,768]{2,1,0:T(8,128)(2,1)}, bf16[256,768]{1,0:T(8,128)(2,1)}) custom-call(bf16[256,768]{1,0:T(8,128)(2,1)} %bitcast.60, f32[2,2,2,768]{3,2,1,0:T(2,128)} %copy_convert_fusion.norms, bf16[2,2,6,128,128]{4,3,2,1,0:T(8,128)(2,1)} %fusion.10.maps, f32[2,128,128]{2,1,0:T(8,128)} %compare_select_fusion.mask, ...), custom_call_target="tpu_custom_call" | custom-call | tf_op jit(solution)/shard_map/backward/pallas_call | solution.py:907
  394.3 0.7 slice.48
  395.0 0.1 dynamic-slice_convert_fusion
  395.1 0.6 copy.92
  395.7 0.6 copy.90
  396.3 0.6 copy.91
  396.9 0.9 slice_convert_fusion
  397.8 0.4 reshape.300
  398.2 0.4 fusion.8
  398.7 0.9 copy.66
  399.5 0.0 copy-start
  399.5 3.1 copy-done
  402.6 0.0 copy-start.4
  402.6 0.0 copy-start.5
  402.6 6.8 %finish.1 = (f32[2,192,3072]{2,1,0:T(8,128)}, f32[2,768,768]{2,1,0:T(8,128)}, f32[2,192,768]{2,1,0:T(8,128)}, f32[2,576,768]{2,1,0:T(8,128)}) custom-call(bf16[25,192,768]{2,1,0:T(8,128)(2,1)S(1)} %copy-done), custom_call_target="tpu_custom_call" | custom-call | tf_op jit(solution)/shard_map/finish/pallas_call | solution.py:952
  409.4 0.0 copy-done.4
  409.4 0.7 copy.95
  410.2 0.0 copy-done.5
  410.2 0.7 copy.96
  (16 shorter events, 0.2 us)
Async XLA Ops:
  27.8 3.2 copy-start.2
  27.8 3.2 copy-start.3
  29.0 2.6 copy-start.1
  399.5 3.1 copy-start
  402.6 6.8 %copy-start.4 = (bf16[256,768]{1,0:T(8,128)(2,1)S(1)}, bf16[256,768]{1,0:T(8,128)(2,1)}, u32[]{:S(2)}) copy-start(bf16[256,768]{1,0:T(8,128)(2,1)} %get-tuple-element.31) | copy-start | bytes 1179652
  402.6 7.5 %copy-start.5 = (bf16[256,768]{1,0:T(8,128)(2,1)S(1)}, bf16[256,768]{1,0:T(8,128)(2,1)}, u32[]{:S(2)}) copy-start(bf16[256,768]{1,0:T(8,128)(2,1)} %get-tuple-element.46) | copy-start | bytes 1179652
